TPU v7x, 256 devices: a whole 4x4x8 slice. The times are simulated.
256 devices in a mesh: seq: 16 (over z_hi, y, core), chan: 16 (over x, z_lo).
Axes of the slice: x: 4, y: 4, z: 8 (z_hi: 2, z_lo: 4; z = z_hi * 4 + z_lo), core: 2. Of those that a mesh axis runs over, the one named last changes fastest.
Arguments:
- query: bfloat16 [4096, 8192], P('seq', 'chan'), may hold values from -6 to 6
- key_in: bfloat16 [4096, 8192], P('seq', 'chan'), may hold values from -6 to 6
- value_in: bfloat16 [4096, 8192], P('seq', 'chan'), may hold values from -6 to 6
- filter_taps: float32 [4096, 8192], P('seq', 'chan'), may hold values from -4 to 4
- conv_bias: float32 [8192], P('chan'), may hold values from -4 to 4
- out_weight: bfloat16 [8192, 8192], P('seq', 'chan'), may hold values from -0.0625 to 0.0625
Outputs:
- block_out: bfloat16 [4096, 8192], P('seq', 'chan')
All inputs are finite; a program needn't handle non-finite values.
Results may differ from a plain program's by a relative error of at most 0.0049.
Values may be sent and summed in bfloat16 or wider, within the bound.
No kernel may reach another device: no remote copies, remote signals or barrier semaphores. Data moves between devices by JAX's collectives and lax.ppermute only.
A program may use at most 64 MiB of HBM per device.

v0:
```python
import math

import jax
import jax.numpy as jnp
from jax import lax
from jax.sharding import PartitionSpec as P

best_precision = lax.Precision.HIGHEST


def phases(left_idx, right_idx, period):
    prod_index = left_idx[:, None] * right_idx[None, :] % period
    phase_angle = prod_index.astype(jnp.float32) * (2.0 * math.pi / period)
    return (jnp.cos(phase_angle), jnp.sin(phase_angle))


def twiddle(real_part, imag_part, freq_index, within, fft_size, conj_sign):
    cosine, sine_tab = phases(freq_index, within, fft_size)
    cosine = cosine[:, :, None]
    sine_tab = conj_sign * sine_tab[:, :, None]
    return (real_part * cosine - imag_part * sine_tab, imag_part * cosine + real_part * sine_tab)


def forward(blocks, freq_index, within, period, fft_size):
    block_index = jnp.arange(blocks.shape[0], dtype=jnp.int32)
    cosine, sine_tab = phases(freq_index, block_index, period)
    real_part = jnp.einsum("ka,agc->kgc", cosine, blocks, precision=best_precision)
    imag_part = -jnp.einsum("ka,agc->kgc", sine_tab, blocks, precision=best_precision)
    return twiddle(real_part, imag_part, freq_index, within, fft_size, -1.0)


def over_rows(real_part, imag_part, conj_sign):
    count_of_rows = real_part.shape[1]
    row_index = jnp.arange(count_of_rows, dtype=jnp.int32)
    cosine, sine_tab = phases(row_index, row_index, count_of_rows)
    sine_tab = conj_sign * sine_tab
    new_real = jnp.einsum("kbc,bj->kjc", real_part, cosine, precision=best_precision) - jnp.einsum(
        "kbc,bj->kjc", imag_part, sine_tab, precision=best_precision
    )
    new_imag = jnp.einsum("kbc,bj->kjc", imag_part, cosine, precision=best_precision) + jnp.einsum(
        "kbc,bj->kjc", real_part, sine_tab, precision=best_precision
    )
    return (new_real, new_imag)


def to_blocks(real_part, imag_part, freq_index, block_count, period, inv_size):
    block_index = jnp.arange(block_count, dtype=jnp.int32)
    cosine, sine_tab = phases(block_index, freq_index, period)
    summed = jnp.einsum("ak,kgc->agc", cosine, real_part, precision=best_precision) - jnp.einsum(
        "ak,kgc->agc", sine_tab, imag_part, precision=best_precision
    )
    return inv_size * summed


def spectral_product(sig_re, sig_im, tap_re, tap_im):
    sig_re, sig_im = over_rows(sig_re, sig_im, -1.0)
    tap_re, tap_im = over_rows(tap_re, tap_im, -1.0)
    prod_re = sig_re * tap_re - sig_im * tap_im
    prod_im = sig_re * tap_im + sig_im * tap_re
    return over_rows(prod_re, prod_im, 1.0)


def body(query, key_in, value_in, filter_taps, conv_bias, out_weight):
    tok_rows = query.shape[0]
    seq_count = lax.axis_size("seq")
    period = 2 * seq_count
    fft_size = period * tok_rows
    inv_size = 1.0 / fft_size
    signal = key_in.astype(jnp.float32) * value_in.astype(jnp.float32)
    all_freqs = jnp.arange(period, dtype=jnp.int32)
    row_share = tok_rows // seq_count
    freq_share = period // seq_count
    block_signal, block_taps = (
        lax.all_to_all(signal[None], "seq", split_axis=1, concat_axis=0, tiled=True),
        lax.all_to_all(filter_taps[None], "seq", split_axis=1, concat_axis=0, tiled=True),
    )
    within = lax.axis_index("seq") * row_share + jnp.arange(row_share, dtype=jnp.int32)
    sig_re, sig_im = forward(block_signal, all_freqs, within, period, fft_size)
    tap_re, tap_im = forward(block_taps, all_freqs, within, period, fft_size)
    sig_re, sig_im, tap_re, tap_im = (
        lax.all_to_all(sig_re, "seq", split_axis=0, concat_axis=1, tiled=True),
        lax.all_to_all(sig_im, "seq", split_axis=0, concat_axis=1, tiled=True),
        lax.all_to_all(tap_re, "seq", split_axis=0, concat_axis=1, tiled=True),
        lax.all_to_all(tap_im, "seq", split_axis=0, concat_axis=1, tiled=True),
    )
    my_freqs = lax.axis_index("seq") * freq_share + jnp.arange(freq_share, dtype=jnp.int32)
    all_rows = jnp.arange(tok_rows, dtype=jnp.int32)
    back_re, inverse_imaginary = spectral_product(sig_re, sig_im, tap_re, tap_im)
    back_re, inverse_imaginary = twiddle(
        back_re, inverse_imaginary, my_freqs, all_rows, fft_size, 1.0
    )
    back_re, inverse_imaginary = (
        lax.all_to_all(back_re, "seq", split_axis=1, concat_axis=0, tiled=True),
        lax.all_to_all(inverse_imaginary, "seq", split_axis=1, concat_axis=0, tiled=True),
    )
    result = to_blocks(back_re, inverse_imaginary, all_freqs, seq_count, period, inv_size)
    convolved = lax.all_to_all(result, "seq", split_axis=0, concat_axis=1, tiled=True)[0]
    gated_out = (query.astype(jnp.float32) * (convolved + conv_bias[None, :] * signal)).astype(
        jnp.bfloat16
    )
    gathered = lax.all_gather(gated_out, "chan", axis=1, tiled=True)
    projected = jnp.dot(
        gathered,
        lax.all_gather(out_weight, "seq", axis=0, tiled=True),
        preferred_element_type=jnp.float32,
    )
    return projected.astype(jnp.bfloat16)


def solution(mesh):
    placed = (
        P("seq", "chan"),
        P("seq", "chan"),
        P("seq", "chan"),
        P("seq", "chan"),
        P("chan"),
        P("seq", "chan"),
    )
    return jax.shard_map(
        body, mesh=mesh, in_specs=placed, out_specs=P("seq", "chan"), check_vma=False
    )
```

profile of v0, /device:TPU:1, one launch (start us, length us, event | category | flops | bytes accessed | tf_op | source)
XLA Modules:
  0.0 538.6 jit_solution(11697670570617735816)
XLA Ops:
  9.0 12.6 %all-to-all-start = ((f32[1,256,512]{2,0,1:T(1,128)}), f32[1,256,512]{2,0,1:T(1,128)S(1)}, u32[]{:S(2)}, u32[]{:S(2)}) async-start(f32[1,256,512]{2,0,1:T(1,128)} %copy.24), calls=%async_computation | async-start | bytes 1048576 | tf_op jit(solution)/shard_map/all_to_all | solution.py:74
  21.6 2.2 broadcast_in_dim.5
  23.8 12.8 %all-to-all-done = f32[1,256,512]{2,0,1:T(1,128)S(1)} async-done(((f32[1,256,512]{2,0,1:T(1,128)}), f32[1,256,512]{2,0,1:T(1,128)S(1)}, u32[]{:S(2)}, u32[]{:S(2)}) %all-to-all-start) | async-done | bytes 524320 | tf_op jit(solution)/shard_map/all_to_all | solution.py:74
  36.6 4.4 all-to-all-start.3
  42.5 2.2 fusion.16
  44.7 10.3 %all-to-all-done.3 = f32[1,256,512]{2,0,1:T(1,128)S(1)} async-done(((f32[1,256,512]{2,0,1:T(1,128)}), f32[1,256,512]{2,0,1:T(1,128)S(1)}, u32[]{:S(2)}, u32[]{:S(2)}) %all-to-all-start.3) | async-done | bytes 524320 | tf_op jit(solution)/shard_map/all_to_all | solution.py:75
  56.2 3.8 multiply_add_fusion.2
  61.6 8.0 %all-to-all-start.4 = ((f32[32,16,512]{2,1,0:T(8,128)}), f32[32,16,512]{2,1,0:T(8,128)S(1)}, u32[]{:S(2)}, u32[]{:S(2)}) async-start(f32[32,16,512]{2,1,0:T(8,128)} %copy.33), calls=%async_computation.4 | async-start | bytes 2097152 | tf_op jit(solution)/shard_map/all_to_all | solution.py:83
  69.6 2.8 copy.35
  72.4 16.9 %all-to-all-done.4 = f32[32,16,512]{2,1,0:T(8,128)S(1)} async-done(((f32[32,16,512]{2,1,0:T(8,128)}), f32[32,16,512]{2,1,0:T(8,128)S(1)}, u32[]{:S(2)}, u32[]{:S(2)}) %all-to-all-start.4) | async-done | bytes 1048608 | tf_op jit(solution)/shard_map/all_to_all | solution.py:83
  89.3 13.3 %all-to-all-start.5 = ((f32[32,16,512]{2,1,0:T(8,128)}), f32[32,16,512]{2,1,0:T(8,128)}, u32[]{:S(2)}, u32[]{:S(2)}) async-start(f32[32,16,512]{2,1,0:T(8,128)} %copy.35), calls=%async_computation.5 | async-start | bytes 2097152 | tf_op jit(solution)/shard_map/all_to_all | solution.py:84
  104.2 18.3 %all-to-all-done.5 = f32[32,16,512]{2,1,0:T(8,128)} async-done(((f32[32,16,512]{2,1,0:T(8,128)}), f32[32,16,512]{2,1,0:T(8,128)}, u32[]{:S(2)}, u32[]{:S(2)}) %all-to-all-start.5) | async-done | bytes 1048608 | tf_op jit(solution)/shard_map/all_to_all | solution.py:84
  122.5 13.3 %all-to-all-start.1 = ((f32[32,16,512]{2,1,0:T(8,128)}), f32[32,16,512]{2,1,0:T(8,128)S(1)}, u32[]{:S(2)}, u32[]{:S(2)}) async-start(f32[32,16,512]{2,1,0:T(8,128)} %copy.27), calls=%async_computation.1 | async-start | bytes 2097152 | tf_op jit(solution)/shard_map/all_to_all | solution.py:81
  137.3 18.2 %all-to-all-done.1 = f32[32,16,512]{2,1,0:T(8,128)S(1)} async-done(((f32[32,16,512]{2,1,0:T(8,128)}), f32[32,16,512]{2,1,0:T(8,128)S(1)}, u32[]{:S(2)}, u32[]{:S(2)}) %all-to-all-start.1) | async-done | bytes 1048608 | tf_op jit(solution)/shard_map/all_to_all | solution.py:81
  155.5 13.7 %all-to-all-start.2 = ((f32[32,16,512]{2,1,0:T(8,128)}), f32[32,16,512]{2,1,0:T(8,128)}, u32[]{:S(2)}, u32[]{:S(2)}) async-start(f32[32,16,512]{2,1,0:T(8,128)} %copy.29), calls=%async_computation.2 | async-start | bytes 2097152 | tf_op jit(solution)/shard_map/all_to_all | solution.py:82
  174.1 3.0 fusion.35
  177.1 3.0 fusion.29
  180.1 2.0 convolution_subtract_fusion.1
  182.1 6.5 %all-to-all-done.2 = f32[32,16,512]{2,1,0:T(8,128)} async-done(((f32[32,16,512]{2,1,0:T(8,128)}), f32[32,16,512]{2,1,0:T(8,128)}, u32[]{:S(2)}, u32[]{:S(2)}) %all-to-all-start.2) | async-done | bytes 1048608 | tf_op jit(solution)/shard_map/all_to_all | solution.py:82
  192.0 3.5 convolution_subtract_fusion.2
  195.5 3.3 convolution_add_fusion.1
  198.8 2.4 multiply_subtract_fusion.1
  205.2 2.1 fusion
  207.3 2.5 multiply_add_fusion
  211.6 13.3 %all-to-all-start.6 = ((f32[2,256,512]{2,0,1:T(2,128)}), f32[2,256,512]{2,0,1:T(2,128)S(1)}, u32[]{:S(2)}, u32[]{:S(2)}) async-start(f32[2,256,512]{2,0,1:T(2,128)} %copy.37), calls=%async_computation.6 | async-start | bytes 2097152 | tf_op jit(solution)/shard_map/all_to_all | solution.py:93
  226.7 18.0 %all-to-all-done.6 = f32[2,256,512]{2,0,1:T(2,128)S(1)} async-done(((f32[2,256,512]{2,0,1:T(2,128)}), f32[2,256,512]{2,0,1:T(2,128)S(1)}, u32[]{:S(2)}, u32[]{:S(2)}) %all-to-all-start.6) | async-done | bytes 1048608 | tf_op jit(solution)/shard_map/all_to_all | solution.py:93
  244.6 13.3 %all-to-all-start.7 = ((f32[2,256,512]{2,0,1:T(2,128)}), f32[2,256,512]{2,0,1:T(2,128)S(1)}, u32[]{:S(2)}, u32[]{:S(2)}) async-start(f32[2,256,512]{2,0,1:T(2,128)} %copy.39), calls=%async_computation.7 | async-start | bytes 2097152 | tf_op jit(solution)/shard_map/all_to_all | solution.py:94
  260.7 17.0 %all-to-all-done.7 = f32[2,256,512]{2,0,1:T(2,128)S(1)} async-done(((f32[2,256,512]{2,0,1:T(2,128)}), f32[2,256,512]{2,0,1:T(2,128)S(1)}, u32[]{:S(2)}, u32[]{:S(2)}) %all-to-all-start.7) | async-done | bytes 1048608 | tf_op jit(solution)/shard_map/all_to_all | solution.py:94
  281.0 26.8 %all_to_all.141 = f32[16,16,512]{2,1,0:T(8,128)S(1)} all-to-all(f32[16,16,512]{2,1,0:T(8,128)S(1)} %copy.41), channel_id=1, replica_groups=mesh['seq'=16,'chan'=16] {'seq'}, dimensions={0} | all-to-all | bytes 1048576 | tf_op jit(solution)/shard_map/all_to_all | solution.py:97
  310.5 104.4 %all-gather.3.cloned.1.call-done = bf16[256,8192]{1,0:T(8,128)(2,1)} async-done(((bf16[256,512]{1,0:T(8,128)(2,1)}), bf16[256,8192]{1,0:T(8,128)(2,1)}) %all-gather.3.cloned.1.call-update) | async-done | bytes 4194320 | tf_op jit(solution)/shard_map/all_gather | solution.py:101
  414.9 108.9 %all-gather.5.cloned.1.call-done = bf16[8192,512]{1,0:T(8,128)(2,1)} async-done(((bf16[512,512]{1,0:T(8,128)(2,1)}), bf16[8192,512]{1,0:T(8,128)(2,1)}) %all-gather.5.cloned.1.call-update) | async-done | bytes 8388624 | tf_op jit(solution)/shard_map/all_gather | solution.py:104
  523.8 7.7 %convolution_convert_fusion = bf16[256,512]{1,0:T(8,128)(2,1)} fusion(bf16[256,8192]{1,0:T(8,128)(2,1)} %all-gather.3.cloned.1.call-done, bf16[8192,512]{1,0:T(8,128)(2,1)} %all-gather.5.cloned.1.call-done), kind=kOutput, calls=%fused_computation.12 | convolution fusion | flops 2147614720 | bytes 12845056 | tf_op jit(solution)/shard_map/dot_general | solution.py:102
  (41 shorter events, 34.4 us)
Async XLA Ops:
  9.0 27.6 %all-to-all-start = ((f32[1,256,512]{2,0,1:T(1,128)}), f32[1,256,512]{2,0,1:T(1,128)S(1)}, u32[]{:S(2)}, u32[]{:S(2)}) async-start(f32[1,256,512]{2,0,1:T(1,128)} %copy.24), calls=%async_computation | async-start | bytes 1048576 | tf_op jit(solution)/shard_map/all_to_all | solution.py:74
  36.6 18.3 %all-to-all-start.3 = ((f32[1,256,512]{2,0,1:T(1,128)}), f32[1,256,512]{2,0,1:T(1,128)S(1)}, u32[]{:S(2)}, u32[]{:S(2)}) async-start(f32[1,256,512]{2,0,1:T(1,128)} %broadcast_in_dim.5), calls=%async_computation.3 | async-start | bytes 1048576 | tf_op jit(solution)/shard_map/all_to_all | solution.py:75
  61.6 27.7 %all-to-all-start.4 = ((f32[32,16,512]{2,1,0:T(8,128)}), f32[32,16,512]{2,1,0:T(8,128)S(1)}, u32[]{:S(2)}, u32[]{:S(2)}) async-start(f32[32,16,512]{2,1,0:T(8,128)} %copy.33), calls=%async_computation.4 | async-start | bytes 2097152 | tf_op jit(solution)/shard_map/all_to_all | solution.py:83
  89.3 33.1 %all-to-all-start.5 = ((f32[32,16,512]{2,1,0:T(8,128)}), f32[32,16,512]{2,1,0:T(8,128)}, u32[]{:S(2)}, u32[]{:S(2)}) async-start(f32[32,16,512]{2,1,0:T(8,128)} %copy.35), calls=%async_computation.5 | async-start | bytes 2097152 | tf_op jit(solution)/shard_map/all_to_all | solution.py:84
  122.5 33.0 %all-to-all-start.1 = ((f32[32,16,512]{2,1,0:T(8,128)}), f32[32,16,512]{2,1,0:T(8,128)S(1)}, u32[]{:S(2)}, u32[]{:S(2)}) async-start(f32[32,16,512]{2,1,0:T(8,128)} %copy.27), calls=%async_computation.1 | async-start | bytes 2097152 | tf_op jit(solution)/shard_map/all_to_all | solution.py:81
  155.5 15.3 %copy-start = (f32[32,16,512]{2,1,0:T(8,128)}, f32[32,16,512]{2,1,0:T(8,128)S(1)}, u32[]{:S(2)}) copy-start(f32[32,16,512]{2,1,0:T(8,128)S(1)} %all-to-all-done.1) | copy-start | bytes 3145732
  155.5 33.1 %all-to-all-start.2 = ((f32[32,16,512]{2,1,0:T(8,128)}), f32[32,16,512]{2,1,0:T(8,128)}, u32[]{:S(2)}, u32[]{:S(2)}) async-start(f32[32,16,512]{2,1,0:T(8,128)} %copy.29), calls=%async_computation.2 | async-start | bytes 2097152 | tf_op jit(solution)/shard_map/all_to_all | solution.py:82
  211.6 33.0 %all-to-all-start.6 = ((f32[2,256,512]{2,0,1:T(2,128)}), f32[2,256,512]{2,0,1:T(2,128)S(1)}, u32[]{:S(2)}, u32[]{:S(2)}) async-start(f32[2,256,512]{2,0,1:T(2,128)} %copy.37), calls=%async_computation.6 | async-start | bytes 2097152 | tf_op jit(solution)/shard_map/all_to_all | solution.py:93
  226.7 81.1 %copy-start.1 = (bf16[256,512]{1,0:T(8,128)(2,1)S(1)}, bf16[256,512]{1,0:T(8,128)(2,1)}, u32[]{:S(2)}) copy-start(bf16[256,512]{1,0:T(8,128)(2,1)} %param.8) | copy-start | bytes 786436
  226.7 81.1 %copy-start.2 = (f32[512]{0:T(512)S(1)}, f32[512]{0:T(512)}, u32[]{:S(2)}) copy-start(f32[512]{0:T(512)} %param.10) | copy-start | bytes 6148
  244.6 33.0 %all-to-all-start.7 = ((f32[2,256,512]{2,0,1:T(2,128)}), f32[2,256,512]{2,0,1:T(2,128)S(1)}, u32[]{:S(2)}, u32[]{:S(2)}) async-start(f32[2,256,512]{2,0,1:T(2,128)} %copy.39), calls=%async_computation.7 | async-start | bytes 2097152 | tf_op jit(solution)/shard_map/all_to_all | solution.py:94
  257.9 157.0 %all-gather.3.cloned.1.call-start = ((), (), s32[]{:S(2)}) async-start(), calls=%async_computation.9 | async-start | bytes 4456448 | tf_op jit(solution)/shard_map/all_gather | solution.py:101
  309.7 214.1 %all-gather.5.cloned.1.call-start = ((), (), s32[]{:S(2)}) async-start(), calls=%async_computation.10 | async-start | bytes 8912896 | tf_op jit(solution)/shard_map/all_gather | solution.py:104
Sparse Core Ops, SparseCore 0:
  309.8 105.0 all-gather.2
  417.6 106.1 all-gather.4
where the time goes:
time: 547 us; the launch traced here: 539 us
  waiting for transfers between devices  332 us (61%)
  starting transfers between devices  91.8 us (17%)
  matrix products  49.2 us (9%)
  blocking collectives  26.8 us (5%)
  local copies, waits for them, and re-layouts  21.7 us (4%)
  between operations  13.9 us (3%)
    all_gather x1, waiting for transfers between devices, body(): lax.all_gather(out_weight, 'seq', axis=0, tiled=True)  109 us
    all_gather x1, waiting for transfers between devices, body(): gathered = lax.all_gather(gated_out, 'chan', axis=1, tiled=True)  104 us
    all_to_all x1, blocking collectives, body(): lax.all_to_all(result, 'seq', split_axis=0, concat_axis=1, tiled=True)[0]  26.8 us
    all_to_all x1, waiting for transfers between devices, body(): lax.all_to_all(tap_im, 'seq', split_axis=0, concat_axis=1, tiled=True)  18.3 us
    all_to_all x1, waiting for transfers between devices, body(): lax.all_to_all(sig_re, 'seq', split_axis=0, concat_axis=1, tiled=True)  18.2 us
    all_to_all x1, waiting for transfers between devices, body(): lax.all_to_all(back_re, 'seq', split_axis=1, concat_axis=0, tiled=True)  18 us
    all_to_all x1, waiting for transfers between devices, body(): lax.all_to_all(inverse_imaginary, 'seq', split_axis=1, concat_axis=0, til...  17 us
    all_to_all x1, waiting for transfers between devices, body(): lax.all_to_all(tap_re, 'seq', split_axis=0, concat_axis=1, tiled=True)  16.9 us
  transfers between devices with their start and end apart: 10, of which 10 were waited for; matrix products, arithmetic and copies ran while one was open for 5% of the time, Pallas kernels for 0%

commit v1 on v0

v1 whole, which is shorter than its diff:
```python
import functools

import jax
import jax.numpy as jnp
import numpy as np
from jax import lax
from jax.experimental import pallas as pl
from jax.experimental.pallas import tpu as pltpu
from jax.sharding import Mesh
from jax.sharding import PartitionSpec as P

bf16 = jnp.bfloat16
f32 = jnp.float32
AXES = ("h", "y", "k", "x", "l")
SEQ = ("h", "y", "k")
CHAN = ("x", "l")
N = 1024
STEPS = 4
FREQS = 128
MIB = 1 << 20


def transform_tables():
    k = np.arange(N // 2)[:, None]
    a = np.arange(N // 2)[None, :]
    angle = 2.0 * np.pi * ((k * a) % N) / N
    re, im = np.cos(angle), -np.sin(angle)
    im[0] = 1.0 - 2.0 * (np.arange(N // 2) % 2)
    weight = np.full((N // 2, 1), 2.0 / N)
    weight[0] = 1.0 / N
    forward = np.concatenate([re.reshape(STEPS, FREQS, -1), im.reshape(STEPS, FREQS, -1)], 1)
    back = np.concatenate(
        [(re * weight).reshape(STEPS, FREQS, -1), (im * weight).reshape(STEPS, FREQS, -1)], 1
    ).transpose(0, 2, 1)

    def split(m):
        high = m.astype(np.float32).astype(jnp.bfloat16)
        low = (m - high.astype(np.float64)).astype(np.float32).astype(jnp.bfloat16)
        return np.stack([high, low], 1)

    return split(forward), split(back)


def lanes(rows):
    return lax.broadcasted_iota(jnp.int32, (rows, 128), 1)


def swap_groups(blocks):
    a0, a1, a2, a3 = blocks
    lane = lanes(a0.shape[0])
    low, even = lane < 64, (lane & 32) == 0
    roll = lambda v, n: pltpu.roll(v, n, 1)
    b0, b2 = jnp.where(low, a0, roll(a2, 64)), jnp.where(low, roll(a0, 64), a2)
    b1, b3 = jnp.where(low, a1, roll(a3, 64)), jnp.where(low, roll(a1, 64), a3)
    c0, c1 = jnp.where(even, b0, roll(b1, 32)), jnp.where(even, roll(b0, 96), b1)
    c2, c3 = jnp.where(even, b2, roll(b3, 32)), jnp.where(even, roll(b2, 96), b3)
    return c0, c1, c2, c3


def pack_kernel(key_ref, value_ref, taps_ref, out_ref):
    for v in range(4):
        cols = slice(v * 128, (v + 1) * 128)
        signal, taps = [], []
        for r in range(4):
            rows = slice(r * 64, (r + 1) * 64)
            signal.append(key_ref[rows, cols].astype(f32) * value_ref[rows, cols].astype(f32))
            taps.append(taps_ref[rows, cols])
        for which, blocks in enumerate((signal, taps)):
            for y, block in enumerate(swap_groups(blocks)):
                out_ref[v % 2, y, v // 2, which] = block.astype(bf16)


def pick(position, choices):
    return jnp.where(
        position == 0,
        choices[0],
        jnp.where(position == 1, choices[1], jnp.where(position == 2, choices[2], choices[3])),
    )


def conv_kernel(in_ref, fwd_ref, back_ref, *refs):
    out_refs, (sig, taps, spec_s, spec_t, prod, acc, spread) = refs[:4], refs[4:]
    step = pl.program_id(0)

    @pl.when(step == 0)
    def _():
        for which, dst in enumerate((sig, taps)):
            for h in range(2):
                for kk in range(2):
                    blocks = [in_ref[h * 8 + y * 2 + kk, which].astype(f32) for y in range(4)]
                    for r, block in enumerate(swap_groups(blocks)):
                        row = kk * 256 + r * 64
                        dst[row : row + 64, h * 128 : (h + 1) * 128] = block.astype(bf16)
        acc[...] = jnp.zeros_like(acc)

    dot = functools.partial(jnp.dot, preferred_element_type=f32)
    spec_s[...] = dot(fwd_ref[0], sig[...]) + dot(fwd_ref[1], sig[...])
    spec_t[...] = dot(fwd_ref[0], taps[...]) + dot(fwd_ref[1], taps[...])

    rows = 8
    position = lanes(rows) // 32
    row_id = lax.broadcasted_iota(jnp.int32, (rows, 128), 0)
    sign = (1 - 2 * (row_id & 1)).astype(f32)
    first_row = row_id == 0

    def rolled(v):
        return [v] + [pltpu.roll(v, 32 * i, 1) for i in (1, 2, 3)]

    def body(i, carry):
        base = pl.multiple_of(i * rows, rows)
        re, im = pl.ds(base, rows), pl.ds(base + FREQS, rows)
        left, right = slice(0, 128), slice(128, 256)
        s = [rolled(spec_s[part, side]) for side in (left, right) for part in (re, im)]
        t = [rolled(spec_t[part, side]) for side in (left, right) for part in (re, im)]
        total = [[None] * 4 for _ in range(2)]

        def add(tile, tap, src):
            terms = (tap[0] * src[0], tap[1] * src[1], tap[1] * src[0], tap[0] * src[1])
            for n, term in enumerate(terms):
                total[tile][n] = term if total[tile][n] is None else total[tile][n] + term

        for j in range(4):
            near = [pick(position, [t[part][(p - j) % 4] for p in range(4)]) for part in (0, 1)]
            far = [pick(position, [t[part][(p - j) % 4] for p in range(4)]) for part in (2, 3)]
            here = position >= j
            shifted = [jnp.where(here, s[part][j], 0.0) for part in (0, 1)]
            mixed = [jnp.where(here, s[part + 2][j], s[part][j]) for part in (0, 1)]
            add(0, near, shifted)
            add(1, near, mixed)
            add(1, far, shifted)
        special = jnp.logical_and(first_row, jnp.logical_and(step == 0, i == 0))
        prods = []
        for rr, ii, ri, ir in total:
            prods.append((rr - jnp.where(special, 0.0, ii), jnp.where(special, ii, ri + ir)))
        for part, dst in enumerate((re, im)):
            p0, p1 = prods[0][part], prods[1][part]
            q0, q1 = pltpu.roll(p0, 32, 1), pltpu.roll(p1, 32, 1)
            prod[dst, left] = p0 + sign * jnp.where(position >= 1, q0, 0.0)
            prod[dst, right] = p1 + sign * jnp.where(position >= 1, q1, q0)
        return carry

    lax.fori_loop(0, FREQS // rows, body, 0, unroll=2)
    whole = prod[...]
    high = whole.astype(bf16)
    low = (whole - high.astype(f32)).astype(bf16)
    acc[...] += dot(back_ref[0], high) + dot(back_ref[1], high) + dot(back_ref[0], low)

    @pl.when(step == STEPS - 1)
    def _():
        my_h, my_y = lax.axis_index("h"), lax.axis_index("y")
        for h in range(2):
            for kk in range(2):
                blocks = [
                    acc[kk * 256 + r * 64 : kk * 256 + (r + 1) * 64, h * 128 : (h + 1) * 128]
                    for r in range(4)
                ]
                for y, block in enumerate(swap_groups(blocks)):
                    spread[h, y, kk] = block.astype(bf16)
        for shift, out_ref in enumerate(out_refs):
            for far in range(2):
                out_ref[far] = spread[(my_h + far) % 2, (my_y + shift) % 4]


def gate_kernel(far, *refs):
    parts, (q0, k0, v0, q1, k1, v1, bias_ref, out_ref, held) = refs[:4], refs[4:]
    my_h, my_y, my_k = lax.axis_index("h"), lax.axis_index("y"), lax.axis_index("k")
    for shift, part in enumerate(parts):
        held[(my_y - shift + 4) % 4] = part[...]
    col = pl.multiple_of((my_k * 2 + (my_h + far) % 2) * 128, 128)
    cols = pl.ds(col, 128)
    bias = bias_ref[:, cols]
    for own, (q, k, v) in enumerate(((q0, k0, v0), (q1, k1, v1))):
        kk = (my_k + own) % 2
        blocks = swap_groups([held[y, kk].astype(f32) for y in range(4)])
        for r, conv in enumerate(blocks):
            rows = slice(r * 64, (r + 1) * 64)
            signal = k[rows, cols].astype(f32) * v[rows, cols].astype(f32)
            out_ref[own, rows, :] = (q[rows, cols].astype(f32) * (conv + bias * signal)).astype(bf16)


def project_kernel(far, last, *refs):
    g, w, rest = refs[:10], refs[10:20], refs[20:]
    if last:
        before, own_ref, other_ref, lhs, rhs, sems = rest
    else:
        out_ref, lhs, rhs, sems = rest
    ax = {a: lax.axis_index(a) for a in AXES}
    half = pl.multiple_of(((ax["h"] + far) % 2) * 128, 128)
    copies = []

    def start(src, dst):
        copy = pltpu.make_async_copy(src, dst, sems.at[len(copies)])
        copy.start()
        copies.append(copy)

    for dh in range(2):
        for which, (dy, parts) in enumerate(((0, (0, 1)), (3, (0, 1)), (1, (0, 1)), (2, (0,)), (2, (1,)))):
            src = w[dh * 5 + which]
            for p in parts:
                h, y, k = (ax["h"] + dh) % 2, (ax["y"] + dy) % 4, (ax["k"] + p) % 2
                row = pl.multiple_of((h * 8 + y * 2 + k) * 128, 128)
                piece = src.at[p] if len(parts) == 2 else src
                start(piece.at[pl.ds(half, 128)], rhs.at[pl.ds(row, 128)])
    for far_l in range(2):
        for which, (dx, parts) in enumerate(((0, (0, 1)), (3, (0, 1)), (1, (0, 1)), (2, (0,)), (2, (1,)))):
            src = g[far_l * 5 + which]
            x = (ax["x"] + dx) % 4
            for p in parts:
                piece = src.at[p] if len(parts) == 2 else src
                rows = pl.ds(p * 256, 256)
                for j in (1, 2, 3) if far_l else (0,):
                    col = pl.multiple_of((x * 4 + (ax["l"] + 4 - j) % 4) * 128, 128)
                    start(piece.at[j - 1] if far_l else piece, lhs.at[rows, pl.ds(col, 128)])
    for copy in copies:
        copy.wait()

    def tile(i, carry):
        rows = pl.ds(pl.multiple_of(i * 128, 128), 128)
        part = jnp.dot(lhs[rows, :], rhs[...], preferred_element_type=f32)
        if last:
            here = pl.ds(pl.multiple_of((i % 2) * 128, 128), 128)

            @pl.when(i < 2)
            def _():
                own_ref[here, :] = before[rows, :] + part

            @pl.when(i >= 2)
            def _():
                other_ref[here, :] = before[rows, :] + part
        else:
            out_ref[rows, :] = part
        return carry

    lax.fori_loop(0, 4, tile, 0)


VMEM = pl.BlockSpec(memory_space=pltpu.VMEM)
ANY = pl.BlockSpec(memory_space=pl.ANY)


def params(limit=48 * MIB, **kw):
    return pltpu.CompilerParams(vmem_limit_bytes=limit, **kw)


def pack(key_in, value_in, taps):
    return pl.pallas_call(
        pack_kernel,
        out_shape=jax.ShapeDtypeStruct((2, 4, 2, 2, 64, 128), bf16),
        in_specs=[VMEM] * 3,
        out_specs=VMEM,
        compiler_params=params(),
        name="pack",
    )(key_in, value_in, taps)


def convolve(received):
    fwd, back = transform_tables()
    out = jax.ShapeDtypeStruct((2, 2, 64, 128), bf16)
    whole = lambda shape: pl.BlockSpec(shape, lambda i: (0,) * len(shape))
    return pl.pallas_call(
        conv_kernel,
        grid=(STEPS,),
        out_shape=[out] * 4,
        in_specs=[
            whole((16, 2, 64, 128)),
            pl.BlockSpec((None, 2, 2 * FREQS, 512), lambda i: (i, 0, 0, 0)),
            pl.BlockSpec((None, 2, 512, 2 * FREQS), lambda i: (i, 0, 0, 0)),
        ],
        out_specs=[whole((2, 2, 64, 128))] * 4,
        scratch_shapes=[
            pltpu.VMEM((512, 256), bf16),
            pltpu.VMEM((512, 256), bf16),
            pltpu.VMEM((2 * FREQS, 256), f32),
            pltpu.VMEM((2 * FREQS, 256), f32),
            pltpu.VMEM((2 * FREQS, 256), f32),
            pltpu.VMEM((512, 256), f32),
            pltpu.VMEM((2, 4, 2, 64, 128), bf16),
        ],
        compiler_params=params(dimension_semantics=("arbitrary",)),
        name="convolve",
    )(received, jnp.asarray(fwd), jnp.asarray(back))


def gate(far, parts, own, partner, bias):
    return pl.pallas_call(
        functools.partial(gate_kernel, far),
        out_shape=jax.ShapeDtypeStruct((2, 256, 128), bf16),
        in_specs=[VMEM] * 11,
        out_specs=VMEM,
        scratch_shapes=[pltpu.VMEM((4, 2, 64, 128), bf16)],
        compiler_params=params(),
        name="gate",
    )(*parts, *own, *partner, bias)


def project(far, gated, weights, before=None):
    last = before is not None
    half = jax.ShapeDtypeStruct((256, 512), f32)
    return pl.pallas_call(
        functools.partial(project_kernel, far, last),
        out_shape=[half] * 2 if last else jax.ShapeDtypeStruct((512, 512), f32),
        in_specs=[ANY] * 20 + [VMEM] * last,
        out_specs=[VMEM] * 2 if last else VMEM,
        scratch_shapes=[
            pltpu.VMEM((512, 2048), bf16),
            pltpu.VMEM((2048, 512), bf16),
            pltpu.SemaphoreType.DMA((48,)),
        ],
        compiler_params=params(),
        name="project",
    )(*gated, *weights, *([before] if last else []))


def shift(v, axis, by):
    n = lax.axis_size(axis)
    return lax.ppermute(v, axis, [(i, (i + by) % n) for i in range(n)])


def ring(v, axis):
    up, down = shift(v, axis, 1), shift(v, axis, -1)
    return [v, up, down, shift(up[0], axis, 1), shift(down[1], axis, -1)]


def gather_gated(v):
    others = jnp.stack([shift(v, "l", j) for j in (1, 2, 3)], axis=1)
    return ring(v, "x") + ring(others, "x")


def body(query, key_in, value_in, filter_taps, conv_bias, out_weight):
    core = lax.axis_index("k")
    packed = pack(key_in, value_in, filter_taps).reshape(16, 2, 64, 128)
    own = (query, key_in, value_in)
    partner = tuple(shift(v, "k", 1) for v in own)
    keep = lax.dynamic_slice(out_weight, (core * 256, 0), (256, 512))
    give = lax.dynamic_slice(out_weight, ((1 - core) * 256, 0), (256, 512))
    weight = jnp.stack([keep, shift(give, "k", 1)])
    weights = ring(weight, "y")
    received = lax.all_to_all(packed, SEQ, split_axis=0, concat_axis=0, tiled=True)
    weights += ring(shift(weight, "h", 1), "y")

    to_y = convolve(received)
    parts = [to_y[0]] + [shift(to_y[s], "y", s) for s in (1, 2, 3)]
    crossing = shift(jnp.stack([p[1] for p in parts]), "h", 1)
    bias = conv_bias.reshape(1, 512)
    near = gather_gated(gate(0, [p[0] for p in parts], own, partner, bias))
    far = gather_gated(gate(1, [crossing[s] for s in range(4)], own, partner, bias))

    half = project(0, near, weights)
    mine, other = project(1, far, weights, half)
    return (mine + shift(other, "k", 1)).astype(bf16)


def solution(mesh):
    fine = Mesh(mesh.devices.reshape(2, 4, 2, 4, 4), AXES)
    block = P(SEQ, CHAN)
    return jax.shard_map(
        body,
        mesh=fine,
        in_specs=(block, block, block, block, P(CHAN), block),
        out_specs=block,
        check_vma=False,
    )
```

time: 547 us -> 168 us (0.31); the launches traced: 539 us -> 167 us
  waiting for transfers between devices: 332 us -> 40.7 us
  matrix products: 49.2 us -> 0 us
  Pallas kernels: 0 us -> 27.7 us
  blocking collectives: 26.8 us -> 0 us
  local copies, waits for them, and re-layouts: 21.7 us -> 8.17 us
  between operations: 13.9 us -> 0.4 us
    all_gather x2 -> x0, waiting for transfers between devices: 213 us -> none  [the longest x1 109 us: body(): lax.all_gather(out_weight, 'seq', axis=0, tiled=True)]
    all_to_all x8 -> x1, waiting for transfers between devices: 118 us -> 0.01 us  [body(): lax.all_to_all(packed, SEQ, split_axis=0, concat_axis=0, tiled=True)]
    all_to_all x8 -> x1, starting transfers between devices: 91.7 us -> 9.49 us  [body(): lax.all_to_all(packed, SEQ, split_axis=0, concat_axis=0, tiled=True)]
    ppermute x0 -> x40, starting transfers between devices: none -> 79.7 us  [shift(): return lax.ppermute(v, axis, [(i, (i + by) % n) for i in range(n)])]
    dot_general x19 -> x0, matrix products: 49.2 us -> none  [the longest x3 8.08 us: over_rows(): jnp.einsum('kbc,bj->kjc', imag_part, sine_tab, precision=best_precision)]
    ppermute x0 -> x40, waiting for transfers between devices: none -> 40.7 us  [shift(): return lax.ppermute(v, axis, [(i, (i + by) % n) for i in range(n)])]
    pallas_call x0 -> x6, Pallas kernels: none -> 27.7 us  [the longest x2 12.6 us: project(): pl.pallas_call(functools.partial(project_kernel, far, last), out_shape=[h...]
    all_to_all x1 -> x0, blocking collectives: 26.8 us -> none  [body(): lax.all_to_all(result, 'seq', split_axis=0, concat_axis=1, tiled=True)[0]]
  transfers between devices with their start and end apart: 10 -> 41, of which waited for: 10 -> 11; matrix products, arithmetic and copies ran while one was open for 5% -> 1% of each run, Pallas kernels for 0% -> 13%
where the time goes in v1:
time: 168 us; the launch traced here: 167 us
  starting transfers between devices  89.2 us (53%)
  waiting for transfers between devices  40.7 us (24%)
  Pallas kernels  27.7 us (16%)
  local copies, waits for them, and re-layouts  8.17 us (5%)
    ppermute x40, starting transfers between devices, shift(): return lax.ppermute(v, axis, [(i, (i + by) % n) for i in range(n)])  79.7 us
    ppermute x40, waiting for transfers between devices, shift(): return lax.ppermute(v, axis, [(i, (i + by) % n) for i in range(n)])  40.7 us
    pallas_call x2, Pallas kernels, project(): pl.pallas_call(functools.partial(project_kernel, far, last), out_shape=[h...  12.6 us
    pallas_call x1, Pallas kernels, convolve(): pl.pallas_call(conv_kernel, grid=(STEPS,), out_shape=[out] * 4, in_specs=...  11.2 us
    all_to_all x1, starting transfers between devices, body(): lax.all_to_all(packed, SEQ, split_axis=0, concat_axis=0, tiled=True)  9.49 us
    unnamed x26, local copies, waits for them, and re-layouts  6.15 us
  transfers between devices with their start and end apart: 41, of which 11 were waited for; matrix products, arithmetic and copies ran while one was open for 1% of the time, Pallas kernels for 13%

profile of v1, /device:TPU:1, one launch (start us, length us, event | category | flops | bytes accessed | tf_op | source)
XLA Modules:
  0.0 167.1 jit_solution(15365393216245600061)
XLA Ops:
  1.2 3.3 %collective-permute-start.18 = (bf16[256,512]{1,0:T(8,128)(2,1)S(1)}, bf16[256,512]{1,0:T(8,128)(2,1)S(1)}, u32[]{:S(2)}, u32[]{:S(2)}) collective-permute-start(bf16[256,512]{1,0:T(8,128)(2,1)S(1)} %get-tuple-element.18), channel_id=1, source_target_pairs={{0,16},{16,0},{1,17},{17,1},{2,18},{18,2},{3,19},{19,3},{4,20},{20... | collective-permute-start | bytes 786440 | tf_op jit(solution)/shard_map/ppermute | solution.py:316
  7.4 1.6 pack.1
  9.0 9.5 %all-to-all-start = ((bf16[16,2,64,128]{3,2,1,0:T(8,128)(2,1)}), bf16[16,2,64,128]{3,2,1,0:T(8,128)(2,1)S(1)}, u32[]{:S(2)}, u32[]{:S(2)}) async-start(bf16[16,2,64,128]{3,2,1,0:T(8,128)(2,1)} %bitcast), calls=%async_computation | async-start | bytes 1048576 | tf_op jit(solution)/shard_map/all_to_all | solution.py:338
  21.2 5.1 %collective-permute-start.23 = (bf16[2,256,512]{2,1,0:T(8,128)(2,1)S(1)}, bf16[2,256,512]{2,1,0:T(8,128)(2,1)S(1)}, u32[]{:S(2)}, u32[]{:S(2)}) collective-permute-start(bf16[2,256,512]{2,1,0:T(8,128)(2,1)S(1)} %pad_maximum_fusion.refs_10_), channel_id=1, source_target_pairs={{0,128},{128,0},{1,129},{129,1},{2,130},{130,2},{3,131},{131,3},{4... | collective-permute-start | bytes 1572872 | tf_op jit(solution)/shard_map/ppermute | solution.py:316
  26.3 12.8 %collective-permute-done.19.refs_11_ = bf16[2,256,512]{2,1,0:T(8,128)(2,1)S(1)} collective-permute-done((bf16[2,256,512]{2,1,0:T(8,128)(2,1)S(1)}, bf16[2,256,512]{2,1,0:T(8,128)(2,1)S(1)}, u32[]{:S(2)}, u32[]{:S(2)}) %collective-permute-start.19) | collective-permute-done | bytes 524320 | tf_op jit(solution)/shard_map/ppermute | solution.py:316
  39.8 1.6 copy-done.6
  41.4 1.6 copy-done.7
  43.0 11.2 %convolve.1 = (bf16[2,2,64,128]{3,2,1,0:T(8,128)(2,1)S(1)}, bf16[2,2,64,128]{3,2,1,0:T(8,128)(2,1)S(1)}, bf16[2,2,64,128]{3,2,1,0:T(8,128)(2,1)S(1)}, bf16[2,2,64,128]{3,2,1,0:T(8,128)(2,1)S(1)}) custom-call(bf16[16,2,64,128]{3,2,1,0:T(8,128)(2,1)S(1)} %all-to-all-done.in_ref, bf16[4,2,256,512]{3,2,1,0:T(8,128)(2,1)S(1)} %copy-done.6, ...), custom_call_target="tpu_custom_call" | custom-call | tf_op jit(solution)/shard_map/convolve/pallas_call | solution.py:260
  54.7 3.0 %collective-permute-done.2 = bf16[2,2,64,128]{3,2,1,0:T(8,128)(2,1)S(1)} collective-permute-done((bf16[2,2,64,128]{3,2,1,0:T(8,128)(2,1)S(1)}, bf16[2,2,64,128]{3,2,1,0:T(8,128)(2,1)S(1)}, u32[]{:S(2)}, u32[]{:S(2)}) %collective-permute-start.2) | collective-permute-done | bytes 65568 | tf_op jit(solution)/shard_map/ppermute | solution.py:316
  58.0 1.6 collective-permute-start.20
  59.6 2.7 %collective-permute-done.1 = bf16[2,2,64,128]{3,2,1,0:T(8,128)(2,1)S(1)} collective-permute-done((bf16[2,2,64,128]{3,2,1,0:T(8,128)(2,1)S(1)}, bf16[2,2,64,128]{3,2,1,0:T(8,128)(2,1)S(1)}, u32[]{:S(2)}, u32[]{:S(2)}) %collective-permute-start.1) | collective-permute-done | bytes 65568 | tf_op jit(solution)/shard_map/ppermute | solution.py:316
  62.3 4.3 %collective-permute-done = bf16[2,2,64,128]{3,2,1,0:T(8,128)(2,1)S(1)} collective-permute-done((bf16[2,2,64,128]{3,2,1,0:T(8,128)(2,1)S(1)}, bf16[2,2,64,128]{3,2,1,0:T(8,128)(2,1)S(1)}, u32[]{:S(2)}, u32[]{:S(2)}) %collective-permute-start) | collective-permute-done | bytes 65568 | tf_op jit(solution)/shard_map/ppermute | solution.py:316
  67.9 9.4 %collective-permute-start.32 = (bf16[2,256,128]{2,1,0:T(8,128)(2,1)S(1)}, bf16[2,256,128]{2,1,0:T(8,128)(2,1)S(1)}, u32[]{:S(2)}, u32[]{:S(2)}) collective-permute-start(bf16[2,256,128]{2,1,0:T(8,128)(2,1)S(1)} %gate.3.refs_0_), channel_id=1, source_target_pairs={{0,1},{1,2},{2,3},{3,0},{4,5},{5,6},{6,7},{7,4},{8,9},{9,10},{10,1... | collective-permute-start | bytes 393224 | tf_op jit(solution)/shard_map/ppermute | solution.py:316
  77.8 2.3 %collective-permute-start.34 = (bf16[2,256,128]{2,1,0:T(8,128)(2,1)S(1)}, bf16[2,256,128]{2,1,0:T(8,128)(2,1)S(1)}, u32[]{:S(2)}, u32[]{:S(2)}) collective-permute-start(bf16[2,256,128]{2,1,0:T(8,128)(2,1)S(1)} %gate.3.refs_0_), channel_id=1, source_target_pairs={{0,3},{1,0},{2,1},{3,2},{4,7},{5,4},{6,5},{7,6},{8,11},{9,8},{10,9... | collective-permute-start | bytes 393224 | tf_op jit(solution)/shard_map/ppermute | solution.py:316
  80.8 2.7 %collective-permute-start.25 = (bf16[2,256,512]{2,1,0:T(8,128)(2,1)S(1)}, bf16[2,256,512]{2,1,0:T(8,128)(2,1)S(1)}, u32[]{:S(2)}, u32[]{:S(2)}) collective-permute-start(bf16[2,256,512]{2,1,0:T(8,128)(2,1)S(1)} %collective-permute-done.23.refs_15_), channel_id=1, source_target_pairs={{0,96},{32,0},{64,32},{96,64},{1,97},{33,1},{65,33},{97,65},{2,98}... | collective-permute-start | bytes 1572872 | tf_op jit(solution)/shard_map/ppermute | solution.py:316
  84.8 1.5 collective-permute-start.29
  86.3 3.3 %collective-permute-done.3 = bf16[4,2,64,128]{3,2,1,0:T(8,128)(2,1)S(1)} collective-permute-done((bf16[4,2,64,128]{3,2,1,0:T(8,128)(2,1)S(1)}, bf16[4,2,64,128]{3,2,1,0:T(8,128)(2,1)S(1)}, u32[]{:S(2)}, u32[]{:S(2)}) %collective-permute-start.3) | collective-permute-done | bytes 131104 | tf_op jit(solution)/shard_map/ppermute | solution.py:316
  90.8 1.5 collective-permute-start.36
  93.5 4.3 %collective-permute-start.13 = (bf16[2,256,128]{2,1,0:T(8,128)(2,1)S(1)}, bf16[2,256,128]{2,1,0:T(8,128)(2,1)S(1)}, u32[]{:S(2)}, u32[]{:S(2)}) collective-permute-start(bf16[2,256,128]{2,1,0:T(8,128)(2,1)S(1)} %gate.2.refs_0_), channel_id=1, source_target_pairs={{0,3},{1,0},{2,1},{3,2},{4,7},{5,4},{6,5},{7,6},{8,11},{9,8},{10,9... | collective-permute-start | bytes 393224 | tf_op jit(solution)/shard_map/ppermute | solution.py:316
  98.7 3.5 %collective-permute-done.8.refs_2_ = bf16[2,256,128]{2,1,0:T(8,128)(2,1)S(1)} collective-permute-done((bf16[2,256,128]{2,1,0:T(8,128)(2,1)S(1)}, bf16[2,256,128]{2,1,0:T(8,128)(2,1)S(1)}, u32[]{:S(2)}, u32[]{:S(2)}) %collective-permute-start.8) | collective-permute-done | bytes 131104 | tf_op jit(solution)/shard_map/ppermute | solution.py:316
  103.6 2.7 %collective-permute-start.22 = (bf16[256,512]{1,0:T(8,128)(2,1)S(1)}, bf16[256,512]{1,0:T(8,128)(2,1)S(1)}, u32[]{:S(2)}, u32[]{:S(2)}) collective-permute-start(bf16[256,512]{1,0:T(8,128)(2,1)S(1)} %slice_bitcast_fusion.2), channel_id=1, source_target_pairs={{0,96},{32,0},{64,32},{96,64},{1,97},{33,1},{65,33},{97,65},{2,98}... | collective-permute-start | bytes 786440 | tf_op jit(solution)/shard_map/ppermute | solution.py:316
  109.0 2.1 %collective-permute-start.15 = (bf16[2,3,256,128]{3,2,1,0:T(8,128)(2,1)S(1)}, bf16[2,3,256,128]{3,2,1,0:T(8,128)(2,1)S(1)}, u32[]{:S(2)}, u32[]{:S(2)}) collective-permute-start(bf16[2,3,256,128]{3,2,1,0:T(8,128)(2,1)S(1)} %pad_maximum_fusion.1.refs_5_), channel_id=1, source_target_pairs={{0,12},{4,0},{8,4},{12,8},{1,13},{5,1},{9,5},{13,9},{2,14},{6,2},{... | collective-permute-start | bytes 1179656 | tf_op jit(solution)/shard_map/ppermute | solution.py:316
  111.2 5.1 %collective-permute-done.14.refs_6_ = bf16[2,3,256,128]{3,2,1,0:T(8,128)(2,1)S(1)} collective-permute-done((bf16[2,3,256,128]{3,2,1,0:T(8,128)(2,1)S(1)}, bf16[2,3,256,128]{3,2,1,0:T(8,128)(2,1)S(1)}, u32[]{:S(2)}, u32[]{:S(2)}) %collective-permute-start.14) | collective-permute-done | bytes 393248 | tf_op jit(solution)/shard_map/ppermute | solution.py:316
  116.6 2.7 %collective-permute-start.31 = (bf16[256,128]{1,0:T(8,128)(2,1)S(1)}, bf16[256,128]{1,0:T(8,128)(2,1)S(1)}, u32[]{:S(2)}, u32[]{:S(2)}) collective-permute-start(bf16[256,128]{1,0:T(8,128)(2,1)S(1)} %slice_bitcast_fusion.8), channel_id=1, source_target_pairs={{0,12},{4,0},{8,4},{12,8},{1,13},{5,1},{9,5},{13,9},{2,14},{6,2},{... | collective-permute-start | bytes 196616 | tf_op jit(solution)/shard_map/ppermute | solution.py:316
  119.3 2.7 %collective-permute-start.27 = (bf16[256,512]{1,0:T(8,128)(2,1)S(1)}, bf16[256,512]{1,0:T(8,128)(2,1)S(1)}, u32[]{:S(2)}, u32[]{:S(2)}) collective-permute-start(bf16[256,512]{1,0:T(8,128)(2,1)S(1)} %slice_bitcast_fusion), channel_id=1, source_target_pairs={{0,96},{32,0},{64,32},{96,64},{1,97},{33,1},{65,33},{97,65},{2,98}... | collective-permute-start | bytes 786440 | tf_op jit(solution)/shard_map/ppermute | solution.py:316
  122.1 2.7 %collective-permute-start.38 = (bf16[3,256,128]{2,1,0:T(8,128)(2,1)S(1)}, bf16[3,256,128]{2,1,0:T(8,128)(2,1)S(1)}, u32[]{:S(2)}, u32[]{:S(2)}) collective-permute-start(bf16[3,256,128]{2,1,0:T(8,128)(2,1)S(1)} %slice_bitcast_fusion.4), channel_id=1, source_target_pairs={{0,12},{4,0},{8,4},{12,8},{1,13},{5,1},{9,5},{13,9},{2,14},{6,2},{... | collective-permute-start | bytes 589832 | tf_op jit(solution)/shard_map/ppermute | solution.py:316
  124.8 2.7 %collective-permute-start.17 = (bf16[3,256,128]{2,1,0:T(8,128)(2,1)S(1)}, bf16[3,256,128]{2,1,0:T(8,128)(2,1)S(1)}, u32[]{:S(2)}, u32[]{:S(2)}) collective-permute-start(bf16[3,256,128]{2,1,0:T(8,128)(2,1)S(1)} %slice_bitcast_fusion.6), channel_id=1, source_target_pairs={{0,12},{4,0},{8,4},{12,8},{1,13},{5,1},{9,5},{13,9},{2,14},{6,2},{... | collective-permute-start | bytes 589832 | tf_op jit(solution)/shard_map/ppermute | solution.py:316
  127.5 2.6 %collective-permute-done.37.refs_8_ = bf16[3,256,128]{2,1,0:T(8,128)(2,1)S(1)} collective-permute-done((bf16[3,256,128]{2,1,0:T(8,128)(2,1)S(1)}, bf16[3,256,128]{2,1,0:T(8,128)(2,1)S(1)}, u32[]{:S(2)}, u32[]{:S(2)}) %collective-permute-start.37) | collective-permute-done | bytes 196640 | tf_op jit(solution)/shard_map/ppermute | solution.py:316
  130.1 6.4 %project.2.refs_20_ = f32[512,512]{1,0:T(8,128)} custom-call(bf16[2,256,128]{2,1,0:T(8,128)(2,1)S(1)} %gate.3.refs_0_, bf16[2,256,128]{2,1,0:T(8,128)(2,1)S(1)} %collective-permute-done.28.refs_1_, bf16[2,256,128]{2,1,0:T(8,128)(2,1)S(1)} %collective-permute-done.29.refs_2_, bf16[256,128]{1,0:T(8,128)(2,1)S(1)} %collective-permute-done.30.refs_3_, ...), custom_call_target="tpu_custom_call" | custom-call | tf_op jit(solution)/shard_map/project/pallas_call | solution.py:299
  136.6 6.2 %project.3 = (f32[256,512]{1,0:T(8,128)S(1)}, f32[256,512]{1,0:T(8,128)S(1)}) custom-call(bf16[2,256,128]{2,1,0:T(8,128)(2,1)S(1)} %gate.2.refs_0_, bf16[2,256,128]{2,1,0:T(8,128)(2,1)S(1)} %collective-permute-done.7.refs_1_, bf16[2,256,128]{2,1,0:T(8,128)(2,1)S(1)} %collective-permute-done.8.refs_2_, bf16[256,128]{1,0:T(8,128)(2,1)S(1)} %collective-permute-done.9.refs_3_, ...), custom_call_target="tpu_custom_call" | custom-call | tf_op jit(solution)/shard_map/project/pallas_call | solution.py:299
  142.8 22.0 %collective-permute-start.39 = (f32[256,512]{1,0:T(8,128)S(1)}, f32[256,512]{1,0:T(8,128)S(1)}, u32[]{:S(2)}, u32[]{:S(2)}) collective-permute-start(f32[256,512]{1,0:T(8,128)S(1)} %get-tuple-element.16), channel_id=1, source_target_pairs={{0,16},{16,0},{1,17},{17,1},{2,18},{18,2},{3,19},{19,3},{4,20},{20... | collective-permute-start | bytes 1572872 | tf_op jit(solution)/shard_map/ppermute | solution.py:316
  164.8 1.5 collective-permute-done.39
  (105 shorter events, 20.6 us)
Async XLA Ops:
  1.2 17.3 %collective-permute-start.18 = (bf16[256,512]{1,0:T(8,128)(2,1)S(1)}, bf16[256,512]{1,0:T(8,128)(2,1)S(1)}, u32[]{:S(2)}, u32[]{:S(2)}) collective-permute-start(bf16[256,512]{1,0:T(8,128)(2,1)S(1)} %get-tuple-element.18), channel_id=1, source_target_pairs={{0,16},{16,0},{1,17},{17,1},{2,18},{18,2},{3,19},{19,3},{4,20},{20... | collective-permute-start | bytes 786440 | tf_op jit(solution)/shard_map/ppermute | solution.py:316
  9.0 30.8 %all-to-all-start = ((bf16[16,2,64,128]{3,2,1,0:T(8,128)(2,1)}), bf16[16,2,64,128]{3,2,1,0:T(8,128)(2,1)S(1)}, u32[]{:S(2)}, u32[]{:S(2)}) async-start(bf16[16,2,64,128]{3,2,1,0:T(8,128)(2,1)} %bitcast), calls=%async_computation | async-start | bytes 1048576 | tf_op jit(solution)/shard_map/all_to_all | solution.py:338
  18.6 20.5 %collective-permute-start.19 = (bf16[2,256,512]{2,1,0:T(8,128)(2,1)S(1)}, bf16[2,256,512]{2,1,0:T(8,128)(2,1)S(1)}, u32[]{:S(2)}, u32[]{:S(2)}) collective-permute-start(bf16[2,256,512]{2,1,0:T(8,128)(2,1)S(1)} %pad_maximum_fusion.refs_10_), channel_id=1, source_target_pairs={{0,32},{32,64},{64,96},{96,0},{1,33},{33,65},{65,97},{97,1},{2,34}... | collective-permute-start | bytes 1572872 | tf_op jit(solution)/shard_map/ppermute | solution.py:316
  20.0 46.6 %collective-permute-start.5 = (bf16[256,512]{1,0:T(8,128)(2,1)S(1)}, bf16[256,512]{1,0:T(8,128)(2,1)S(1)}, u32[]{:S(2)}, u32[]{:S(2)}) collective-permute-start(bf16[256,512]{1,0:T(8,128)(2,1)S(1)} %copy-done.2), channel_id=1, source_target_pairs={{0,16},{16,0},{1,17},{17,1},{2,18},{18,2},{3,19},{19,3},{4,20},{20... | collective-permute-start | bytes 786440 | tf_op jit(solution)/shard_map/ppermute | solution.py:316
  20.7 46.0 %collective-permute-start.6 = (bf16[256,512]{1,0:T(8,128)(2,1)S(1)}, bf16[256,512]{1,0:T(8,128)(2,1)S(1)}, u32[]{:S(2)}, u32[]{:S(2)}) collective-permute-start(bf16[256,512]{1,0:T(8,128)(2,1)S(1)} %copy-done.4), channel_id=1, source_target_pairs={{0,16},{16,0},{1,17},{17,1},{2,18},{18,2},{3,19},{19,3},{4,20},{20... | collective-permute-start | bytes 786440 | tf_op jit(solution)/shard_map/ppermute | solution.py:316
  20.8 45.9 %collective-permute-start.4 = (bf16[256,512]{1,0:T(8,128)(2,1)S(1)}, bf16[256,512]{1,0:T(8,128)(2,1)}, u32[]{:S(2)}, u32[]{:S(2)}) collective-permute-start(bf16[256,512]{1,0:T(8,128)(2,1)S(1)} %copy-done.8), channel_id=1, source_target_pairs={{0,16},{16,0},{1,17},{17,1},{2,18},{18,2},{3,19},{19,3},{4,20},{20... | collective-permute-start | bytes 786440 | tf_op jit(solution)/shard_map/ppermute | solution.py:316
  21.2 36.8 %collective-permute-start.23 = (bf16[2,256,512]{2,1,0:T(8,128)(2,1)S(1)}, bf16[2,256,512]{2,1,0:T(8,128)(2,1)S(1)}, u32[]{:S(2)}, u32[]{:S(2)}) collective-permute-start(bf16[2,256,512]{2,1,0:T(8,128)(2,1)S(1)} %pad_maximum_fusion.refs_10_), channel_id=1, source_target_pairs={{0,128},{128,0},{1,129},{129,1},{2,130},{130,2},{3,131},{131,3},{4... | collective-permute-start | bytes 1572872 | tf_op jit(solution)/shard_map/ppermute | solution.py:316
  58.0 22.1 %collective-permute-start.20 = (bf16[2,256,512]{2,1,0:T(8,128)(2,1)S(1)}, bf16[2,256,512]{2,1,0:T(8,128)(2,1)S(1)}, u32[]{:S(2)}, u32[]{:S(2)}) collective-permute-start(bf16[2,256,512]{2,1,0:T(8,128)(2,1)S(1)} %pad_maximum_fusion.refs_10_), channel_id=1, source_target_pairs={{0,96},{32,0},{64,32},{96,64},{1,97},{33,1},{65,33},{97,65},{2,98}... | collective-permute-start | bytes 1572872 | tf_op jit(solution)/shard_map/ppermute | solution.py:316
  66.6 31.2 %collective-permute-start.24 = (bf16[2,256,512]{2,1,0:T(8,128)(2,1)S(1)}, bf16[2,256,512]{2,1,0:T(8,128)(2,1)S(1)}, u32[]{:S(2)}, u32[]{:S(2)}) collective-permute-start(bf16[2,256,512]{2,1,0:T(8,128)(2,1)S(1)} %collective-permute-done.23.refs_15_), channel_id=1, source_target_pairs={{0,32},{32,64},{64,96},{96,0},{1,33},{33,65},{65,97},{97,1},{2,34}... | collective-permute-start | bytes 1572872 | tf_op jit(solution)/shard_map/ppermute | solution.py:316
  67.9 12.9 %collective-permute-start.32 = (bf16[2,256,128]{2,1,0:T(8,128)(2,1)S(1)}, bf16[2,256,128]{2,1,0:T(8,128)(2,1)S(1)}, u32[]{:S(2)}, u32[]{:S(2)}) collective-permute-start(bf16[2,256,128]{2,1,0:T(8,128)(2,1)S(1)} %gate.3.refs_0_), channel_id=1, source_target_pairs={{0,1},{1,2},{2,3},{3,0},{4,5},{5,6},{6,7},{7,4},{8,9},{9,10},{10,1... | collective-permute-start | bytes 393224 | tf_op jit(solution)/shard_map/ppermute | solution.py:316
  77.8 6.9 %collective-permute-start.34 = (bf16[2,256,128]{2,1,0:T(8,128)(2,1)S(1)}, bf16[2,256,128]{2,1,0:T(8,128)(2,1)S(1)}, u32[]{:S(2)}, u32[]{:S(2)}) collective-permute-start(bf16[2,256,128]{2,1,0:T(8,128)(2,1)S(1)} %gate.3.refs_0_), channel_id=1, source_target_pairs={{0,3},{1,0},{2,1},{3,2},{4,7},{5,4},{6,5},{7,6},{8,11},{9,8},{10,9... | collective-permute-start | bytes 393224 | tf_op jit(solution)/shard_map/ppermute | solution.py:316
  80.1 9.4 %collective-permute-start.3 = (bf16[4,2,64,128]{3,2,1,0:T(8,128)(2,1)S(1)}, bf16[4,2,64,128]{3,2,1,0:T(8,128)(2,1)S(1)}, u32[]{:S(2)}, u32[]{:S(2)}) collective-permute-start(bf16[4,2,64,128]{3,2,1,0:T(8,128)(2,1)S(1)} %pad_maximum_fusion.3), channel_id=1, source_target_pairs={{0,128},{128,0},{1,129},{129,1},{2,130},{130,2},{3,131},{131,3},{4... | collective-permute-start | bytes 393224 | tf_op jit(solution)/shard_map/ppermute | solution.py:316
  80.8 17.2 %collective-permute-start.25 = (bf16[2,256,512]{2,1,0:T(8,128)(2,1)S(1)}, bf16[2,256,512]{2,1,0:T(8,128)(2,1)S(1)}, u32[]{:S(2)}, u32[]{:S(2)}) collective-permute-start(bf16[2,256,512]{2,1,0:T(8,128)(2,1)S(1)} %collective-permute-done.23.refs_15_), channel_id=1, source_target_pairs={{0,96},{32,0},{64,32},{96,64},{1,97},{33,1},{65,33},{97,65},{2,98}... | collective-permute-start | bytes 1572872 | tf_op jit(solution)/shard_map/ppermute | solution.py:316
  83.5 7.2 %collective-permute-start.28 = (bf16[2,256,128]{2,1,0:T(8,128)(2,1)S(1)}, bf16[2,256,128]{2,1,0:T(8,128)(2,1)S(1)}, u32[]{:S(2)}, u32[]{:S(2)}) collective-permute-start(bf16[2,256,128]{2,1,0:T(8,128)(2,1)S(1)} %gate.3.refs_0_), channel_id=1, source_target_pairs={{0,4},{4,8},{8,12},{12,0},{1,5},{5,9},{9,13},{13,1},{2,6},{6,10},{... | collective-permute-start | bytes 393224 | tf_op jit(solution)/shard_map/ppermute | solution.py:316
  84.8 8.8 %collective-permute-start.29 = (bf16[2,256,128]{2,1,0:T(8,128)(2,1)S(1)}, bf16[2,256,128]{2,1,0:T(8,128)(2,1)S(1)}, u32[]{:S(2)}, u32[]{:S(2)}) collective-permute-start(bf16[2,256,128]{2,1,0:T(8,128)(2,1)S(1)} %gate.3.refs_0_), channel_id=1, source_target_pairs={{0,12},{4,0},{8,4},{12,8},{1,13},{5,1},{9,5},{13,9},{2,14},{6,2},{... | collective-permute-start | bytes 393224 | tf_op jit(solution)/shard_map/ppermute | solution.py:316
  89.6 18.7 %collective-permute-start.35 = (bf16[2,3,256,128]{3,2,1,0:T(8,128)(2,1)S(1)}, bf16[2,3,256,128]{3,2,1,0:T(8,128)(2,1)S(1)}, u32[]{:S(2)}, u32[]{:S(2)}) collective-permute-start(bf16[2,3,256,128]{3,2,1,0:T(8,128)(2,1)S(1)} %pad_maximum_fusion.2.refs_5_), channel_id=1, source_target_pairs={{0,4},{4,8},{8,12},{12,0},{1,5},{5,9},{9,13},{13,1},{2,6},{6,10},{... | collective-permute-start | bytes 1179656 | tf_op jit(solution)/shard_map/ppermute | solution.py:316
  90.8 18.2 %collective-permute-start.36 = (bf16[2,3,256,128]{3,2,1,0:T(8,128)(2,1)S(1)}, bf16[2,3,256,128]{3,2,1,0:T(8,128)(2,1)S(1)}, u32[]{:S(2)}, u32[]{:S(2)}) collective-permute-start(bf16[2,3,256,128]{3,2,1,0:T(8,128)(2,1)S(1)} %pad_maximum_fusion.2.refs_5_), channel_id=1, source_target_pairs={{0,12},{4,0},{8,4},{12,8},{1,13},{5,1},{9,5},{13,9},{2,14},{6,2},{... | collective-permute-start | bytes 1179656 | tf_op jit(solution)/shard_map/ppermute | solution.py:316
  93.5 9.0 %collective-permute-start.13 = (bf16[2,256,128]{2,1,0:T(8,128)(2,1)S(1)}, bf16[2,256,128]{2,1,0:T(8,128)(2,1)S(1)}, u32[]{:S(2)}, u32[]{:S(2)}) collective-permute-start(bf16[2,256,128]{2,1,0:T(8,128)(2,1)S(1)} %gate.2.refs_0_), channel_id=1, source_target_pairs={{0,3},{1,0},{2,1},{3,2},{4,7},{5,4},{6,5},{7,6},{8,11},{9,8},{10,9... | collective-permute-start | bytes 393224 | tf_op jit(solution)/shard_map/ppermute | solution.py:316
  102.5 13.8 %collective-permute-start.21 = (bf16[256,512]{1,0:T(8,128)(2,1)S(1)}, bf16[256,512]{1,0:T(8,128)(2,1)S(1)}, u32[]{:S(2)}, u32[]{:S(2)}) collective-permute-start(bf16[256,512]{1,0:T(8,128)(2,1)S(1)} %copy-done.12), channel_id=1, source_target_pairs={{0,32},{32,64},{64,96},{96,0},{1,33},{33,65},{65,97},{97,1},{2,34}... | collective-permute-start | bytes 786440 | tf_op jit(solution)/shard_map/ppermute | solution.py:316
  103.6 13.0 %collective-permute-start.22 = (bf16[256,512]{1,0:T(8,128)(2,1)S(1)}, bf16[256,512]{1,0:T(8,128)(2,1)S(1)}, u32[]{:S(2)}, u32[]{:S(2)}) collective-permute-start(bf16[256,512]{1,0:T(8,128)(2,1)S(1)} %slice_bitcast_fusion.2), channel_id=1, source_target_pairs={{0,96},{32,0},{64,32},{96,64},{1,97},{33,1},{65,33},{97,65},{2,98}... | collective-permute-start | bytes 786440 | tf_op jit(solution)/shard_map/ppermute | solution.py:316
  107.0 17.7 %collective-permute-start.7 = (bf16[2,256,128]{2,1,0:T(8,128)(2,1)S(1)}, bf16[2,256,128]{2,1,0:T(8,128)(2,1)S(1)}, u32[]{:S(2)}, u32[]{:S(2)}) collective-permute-start(bf16[2,256,128]{2,1,0:T(8,128)(2,1)S(1)} %gate.2.refs_0_), channel_id=1, source_target_pairs={{0,4},{4,8},{8,12},{12,0},{1,5},{5,9},{9,13},{13,1},{2,6},{6,10},{... | collective-permute-start | bytes 393224 | tf_op jit(solution)/shard_map/ppermute | solution.py:316
  108.3 8.0 %collective-permute-start.14 = (bf16[2,3,256,128]{3,2,1,0:T(8,128)(2,1)S(1)}, bf16[2,3,256,128]{3,2,1,0:T(8,128)(2,1)S(1)}, u32[]{:S(2)}, u32[]{:S(2)}) collective-permute-start(bf16[2,3,256,128]{3,2,1,0:T(8,128)(2,1)S(1)} %pad_maximum_fusion.1.refs_5_), channel_id=1, source_target_pairs={{0,4},{4,8},{8,12},{12,0},{1,5},{5,9},{9,13},{13,1},{2,6},{6,10},{... | collective-permute-start | bytes 1179656 | tf_op jit(solution)/shard_map/ppermute | solution.py:316
  109.0 10.3 %collective-permute-start.15 = (bf16[2,3,256,128]{3,2,1,0:T(8,128)(2,1)S(1)}, bf16[2,3,256,128]{3,2,1,0:T(8,128)(2,1)S(1)}, u32[]{:S(2)}, u32[]{:S(2)}) collective-permute-start(bf16[2,3,256,128]{3,2,1,0:T(8,128)(2,1)S(1)} %pad_maximum_fusion.1.refs_5_), channel_id=1, source_target_pairs={{0,12},{4,0},{8,4},{12,8},{1,13},{5,1},{9,5},{13,9},{2,14},{6,2},{... | collective-permute-start | bytes 1179656 | tf_op jit(solution)/shard_map/ppermute | solution.py:316
  116.3 8.5 %collective-permute-start.26 = (bf16[256,512]{1,0:T(8,128)(2,1)S(1)}, bf16[256,512]{1,0:T(8,128)(2,1)S(1)}, u32[]{:S(2)}, u32[]{:S(2)}) collective-permute-start(bf16[256,512]{1,0:T(8,128)(2,1)S(1)} %slice_bitcast_fusion.1), channel_id=1, source_target_pairs={{0,32},{32,64},{64,96},{96,0},{1,33},{33,65},{65,97},{97,1},{2,34}... | collective-permute-start | bytes 786440 | tf_op jit(solution)/shard_map/ppermute | solution.py:316
  119.3 8.2 %collective-permute-start.27 = (bf16[256,512]{1,0:T(8,128)(2,1)S(1)}, bf16[256,512]{1,0:T(8,128)(2,1)S(1)}, u32[]{:S(2)}, u32[]{:S(2)}) collective-permute-start(bf16[256,512]{1,0:T(8,128)(2,1)S(1)} %slice_bitcast_fusion), channel_id=1, source_target_pairs={{0,96},{32,0},{64,32},{96,64},{1,97},{33,1},{65,33},{97,65},{2,98}... | collective-permute-start | bytes 786440 | tf_op jit(solution)/shard_map/ppermute | solution.py:316
  122.0 8.1 %collective-permute-start.37 = (bf16[3,256,128]{2,1,0:T(8,128)(2,1)S(1)}, bf16[3,256,128]{2,1,0:T(8,128)(2,1)S(1)}, u32[]{:S(2)}, u32[]{:S(2)}) collective-permute-start(bf16[3,256,128]{2,1,0:T(8,128)(2,1)S(1)} %slice_bitcast_fusion.5), channel_id=1, source_target_pairs={{0,4},{4,8},{8,12},{12,0},{1,5},{5,9},{9,13},{13,1},{2,6},{6,10},{... | collective-permute-start | bytes 589832 | tf_op jit(solution)/shard_map/ppermute | solution.py:316
  122.1 8.0 %collective-permute-start.38 = (bf16[3,256,128]{2,1,0:T(8,128)(2,1)S(1)}, bf16[3,256,128]{2,1,0:T(8,128)(2,1)S(1)}, u32[]{:S(2)}, u32[]{:S(2)}) collective-permute-start(bf16[3,256,128]{2,1,0:T(8,128)(2,1)S(1)} %slice_bitcast_fusion.4), channel_id=1, source_target_pairs={{0,12},{4,0},{8,4},{12,8},{1,13},{5,1},{9,5},{13,9},{2,14},{6,2},{... | collective-permute-start | bytes 589832 | tf_op jit(solution)/shard_map/ppermute | solution.py:316
  124.7 11.9 %collective-permute-start.16 = (bf16[3,256,128]{2,1,0:T(8,128)(2,1)S(1)}, bf16[3,256,128]{2,1,0:T(8,128)(2,1)S(1)}, u32[]{:S(2)}, u32[]{:S(2)}) collective-permute-start(bf16[3,256,128]{2,1,0:T(8,128)(2,1)S(1)} %slice_bitcast_fusion.7), channel_id=1, source_target_pairs={{0,4},{4,8},{8,12},{12,0},{1,5},{5,9},{9,13},{13,1},{2,6},{6,10},{... | collective-permute-start | bytes 589832 | tf_op jit(solution)/shard_map/ppermute | solution.py:316
  124.8 11.9 %collective-permute-start.17 = (bf16[3,256,128]{2,1,0:T(8,128)(2,1)S(1)}, bf16[3,256,128]{2,1,0:T(8,128)(2,1)S(1)}, u32[]{:S(2)}, u32[]{:S(2)}) collective-permute-start(bf16[3,256,128]{2,1,0:T(8,128)(2,1)S(1)} %slice_bitcast_fusion.6), channel_id=1, source_target_pairs={{0,12},{4,0},{8,4},{12,8},{1,13},{5,1},{9,5},{13,9},{2,14},{6,2},{... | collective-permute-start | bytes 589832 | tf_op jit(solution)/shard_map/ppermute | solution.py:316
  127.4 9.1 %collective-permute-start.10 = (bf16[256,128]{1,0:T(8,128)(2,1)S(1)}, bf16[256,128]{1,0:T(8,128)(2,1)S(1)}, u32[]{:S(2)}, u32[]{:S(2)}) collective-permute-start(bf16[256,128]{1,0:T(8,128)(2,1)S(1)} %slice_bitcast_fusion.10), channel_id=1, source_target_pairs={{0,12},{4,0},{8,4},{12,8},{1,13},{5,1},{9,5},{13,9},{2,14},{6,2},{... | collective-permute-start | bytes 196616 | tf_op jit(solution)/shard_map/ppermute | solution.py:316
  130.1 6.5 %collective-permute-start.9 = (bf16[256,128]{1,0:T(8,128)(2,1)S(1)}, bf16[256,128]{1,0:T(8,128)(2,1)S(1)}, u32[]{:S(2)}, u32[]{:S(2)}) collective-permute-start(bf16[256,128]{1,0:T(8,128)(2,1)S(1)} %slice_bitcast_fusion.11), channel_id=1, source_target_pairs={{0,4},{4,8},{8,12},{12,0},{1,5},{5,9},{9,13},{13,1},{2,6},{6,10},{... | collective-permute-start | bytes 196616 | tf_op jit(solution)/shard_map/ppermute | solution.py:316
  142.8 23.6 %collective-permute-start.39 = (f32[256,512]{1,0:T(8,128)S(1)}, f32[256,512]{1,0:T(8,128)S(1)}, u32[]{:S(2)}, u32[]{:S(2)}) collective-permute-start(f32[256,512]{1,0:T(8,128)S(1)} %get-tuple-element.16), channel_id=1, source_target_pairs={{0,16},{16,0},{1,17},{17,1},{2,18},{18,2},{3,19},{19,3},{4,20},{20... | collective-permute-start | bytes 1572872 | tf_op jit(solution)/shard_map/ppermute | solution.py:316
  (22 other events, 295.0 us)

commit v2 on v1

v2 whole, which is shorter than its diff:
```python
import functools

import jax
import jax.numpy as jnp
import numpy as np
from jax import lax
from jax.experimental import pallas as pl
from jax.experimental.pallas import tpu as pltpu
from jax.sharding import Mesh
from jax.sharding import PartitionSpec as P

bf16 = jnp.bfloat16
f32 = jnp.float32
AXES = ("h", "y", "k", "x", "l")
SEQ = ("h", "y", "k")
CHAN = ("x", "l")
N = 1024
STEPS = 4
FREQS = 128
MIB = 1 << 20


def transform_tables():
    k = np.arange(N // 2)[:, None]
    a = np.arange(N // 2)[None, :]
    angle = 2.0 * np.pi * ((k * a) % N) / N
    re, im = np.cos(angle), -np.sin(angle)
    im[0] = 1.0 - 2.0 * (np.arange(N // 2) % 2)
    weight = np.full((N // 2, 1), 2.0 / N)
    weight[0] = 1.0 / N
    forward = np.concatenate([re.reshape(STEPS, FREQS, -1), im.reshape(STEPS, FREQS, -1)], 1)
    back = np.concatenate(
        [(re * weight).reshape(STEPS, FREQS, -1), (im * weight).reshape(STEPS, FREQS, -1)], 1
    ).transpose(0, 2, 1)

    def split(m):
        high = m.astype(np.float32).astype(jnp.bfloat16)
        low = (m - high.astype(np.float64)).astype(np.float32).astype(jnp.bfloat16)
        return np.stack([high, low], 1)

    return split(forward), split(back)


def lanes(rows):
    return lax.broadcasted_iota(jnp.int32, (rows, 128), 1)


def swap_groups(blocks):
    a0, a1, a2, a3 = blocks
    lane = lanes(a0.shape[0])
    low, even = lane < 64, (lane & 32) == 0
    roll = lambda v, n: pltpu.roll(v, n, 1)
    b0, b2 = jnp.where(low, a0, roll(a2, 64)), jnp.where(low, roll(a0, 64), a2)
    b1, b3 = jnp.where(low, a1, roll(a3, 64)), jnp.where(low, roll(a1, 64), a3)
    c0, c1 = jnp.where(even, b0, roll(b1, 32)), jnp.where(even, roll(b0, 96), b1)
    c2, c3 = jnp.where(even, b2, roll(b3, 32)), jnp.where(even, roll(b2, 96), b3)
    return c0, c1, c2, c3


def fetch(pairs, sems):
    copies = [pltpu.make_async_copy(src, dst, sems.at[i]) for i, (src, dst) in enumerate(pairs)]
    for copy in copies:
        copy.start()
    return copies


def pack_kernel(key_hbm, value_hbm, taps_hbm, out_ref, key_ref, value_ref, taps_ref, sems):
    pairs = ((taps_hbm, taps_ref), (key_hbm, key_ref), (value_hbm, value_ref))
    copies = fetch(pairs, sems)

    def scatter(which, read):
        for v in range(4):
            cols = slice(v * 128, (v + 1) * 128)
            blocks = swap_groups([read(slice(r * 64, (r + 1) * 64), cols) for r in range(4)])
            for y, block in enumerate(blocks):
                out_ref[v % 2, y, v // 2, which] = block.astype(bf16)

    copies[0].wait()
    scatter(1, lambda rows, cols: taps_ref[rows, cols])
    copies[1].wait()
    copies[2].wait()
    scatter(0, lambda rows, cols: key_ref[rows, cols].astype(f32) * value_ref[rows, cols].astype(f32))


def pick(position, choices):
    return jnp.where(
        position == 0,
        choices[0],
        jnp.where(position == 1, choices[1], jnp.where(position == 2, choices[2], choices[3])),
    )


def conv_kernel(in_ref, fwd_hbm, back_hbm, *refs):
    out_refs, (fwd, back, both, spec, prod, acc, spread, sems) = refs[:4], refs[4:]
    tables = []
    for i in range(STEPS):
        tables += [(fwd_hbm.at[i], fwd.at[i]), (back_hbm.at[i], back.at[i])]
    copies = fetch(tables, sems)
    for which in range(2):
        for h in range(2):
            for kk in range(2):
                blocks = [in_ref[h * 8 + y * 2 + kk, which].astype(f32) for y in range(4)]
                for r, block in enumerate(swap_groups(blocks)):
                    row, col = kk * 256 + r * 64, which * 256 + h * 128
                    both[row : row + 64, col : col + 128] = block.astype(bf16)

    dot = functools.partial(jnp.dot, preferred_element_type=f32)
    rows = 8
    position = lanes(rows) // 32
    row_id = lax.broadcasted_iota(jnp.int32, (rows, 128), 0)
    sign = (1 - 2 * (row_id & 1)).astype(f32)
    first_row = row_id == 0

    def rolled(v):
        return [v] + [pltpu.roll(v, 32 * i, 1) for i in (1, 2, 3)]

    for step in range(STEPS):
        copies[2 * step].wait()
        spec[...] = dot(fwd[step, 0], both[...]) + dot(fwd[step, 1], both[...])

        def body(i, carry, step=step):
            base = pl.multiple_of(i * rows, rows)
            re, im = pl.ds(base, rows), pl.ds(base + FREQS, rows)
            left, right = slice(0, 128), slice(128, 256)
            s = [rolled(spec[part, side]) for side in (left, right) for part in (re, im)]
            left_t, right_t = slice(256, 384), slice(384, 512)
            t = [rolled(spec[part, side]) for side in (left_t, right_t) for part in (re, im)]
            total = [[None] * 4 for _ in range(2)]

            def add(tile, tap, src):
                terms = (tap[0] * src[0], tap[1] * src[1], tap[1] * src[0], tap[0] * src[1])
                for n, term in enumerate(terms):
                    total[tile][n] = term if total[tile][n] is None else total[tile][n] + term

            for j in range(4):
                near = [pick(position, [t[part][(p - j) % 4] for p in range(4)]) for part in (0, 1)]
                far = [pick(position, [t[part][(p - j) % 4] for p in range(4)]) for part in (2, 3)]
                here = position >= j
                shifted = [jnp.where(here, s[part][j], 0.0) for part in (0, 1)]
                mixed = [jnp.where(here, s[part + 2][j], s[part][j]) for part in (0, 1)]
                add(0, near, shifted)
                add(1, near, mixed)
                add(1, far, shifted)
            prods = []
            for rr, ii, ri, ir in total:
                if step == 0:
                    special = jnp.logical_and(first_row, i == 0)
                    pair = (rr - jnp.where(special, 0.0, ii), jnp.where(special, ii, ri + ir))
                else:
                    pair = (rr - ii, ri + ir)
                prods.append(pair)
            for part, dst in enumerate((re, im)):
                p0, p1 = prods[0][part], prods[1][part]
                q0, q1 = pltpu.roll(p0, 32, 1), pltpu.roll(p1, 32, 1)
                prod[dst, left] = p0 + sign * jnp.where(position >= 1, q0, 0.0)
                prod[dst, right] = p1 + sign * jnp.where(position >= 1, q1, q0)
            return carry

        lax.fori_loop(0, FREQS // rows, body, 0, unroll=8)
        whole = prod[...]
        high = whole.astype(bf16)
        low = (whole - high.astype(f32)).astype(bf16)
        copies[2 * step + 1].wait()
        part = dot(back[step, 0], high) + dot(back[step, 1], high) + dot(back[step, 0], low)
        acc[...] = part if step == 0 else acc[...] + part

    my_h, my_y = lax.axis_index("h"), lax.axis_index("y")
    for h in range(2):
        for kk in range(2):
            blocks = [
                acc[kk * 256 + r * 64 : kk * 256 + (r + 1) * 64, h * 128 : (h + 1) * 128]
                for r in range(4)
            ]
            for y, block in enumerate(swap_groups(blocks)):
                spread[h, y, kk] = block.astype(bf16)
    for shift, out_ref in enumerate(out_refs):
        for far in range(2):
            out_ref[far] = spread[(my_h + far) % 2, (my_y + shift) % 4]


def gate_kernel(far, *refs):
    parts, (q0, k0, v0, q1, k1, v1, bias_ref, out_ref, held) = refs[:4], refs[4:]
    my_h, my_y, my_k = lax.axis_index("h"), lax.axis_index("y"), lax.axis_index("k")
    for shift, part in enumerate(parts):
        held[(my_y - shift + 4) % 4] = part[...]
    col = pl.multiple_of((my_k * 2 + (my_h + far) % 2) * 128, 128)
    cols = pl.ds(col, 128)
    bias = bias_ref[:, cols]
    for own, (q, k, v) in enumerate(((q0, k0, v0), (q1, k1, v1))):
        kk = (my_k + own) % 2
        blocks = swap_groups([held[y, kk].astype(f32) for y in range(4)])
        for r, conv in enumerate(blocks):
            rows = slice(r * 64, (r + 1) * 64)
            signal = k[rows, cols].astype(f32) * v[rows, cols].astype(f32)
            out_ref[own, rows, :] = (q[rows, cols].astype(f32) * (conv + bias * signal)).astype(bf16)


def project_kernel(far, last, *refs):
    g, w, rest = refs[:5], refs[5:15], refs[15:]
    if last:
        before, own_ref, other_ref, lhs, rhs, sems = rest
    else:
        out_ref, lhs, rhs, sems = rest
    ax = {a: lax.axis_index(a) for a in AXES}
    half = pl.multiple_of(((ax["h"] + far) % 2) * 128, 128)
    swapped = (ax["k"] + ax["l"]) % 2
    places = ((0, (0, 1)), (3, (0, 1)), (1, (0, 1)), (2, (0,)), (2, (1,)))
    pairs = []
    for dh in range(2):
        for which, (dy, parts) in enumerate(places):
            src = w[dh * 5 + which]
            h, y = (ax["h"] + dh) % 2, (ax["y"] + dy) % 4
            row = pl.multiple_of((h * 4 + y) * 128, 128)
            for p in parts:
                col = pl.multiple_of(((swapped + p) % 2) * 512, 512)
                piece = src.at[p] if len(parts) == 2 else src
                pairs.append((piece.at[pl.ds(half, 128)], rhs.at[pl.ds(row, 128), pl.ds(col, 512)]))
    for which, (dx, parts) in enumerate(places):
        x = (ax["x"] + dx) % 4
        for p in parts:
            piece = g[which].at[p] if len(parts) == 2 else g[which]
            for j in range(2):
                pair = (ax["l"] // 2 + j) % 2
                col = pl.multiple_of((x * 2 + pair) * 128, 128)
                pairs.append((piece.at[j], lhs.at[pl.ds(p * 256, 256), pl.ds(col, 128)]))
    for copy in fetch(pairs, sems):
        copy.wait()

    def tile(i, carry):
        rows = pl.ds(pl.multiple_of(i * 128, 128), 128)
        part = jnp.dot(lhs[rows, :], rhs[...], preferred_element_type=f32)
        if last:
            here = pl.ds(pl.multiple_of((i % 2) * 128, 128), 128)

            @pl.when(i < 2)
            def _():
                own_ref[here, :] = before[rows, :] + part

            @pl.when(i >= 2)
            def _():
                other_ref[here, :] = before[rows, :] + part
        else:
            out_ref[rows, :] = part
        return carry

    lax.fori_loop(0, 4, tile, 0)


VMEM = pl.BlockSpec(memory_space=pltpu.VMEM)
ANY = pl.BlockSpec(memory_space=pl.ANY)


def params(limit=48 * MIB, **kw):
    return pltpu.CompilerParams(vmem_limit_bytes=limit, **kw)


def pack(key_in, value_in, taps):
    return pl.pallas_call(
        pack_kernel,
        out_shape=jax.ShapeDtypeStruct((2, 4, 2, 2, 64, 128), bf16),
        in_specs=[ANY] * 3,
        out_specs=VMEM,
        scratch_shapes=[
            pltpu.VMEM((256, 512), bf16),
            pltpu.VMEM((256, 512), bf16),
            pltpu.VMEM((256, 512), f32),
            pltpu.SemaphoreType.DMA((3,)),
        ],
        compiler_params=params(),
        name="pack",
    )(key_in, value_in, taps)


def convolve(received):
    fwd, back = transform_tables()
    return pl.pallas_call(
        conv_kernel,
        out_shape=[jax.ShapeDtypeStruct((2, 2, 64, 128), bf16)] * 4,
        in_specs=[VMEM, ANY, ANY],
        out_specs=[VMEM] * 4,
        scratch_shapes=[
            pltpu.VMEM(fwd.shape, bf16),
            pltpu.VMEM(back.shape, bf16),
            pltpu.VMEM((512, 512), bf16),
            pltpu.VMEM((2 * FREQS, 512), f32),
            pltpu.VMEM((2 * FREQS, 256), f32),
            pltpu.VMEM((512, 256), f32),
            pltpu.VMEM((2, 4, 2, 64, 128), bf16),
            pltpu.SemaphoreType.DMA((2 * STEPS,)),
        ],
        compiler_params=params(),
        name="convolve",
    )(received, jnp.asarray(fwd), jnp.asarray(back))


def gate(far, parts, own, partner, bias):
    return pl.pallas_call(
        functools.partial(gate_kernel, far),
        out_shape=jax.ShapeDtypeStruct((2, 256, 128), bf16),
        in_specs=[VMEM] * 11,
        out_specs=VMEM,
        scratch_shapes=[pltpu.VMEM((4, 2, 64, 128), bf16)],
        compiler_params=params(),
        name="gate",
    )(*parts, *own, *partner, bias)


def project(far, gated, weights, before=None):
    last = before is not None
    half = jax.ShapeDtypeStruct((256, 1024), f32)
    return pl.pallas_call(
        functools.partial(project_kernel, far, last),
        out_shape=[half] * 2 if last else jax.ShapeDtypeStruct((512, 1024), f32),
        in_specs=[ANY] * 15 + [VMEM] * last,
        out_specs=[VMEM] * 2 if last else VMEM,
        scratch_shapes=[
            pltpu.VMEM((512, 1024), bf16),
            pltpu.VMEM((1024, 1024), bf16),
            pltpu.SemaphoreType.DMA((32,)),
        ],
        compiler_params=params(),
        name="project",
    )(*gated, *weights, *([before] if last else []))


def shift(v, axis, by):
    n = lax.axis_size(axis)
    return lax.ppermute(v, axis, [(i, (i + by) % n) for i in range(n)])


def ring(v, axis):
    up, down = shift(v, axis, 1), shift(v, axis, -1)
    return [v, up, down, shift(up[0], axis, 1), shift(down[1], axis, -1)]


def gather_gated(v):
    partner = lax.ppermute(v, "l", [(i, i ^ 2) for i in range(4)])
    return ring(jnp.stack([v, partner], axis=1), "x")


def body(query, key_in, value_in, filter_taps, conv_bias, out_weight):
    core = lax.axis_index("k")
    own = (query, key_in, value_in)
    packed = pack(key_in, value_in, filter_taps).reshape(16, 2, 64, 128)
    partner = tuple(shift(v, "k", 1) for v in own)

    swaps = []
    for k in range(2):
        for l in range(4):
            to = (k, l) if k == l % 2 else (1 - k, l ^ 1)
            swaps.append((k * 4 + l, to[0] * 4 + to[1]))
    out_weight = lax.ppermute(out_weight, ("k", "l"), swaps)
    keep = lax.dynamic_slice(out_weight, (core * 256, 0), (256, 512))
    give = lax.dynamic_slice(out_weight, ((1 - core) * 256, 0), (256, 512))
    weight = jnp.stack([keep, shift(give, "k", 1)])

    received = lax.all_to_all(packed, SEQ, split_axis=0, concat_axis=0, tiled=True)
    weights = ring(weight, "y")
    received, partner, weights = lax.optimization_barrier((received, partner, weights))
    across = shift(weights[0], "h", 1)

    to_y = convolve(received)
    parts = [to_y[0]] + [shift(to_y[s], "y", s) for s in (1, 2, 3)]
    parts = lax.optimization_barrier(parts)
    crossing = shift(jnp.stack([p[1] for p in parts]), "h", 1)
    bias = conv_bias.reshape(1, 512)
    near = gather_gated(gate(0, [p[0] for p in parts], own, partner, bias))
    weights = weights + ring(across, "y")
    far = gather_gated(gate(1, [crossing[s] for s in range(4)], own, partner, bias))

    half = project(0, near, weights)
    mine, other = project(1, far, weights, half)
    total = mine + shift(other, "k", 1)
    beside = lax.ppermute(total[:, 512:].astype(bf16), "l", [(i, i ^ 1) for i in range(4)])
    return (total[:, :512] + beside.astype(f32)).astype(bf16)


def solution(mesh):
    fine = Mesh(mesh.devices.reshape(2, 4, 2, 4, 4), AXES)
    block = P(SEQ, CHAN)
    return jax.shard_map(
        body,
        mesh=fine,
        in_specs=(block, block, block, block, P(CHAN), block),
        out_specs=block,
        check_vma=False,
    )
```

time: 168 us -> 167 us (level)
  waiting for transfers between devices: 40.7 us -> 73 us
  starting transfers between devices: 89.2 us -> 61.6 us
  Pallas kernels: 27.7 us -> 22.7 us
    ppermute x40 -> x26, starting transfers between devices: 79.7 us -> 41.4 us  [shift(): return lax.ppermute(v, axis, [(i, (i + by) % n) for i in range(n)])]
    ppermute x0 -> x4, waiting for transfers between devices: none -> 33.1 us  [the longest x2 18.5 us: gather_gated(): partner = lax.ppermute(v, 'l', [(i, i ^ 2) for i in range(4)])]
    ppermute x0 -> x4, starting transfers between devices: none -> 9.09 us  [the longest x1 5.07 us: body(): out_weight = lax.ppermute(out_weight, ('k', 'l'), swaps)]
    ppermute x40 -> x26, waiting for transfers between devices: 40.7 us -> 32 us  [shift(): return lax.ppermute(v, axis, [(i, (i + by) % n) for i in range(n)])]
    all_to_all x1, waiting for transfers between devices: 0.01 us -> 7.98 us  [body(): lax.all_to_all(packed, SEQ, split_axis=0, concat_axis=0, tiled=True)]
    pallas_call x2, Pallas kernels: 12.6 us -> 9.9 us  [project(): pl.pallas_call(functools.partial(project_kernel, far, last), out_shape=[h...]
    pallas_call x2, Pallas kernels: 2.33 us -> 0.47 us  [gate(): pl.pallas_call(functools.partial(gate_kernel, far), out_shape=jax.ShapeDt...]
  transfers between devices with their start and end apart: 41 -> 31, of which waited for: 11 -> 15; matrix products, arithmetic and copies ran while one was open for 1% -> 1% of each run, Pallas kernels for 13% -> 4%
where the time goes in v2:
time: 167 us
  waiting for transfers between devices  73 us (44%)
  starting transfers between devices  61.6 us (37%)
  Pallas kernels  22.7 us (14%)
  local copies, waits for them, and re-layouts  6.94 us (4%)
  other arithmetic  2.26 us (1%)
    ppermute x26, starting transfers between devices, shift(): return lax.ppermute(v, axis, [(i, (i + by) % n) for i in range(n)])  41.4 us
    ppermute x26, waiting for transfers between devices, shift(): return lax.ppermute(v, axis, [(i, (i + by) % n) for i in range(n)])  32 us
    ppermute x2, waiting for transfers between devices, gather_gated(): partner = lax.ppermute(v, 'l', [(i, i ^ 2) for i in range(4)])  18.5 us
    all_to_all x1, starting transfers between devices, body(): lax.all_to_all(packed, SEQ, split_axis=0, concat_axis=0, tiled=True)  11.1 us
    pallas_call x1, Pallas kernels, convolve(): pl.pallas_call(conv_kernel, out_shape=[jax.ShapeDtypeStruct((2, 2, 64, 12...  10.7 us
    pallas_call x2, Pallas kernels, project(): pl.pallas_call(functools.partial(project_kernel, far, last), out_shape=[h...  9.9 us
    all_to_all x1, waiting for transfers between devices, body(): lax.all_to_all(packed, SEQ, split_axis=0, concat_axis=0, tiled=True)  7.98 us
    ppermute x1, waiting for transfers between devices, body(): lax.ppermute(total[:, 512:].astype(bf16), 'l', [(i, i ^ 1) for i in range...  7.51 us
  transfers between devices with their start and end apart: 31, of which 15 were waited for; matrix products, arithmetic and copies ran while one was open for 1% of the time, Pallas kernels for 4%

profile of v2, /device:TPU:1, one launch (start us, length us, event | category | flops | bytes accessed | tf_op | source)
XLA Modules:
  0.0 166.8 jit_solution(1179359007385537781)
XLA Ops:
  0.0 5.1 %collective-permute-start.3 = (bf16[512,512]{1,0:T(8,128)(2,1)}, bf16[512,512]{1,0:T(8,128)(2,1)S(1)}, u32[]{:S(2)}, u32[]{:S(2)}) collective-permute-start(bf16[512,512]{1,0:T(8,128)(2,1)} %param.13), channel_id=1, source_target_pairs={{0,0},{1,16},{2,2},{3,18},{16,1},{17,17},{18,3},{19,19},{4,4},{5,2... | collective-permute-start | bytes 1572872 | tf_op jit(solution)/shard_map/ppermute | solution.py:352
  5.1 7.1 %collective-permute-done.3 = bf16[512,512]{1,0:T(8,128)(2,1)S(1)} collective-permute-done((bf16[512,512]{1,0:T(8,128)(2,1)}, bf16[512,512]{1,0:T(8,128)(2,1)S(1)}, u32[]{:S(2)}, u32[]{:S(2)}) %collective-permute-start.3) | collective-permute-done | bytes 524320 | tf_op jit(solution)/shard_map/ppermute | solution.py:352
  13.9 2.8 %collective-permute-start.6 = (bf16[2,256,512]{2,1,0:T(8,128)(2,1)S(1)}, bf16[2,256,512]{2,1,0:T(8,128)(2,1)S(1)}, u32[]{:S(2)}, u32[]{:S(2)}) collective-permute-start(bf16[2,256,512]{2,1,0:T(8,128)(2,1)S(1)} %pad_maximum_fusion.refs_5_), channel_id=1, source_target_pairs={{0,96},{32,0},{64,32},{96,64},{1,97},{33,1},{65,33},{97,65},{2,98}... | collective-permute-start | bytes 1572872 | tf_op jit(solution)/shard_map/ppermute | solution.py:328
  16.7 1.6 pack.1
  18.4 11.1 %all-to-all-start = ((bf16[16,2,64,128]{3,2,1,0:T(8,128)(2,1)}), bf16[16,2,64,128]{3,2,1,0:T(8,128)(2,1)S(1)}, u32[]{:S(2)}, u32[]{:S(2)}) async-start(bf16[16,2,64,128]{3,2,1,0:T(8,128)(2,1)} %bitcast), calls=%async_computation | async-start | bytes 1048576 | tf_op jit(solution)/shard_map/all_to_all | solution.py:357
  30.9 2.8 %collective-permute-start.8 = (bf16[256,512]{1,0:T(8,128)(2,1)}, bf16[256,512]{1,0:T(8,128)(2,1)S(1)}, u32[]{:S(2)}, u32[]{:S(2)}) collective-permute-start(bf16[256,512]{1,0:T(8,128)(2,1)} %slice_bitcast_fusion.2), channel_id=1, source_target_pairs={{0,96},{32,0},{64,32},{96,64},{1,97},{33,1},{65,33},{97,65},{2,98}... | collective-permute-start | bytes 786440 | tf_op jit(solution)/shard_map/ppermute | solution.py:328
  36.5 8.0 %all-to-all-done.in_ref = bf16[16,2,64,128]{3,2,1,0:T(8,128)(2,1)S(1)} async-done(((bf16[16,2,64,128]{3,2,1,0:T(8,128)(2,1)}), bf16[16,2,64,128]{3,2,1,0:T(8,128)(2,1)S(1)}, u32[]{:S(2)}, u32[]{:S(2)}) %all-to-all-start) | async-done | bytes 524320 | tf_op jit(solution)/shard_map/all_to_all | solution.py:357
  44.5 2.1 %collective-permute-done.7.refs_8_ = bf16[256,512]{1,0:T(8,128)(2,1)S(1)} collective-permute-done((bf16[256,512]{1,0:T(8,128)(2,1)}, bf16[256,512]{1,0:T(8,128)(2,1)S(1)}, u32[]{:S(2)}, u32[]{:S(2)}) %collective-permute-start.7) | collective-permute-done | bytes 262176 | tf_op jit(solution)/shard_map/ppermute | solution.py:328
  46.6 1.6 copy-done.2
  48.2 1.6 copy-done.3
  49.8 10.7 %convolve.1 = (bf16[2,2,64,128]{3,2,1,0:T(8,128)(2,1)S(1)}, bf16[2,2,64,128]{3,2,1,0:T(8,128)(2,1)S(1)}, bf16[2,2,64,128]{3,2,1,0:T(8,128)(2,1)S(1)}, bf16[2,2,64,128]{3,2,1,0:T(8,128)(2,1)S(1)}) custom-call(bf16[16,2,64,128]{3,2,1,0:T(8,128)(2,1)S(1)} %all-to-all-done.in_ref, bf16[4,2,256,512]{3,2,1,0:T(8,128)(2,1)S(1)} %copy-done.3, ...), custom_call_target="tpu_custom_call" | custom-call | tf_op jit(solution)/shard_map/convolve/pallas_call | solution.py:276
  61.2 2.0 %collective-permute-start.11 = (bf16[2,2,64,128]{3,2,1,0:T(8,128)(2,1)S(1)}, bf16[2,2,64,128]{3,2,1,0:T(8,128)(2,1)S(1)}, u32[]{:S(2)}, u32[]{:S(2)}) collective-permute-start(bf16[2,2,64,128]{3,2,1,0:T(8,128)(2,1)S(1)} %get-tuple-element.28), channel_id=1, source_target_pairs={{0,96},{32,0},{64,32},{96,64},{1,97},{33,1},{65,33},{97,65},{2,98}... | collective-permute-start | bytes 196616 | tf_op jit(solution)/shard_map/ppermute | solution.py:328
  63.2 2.3 %collective-permute-done.9 = bf16[2,2,64,128]{3,2,1,0:T(8,128)(2,1)S(1)} collective-permute-done((bf16[2,2,64,128]{3,2,1,0:T(8,128)(2,1)S(1)}, bf16[2,2,64,128]{3,2,1,0:T(8,128)(2,1)S(1)}, u32[]{:S(2)}, u32[]{:S(2)}) %collective-permute-start.9) | collective-permute-done | bytes 65568 | tf_op jit(solution)/shard_map/ppermute | solution.py:328
  66.8 3.8 %collective-permute-start.23 = (bf16[2,256,128]{2,1,0:T(8,128)(2,1)S(1)}, bf16[2,256,128]{2,1,0:T(8,128)(2,1)S(1)}, u32[]{:S(2)}, u32[]{:S(2)}) collective-permute-start(bf16[2,256,128]{2,1,0:T(8,128)(2,1)S(1)} %gate.3), channel_id=1, source_target_pairs={{0,2},{1,3},{2,0},{3,1},{4,6},{5,7},{6,4},{7,5},{8,10},{9,11},{10,... | collective-permute-start | bytes 393224 | tf_op jit(solution)/shard_map/ppermute | solution.py:337
  71.6 4.5 %collective-permute-start.18 = (bf16[2,256,512]{2,1,0:T(8,128)(2,1)S(1)}, bf16[2,256,512]{2,1,0:T(8,128)(2,1)S(1)}, u32[]{:S(2)}, u32[]{:S(2)}) collective-permute-start(bf16[2,256,512]{2,1,0:T(8,128)(2,1)S(1)} %pad_maximum_fusion.refs_5_), channel_id=1, source_target_pairs={{0,128},{128,0},{1,129},{129,1},{2,130},{130,2},{3,131},{131,3},{4... | collective-permute-start | bytes 1572872 | tf_op jit(solution)/shard_map/ppermute | solution.py:328
  76.1 2.6 %collective-permute-start.25 = (bf16[2,2,256,128]{3,2,1,0:T(8,128)(2,1)S(1)}, bf16[2,2,256,128]{3,2,1,0:T(8,128)(2,1)S(1)}, u32[]{:S(2)}, u32[]{:S(2)}) collective-permute-start(bf16[2,2,256,128]{3,2,1,0:T(8,128)(2,1)S(1)} %pad_maximum_fusion.2.refs_0_), channel_id=1, source_target_pairs={{0,12},{4,0},{8,4},{12,8},{1,13},{5,1},{9,5},{13,9},{2,14},{6,2},{... | collective-permute-start | bytes 786440 | tf_op jit(solution)/shard_map/ppermute | solution.py:328
  78.7 8.7 %collective-permute-done.12 = bf16[4,2,64,128]{3,2,1,0:T(8,128)(2,1)S(1)} collective-permute-done((bf16[4,2,64,128]{3,2,1,0:T(8,128)(2,1)S(1)}, bf16[4,2,64,128]{3,2,1,0:T(8,128)(2,1)S(1)}, u32[]{:S(2)}, u32[]{:S(2)}) %collective-permute-start.12) | collective-permute-done | bytes 131104 | tf_op jit(solution)/shard_map/ppermute | solution.py:328
  89.0 18.5 %collective-permute-done.13 = bf16[2,256,128]{2,1,0:T(8,128)(2,1)S(1)} collective-permute-done((bf16[2,256,128]{2,1,0:T(8,128)(2,1)S(1)}, bf16[2,256,128]{2,1,0:T(8,128)(2,1)S(1)}, u32[]{:S(2)}, u32[]{:S(2)}) %collective-permute-start.13) | collective-permute-done | bytes 131104 | tf_op jit(solution)/shard_map/ppermute | solution.py:337
  107.6 2.6 %collective-permute-start.15 = (bf16[2,2,256,128]{3,2,1,0:T(8,128)(2,1)S(1)}, bf16[2,2,256,128]{3,2,1,0:T(8,128)(2,1)S(1)}, u32[]{:S(2)}, u32[]{:S(2)}) collective-permute-start(bf16[2,2,256,128]{3,2,1,0:T(8,128)(2,1)S(1)} %pad_maximum_fusion.1.refs_0_), channel_id=1, source_target_pairs={{0,12},{4,0},{8,4},{12,8},{1,13},{5,1},{9,5},{13,9},{2,14},{6,2},{... | collective-permute-start | bytes 786440 | tf_op jit(solution)/shard_map/ppermute | solution.py:328
  110.1 1.6 collective-permute-start.20
  111.7 2.8 %collective-permute-start.27 = (bf16[2,256,128]{2,1,0:T(8,128)(2,1)S(1)}, bf16[2,256,128]{2,1,0:T(8,128)(2,1)S(1)}, u32[]{:S(2)}, u32[]{:S(2)}) collective-permute-start(bf16[2,256,128]{2,1,0:T(8,128)(2,1)S(1)} %slice_bitcast_fusion.4), channel_id=1, source_target_pairs={{0,12},{4,0},{8,4},{12,8},{1,13},{5,1},{9,5},{13,9},{2,14},{6,2},{... | collective-permute-start | bytes 393224 | tf_op jit(solution)/shard_map/ppermute | solution.py:328
  116.4 2.1 %collective-permute-done.20.refs_12_ = bf16[2,256,512]{2,1,0:T(8,128)(2,1)S(1)} collective-permute-done((bf16[2,256,512]{2,1,0:T(8,128)(2,1)S(1)}, bf16[2,256,512]{2,1,0:T(8,128)(2,1)S(1)}, u32[]{:S(2)}, u32[]{:S(2)}) %collective-permute-start.20) | collective-permute-done | bytes 524320 | tf_op jit(solution)/shard_map/ppermute | solution.py:328
  118.5 2.4 %collective-permute-start.17 = (bf16[2,256,128]{2,1,0:T(8,128)(2,1)S(1)}, bf16[2,256,128]{2,1,0:T(8,128)(2,1)S(1)}, u32[]{:S(2)}, u32[]{:S(2)}) collective-permute-start(bf16[2,256,128]{2,1,0:T(8,128)(2,1)S(1)} %slice_bitcast_fusion.6), channel_id=1, source_target_pairs={{0,12},{4,0},{8,4},{12,8},{1,13},{5,1},{9,5},{13,9},{2,14},{6,2},{... | collective-permute-start | bytes 393224 | tf_op jit(solution)/shard_map/ppermute | solution.py:328
  120.9 3.1 %collective-permute-done.19.refs_11_ = bf16[2,256,512]{2,1,0:T(8,128)(2,1)S(1)} collective-permute-done((bf16[2,256,512]{2,1,0:T(8,128)(2,1)S(1)}, bf16[2,256,512]{2,1,0:T(8,128)(2,1)S(1)}, u32[]{:S(2)}, u32[]{:S(2)}) %collective-permute-start.19) | collective-permute-done | bytes 524320 | tf_op jit(solution)/shard_map/ppermute | solution.py:328
  124.0 1.5 collective-permute-start.21
  125.9 5.1 %collective-permute-done.22.refs_14_ = bf16[256,512]{1,0:T(8,128)(2,1)S(1)} collective-permute-done((bf16[256,512]{1,0:T(8,128)(2,1)S(1)}, bf16[256,512]{1,0:T(8,128)(2,1)S(1)}, u32[]{:S(2)}, u32[]{:S(2)}) %collective-permute-start.22) | collective-permute-done | bytes 262176 | tf_op jit(solution)/shard_map/ppermute | solution.py:328
  131.1 2.6 %collective-permute-done.21.refs_13_ = bf16[256,512]{1,0:T(8,128)(2,1)S(1)} collective-permute-done((bf16[256,512]{1,0:T(8,128)(2,1)S(1)}, bf16[256,512]{1,0:T(8,128)(2,1)S(1)}, u32[]{:S(2)}, u32[]{:S(2)}) %collective-permute-start.21) | collective-permute-done | bytes 262176 | tf_op jit(solution)/shard_map/ppermute | solution.py:328
  133.7 4.1 %project.2.refs_15_ = f32[512,1024]{1,0:T(8,128)} custom-call(bf16[2,2,256,128]{3,2,1,0:T(8,128)(2,1)S(1)} %pad_maximum_fusion.2.refs_0_, bf16[2,2,256,128]{3,2,1,0:T(8,128)(2,1)S(1)} %collective-permute-done.24.refs_1_, bf16[2,2,256,128]{3,2,1,0:T(8,128)(2,1)S(1)} %collective-permute-done.25.refs_2_, ...), custom_call_target="tpu_custom_call" | custom-call | tf_op jit(solution)/shard_map/project/pallas_call | solution.py:311
  137.7 5.8 %project.3 = (f32[256,1024]{1,0:T(8,128)}, f32[256,1024]{1,0:T(8,128)}) custom-call(bf16[2,2,256,128]{3,2,1,0:T(8,128)(2,1)S(1)} %pad_maximum_fusion.1.refs_0_, bf16[2,2,256,128]{3,2,1,0:T(8,128)(2,1)S(1)} %collective-permute-done.14.refs_1_, bf16[2,2,256,128]{3,2,1,0:T(8,128)(2,1)S(1)} %collective-permute-done.15.refs_2_, ...), custom_call_target="tpu_custom_call" | custom-call | tf_op jit(solution)/shard_map/project/pallas_call | solution.py:311
  143.6 10.9 %collective-permute-start.28 = (f32[256,1024]{1,0:T(8,128)}, f32[256,1024]{1,0:T(8,128)S(1)}, u32[]{:S(2)}, u32[]{:S(2)}) collective-permute-start(f32[256,1024]{1,0:T(8,128)} %get-tuple-element.42), channel_id=1, source_target_pairs={{0,16},{16,0},{1,17},{17,1},{2,18},{18,2},{3,19},{19,3},{4,20},{20... | collective-permute-start | bytes 3145736 | tf_op jit(solution)/shard_map/ppermute | solution.py:328
  154.5 2.5 %collective-permute-done.28 = f32[256,1024]{1,0:T(8,128)S(1)} collective-permute-done((f32[256,1024]{1,0:T(8,128)}, f32[256,1024]{1,0:T(8,128)S(1)}, u32[]{:S(2)}, u32[]{:S(2)}) %collective-permute-start.28) | collective-permute-done | bytes 1048608 | tf_op jit(solution)/shard_map/ppermute | solution.py:328
  158.5 7.5 %collective-permute-done.29 = bf16[256,512]{1,0:T(8,128)(2,1)S(1)} collective-permute-done((bf16[256,512]{1,0:T(8,128)(2,1)S(1)}, bf16[256,512]{1,0:T(8,128)(2,1)S(1)}, u32[]{:S(2)}, u32[]{:S(2)}) %collective-permute-start.29) | collective-permute-done | bytes 262176 | tf_op jit(solution)/shard_map/ppermute | solution.py:374
  (81 shorter events, 15.1 us)
Async XLA Ops:
  0.0 12.1 %collective-permute-start.3 = (bf16[512,512]{1,0:T(8,128)(2,1)}, bf16[512,512]{1,0:T(8,128)(2,1)S(1)}, u32[]{:S(2)}, u32[]{:S(2)}) collective-permute-start(bf16[512,512]{1,0:T(8,128)(2,1)} %param.13), channel_id=1, source_target_pairs={{0,0},{1,16},{2,2},{3,18},{16,1},{17,17},{18,3},{19,19},{4,4},{5,2... | collective-permute-start | bytes 1572872 | tf_op jit(solution)/shard_map/ppermute | solution.py:352
  12.2 1.6 collective-permute-start.4
  13.9 16.3 %collective-permute-start.6 = (bf16[2,256,512]{2,1,0:T(8,128)(2,1)S(1)}, bf16[2,256,512]{2,1,0:T(8,128)(2,1)S(1)}, u32[]{:S(2)}, u32[]{:S(2)}) collective-permute-start(bf16[2,256,512]{2,1,0:T(8,128)(2,1)S(1)} %pad_maximum_fusion.refs_5_), channel_id=1, source_target_pairs={{0,96},{32,0},{64,32},{96,64},{1,97},{33,1},{65,33},{97,65},{2,98}... | collective-permute-start | bytes 1572872 | tf_op jit(solution)/shard_map/ppermute | solution.py:328
  16.7 17.0 %collective-permute-start.5 = (bf16[2,256,512]{2,1,0:T(8,128)(2,1)S(1)}, bf16[2,256,512]{2,1,0:T(8,128)(2,1)S(1)}, u32[]{:S(2)}, u32[]{:S(2)}) collective-permute-start(bf16[2,256,512]{2,1,0:T(8,128)(2,1)S(1)} %pad_maximum_fusion.refs_5_), channel_id=1, source_target_pairs={{0,32},{32,64},{64,96},{96,0},{1,33},{33,65},{65,97},{97,1},{2,34}... | collective-permute-start | bytes 1572872 | tf_op jit(solution)/shard_map/ppermute | solution.py:328
  18.4 26.2 %all-to-all-start = ((bf16[16,2,64,128]{3,2,1,0:T(8,128)(2,1)}), bf16[16,2,64,128]{3,2,1,0:T(8,128)(2,1)S(1)}, u32[]{:S(2)}, u32[]{:S(2)}) async-start(bf16[16,2,64,128]{3,2,1,0:T(8,128)(2,1)} %bitcast), calls=%async_computation | async-start | bytes 1048576 | tf_op jit(solution)/shard_map/all_to_all | solution.py:357
  29.5 5.6 %collective-permute-start.1 = (bf16[256,512]{1,0:T(8,128)(2,1)S(1)}, bf16[256,512]{1,0:T(8,128)(2,1)S(1)}, u32[]{:S(2)}, u32[]{:S(2)}) collective-permute-start(bf16[256,512]{1,0:T(8,128)(2,1)S(1)} %copy-done), channel_id=1, source_target_pairs={{0,16},{16,0},{1,17},{17,1},{2,18},{18,2},{3,19},{19,3},{4,20},{20... | collective-permute-start | bytes 786440 | tf_op jit(solution)/shard_map/ppermute | solution.py:328
  29.7 6.2 %collective-permute-start.2 = (bf16[256,512]{1,0:T(8,128)(2,1)S(1)}, bf16[256,512]{1,0:T(8,128)(2,1)S(1)}, u32[]{:S(2)}, u32[]{:S(2)}) collective-permute-start(bf16[256,512]{1,0:T(8,128)(2,1)S(1)} %copy-done.1), channel_id=1, source_target_pairs={{0,16},{16,0},{1,17},{17,1},{2,18},{18,2},{3,19},{19,3},{4,20},{20... | collective-permute-start | bytes 786440 | tf_op jit(solution)/shard_map/ppermute | solution.py:328
  30.0 4.4 %collective-permute-start = (bf16[256,512]{1,0:T(8,128)(2,1)S(1)}, bf16[256,512]{1,0:T(8,128)(2,1)S(1)}, u32[]{:S(2)}, u32[]{:S(2)}) collective-permute-start(bf16[256,512]{1,0:T(8,128)(2,1)S(1)} %copy-done.4), channel_id=1, source_target_pairs={{0,16},{16,0},{1,17},{17,1},{2,18},{18,2},{3,19},{19,3},{4,20},{20... | collective-permute-start | bytes 786440 | tf_op jit(solution)/shard_map/ppermute | solution.py:328
  30.9 13.6 %collective-permute-start.8 = (bf16[256,512]{1,0:T(8,128)(2,1)}, bf16[256,512]{1,0:T(8,128)(2,1)S(1)}, u32[]{:S(2)}, u32[]{:S(2)}) collective-permute-start(bf16[256,512]{1,0:T(8,128)(2,1)} %slice_bitcast_fusion.2), channel_id=1, source_target_pairs={{0,96},{32,0},{64,32},{96,64},{1,97},{33,1},{65,33},{97,65},{2,98}... | collective-permute-start | bytes 786440 | tf_op jit(solution)/shard_map/ppermute | solution.py:328
  33.7 32.8 %copy-start.12 = (f32[512]{0:T(512)S(1)}, f32[512]{0:T(512)}, u32[]{:S(2)}) copy-start(f32[512]{0:T(512)} %param.12) | copy-start | bytes 6148
  34.4 12.2 %collective-permute-start.7 = (bf16[256,512]{1,0:T(8,128)(2,1)}, bf16[256,512]{1,0:T(8,128)(2,1)S(1)}, u32[]{:S(2)}, u32[]{:S(2)}) collective-permute-start(bf16[256,512]{1,0:T(8,128)(2,1)} %slice_bitcast_fusion.3), channel_id=1, source_target_pairs={{0,32},{32,64},{64,96},{96,0},{1,33},{33,65},{65,97},{97,1},{2,34}... | collective-permute-start | bytes 786440 | tf_op jit(solution)/shard_map/ppermute | solution.py:328
  60.5 5.1 %collective-permute-start.9 = (bf16[2,2,64,128]{3,2,1,0:T(8,128)(2,1)S(1)}, bf16[2,2,64,128]{3,2,1,0:T(8,128)(2,1)S(1)}, u32[]{:S(2)}, u32[]{:S(2)}) collective-permute-start(bf16[2,2,64,128]{3,2,1,0:T(8,128)(2,1)S(1)} %get-tuple-element.26), channel_id=1, source_target_pairs={{0,32},{32,64},{64,96},{96,0},{1,33},{33,65},{65,97},{97,1},{2,34}... | collective-permute-start | bytes 196616 | tf_op jit(solution)/shard_map/ppermute | solution.py:328
  60.6 5.0 %collective-permute-start.10 = (bf16[2,2,64,128]{3,2,1,0:T(8,128)(2,1)S(1)}, bf16[2,2,64,128]{3,2,1,0:T(8,128)(2,1)S(1)}, u32[]{:S(2)}, u32[]{:S(2)}) collective-permute-start(bf16[2,2,64,128]{3,2,1,0:T(8,128)(2,1)S(1)} %get-tuple-element.27), channel_id=1, source_target_pairs={{0,64},{32,96},{64,0},{96,32},{1,65},{33,97},{65,1},{97,33},{2,66}... | collective-permute-start | bytes 196616 | tf_op jit(solution)/shard_map/ppermute | solution.py:328
  61.2 5.2 %collective-permute-start.11 = (bf16[2,2,64,128]{3,2,1,0:T(8,128)(2,1)S(1)}, bf16[2,2,64,128]{3,2,1,0:T(8,128)(2,1)S(1)}, u32[]{:S(2)}, u32[]{:S(2)}) collective-permute-start(bf16[2,2,64,128]{3,2,1,0:T(8,128)(2,1)S(1)} %get-tuple-element.28), channel_id=1, source_target_pairs={{0,96},{32,0},{64,32},{96,64},{1,97},{33,1},{65,33},{97,65},{2,98}... | collective-permute-start | bytes 196616 | tf_op jit(solution)/shard_map/ppermute | solution.py:328
  66.8 9.3 %collective-permute-start.23 = (bf16[2,256,128]{2,1,0:T(8,128)(2,1)S(1)}, bf16[2,256,128]{2,1,0:T(8,128)(2,1)S(1)}, u32[]{:S(2)}, u32[]{:S(2)}) collective-permute-start(bf16[2,256,128]{2,1,0:T(8,128)(2,1)S(1)} %gate.3), channel_id=1, source_target_pairs={{0,2},{1,3},{2,0},{3,1},{4,6},{5,7},{6,4},{7,5},{8,10},{9,11},{10,... | collective-permute-start | bytes 393224 | tf_op jit(solution)/shard_map/ppermute | solution.py:337
  70.6 16.7 %collective-permute-start.12 = (bf16[4,2,64,128]{3,2,1,0:T(8,128)(2,1)S(1)}, bf16[4,2,64,128]{3,2,1,0:T(8,128)(2,1)S(1)}, u32[]{:S(2)}, u32[]{:S(2)}) collective-permute-start(bf16[4,2,64,128]{3,2,1,0:T(8,128)(2,1)S(1)} %pad_maximum_fusion.3), channel_id=1, source_target_pairs={{0,128},{128,0},{1,129},{129,1},{2,130},{130,2},{3,131},{131,3},{4... | collective-permute-start | bytes 393224 | tf_op jit(solution)/shard_map/ppermute | solution.py:328
  71.6 38.6 %collective-permute-start.18 = (bf16[2,256,512]{2,1,0:T(8,128)(2,1)S(1)}, bf16[2,256,512]{2,1,0:T(8,128)(2,1)S(1)}, u32[]{:S(2)}, u32[]{:S(2)}) collective-permute-start(bf16[2,256,512]{2,1,0:T(8,128)(2,1)S(1)} %pad_maximum_fusion.refs_5_), channel_id=1, source_target_pairs={{0,128},{128,0},{1,129},{129,1},{2,130},{130,2},{3,131},{131,3},{4... | collective-permute-start | bytes 1572872 | tf_op jit(solution)/shard_map/ppermute | solution.py:328
  76.1 35.6 %collective-permute-start.25 = (bf16[2,2,256,128]{3,2,1,0:T(8,128)(2,1)S(1)}, bf16[2,2,256,128]{3,2,1,0:T(8,128)(2,1)S(1)}, u32[]{:S(2)}, u32[]{:S(2)}) collective-permute-start(bf16[2,2,256,128]{3,2,1,0:T(8,128)(2,1)S(1)} %pad_maximum_fusion.2.refs_0_), channel_id=1, source_target_pairs={{0,12},{4,0},{8,4},{12,8},{1,13},{5,1},{9,5},{13,9},{2,14},{6,2},{... | collective-permute-start | bytes 786440 | tf_op jit(solution)/shard_map/ppermute | solution.py:328
  87.6 19.9 %collective-permute-start.13 = (bf16[2,256,128]{2,1,0:T(8,128)(2,1)S(1)}, bf16[2,256,128]{2,1,0:T(8,128)(2,1)S(1)}, u32[]{:S(2)}, u32[]{:S(2)}) collective-permute-start(bf16[2,256,128]{2,1,0:T(8,128)(2,1)S(1)} %gate.2), channel_id=1, source_target_pairs={{0,2},{1,3},{2,0},{3,1},{4,6},{5,7},{6,4},{7,5},{8,10},{9,11},{10,... | collective-permute-start | bytes 393224 | tf_op jit(solution)/shard_map/ppermute | solution.py:337
  87.7 26.8 %collective-permute-start.24 = (bf16[2,2,256,128]{3,2,1,0:T(8,128)(2,1)S(1)}, bf16[2,2,256,128]{3,2,1,0:T(8,128)(2,1)S(1)}, u32[]{:S(2)}, u32[]{:S(2)}) collective-permute-start(bf16[2,2,256,128]{3,2,1,0:T(8,128)(2,1)S(1)} %pad_maximum_fusion.2.refs_0_), channel_id=1, source_target_pairs={{0,4},{4,8},{8,12},{12,0},{1,5},{5,9},{9,13},{13,1},{2,6},{6,10},{... | collective-permute-start | bytes 786440 | tf_op jit(solution)/shard_map/ppermute | solution.py:328
  107.6 7.8 %collective-permute-start.15 = (bf16[2,2,256,128]{3,2,1,0:T(8,128)(2,1)S(1)}, bf16[2,2,256,128]{3,2,1,0:T(8,128)(2,1)S(1)}, u32[]{:S(2)}, u32[]{:S(2)}) collective-permute-start(bf16[2,2,256,128]{3,2,1,0:T(8,128)(2,1)S(1)} %pad_maximum_fusion.1.refs_0_), channel_id=1, source_target_pairs={{0,12},{4,0},{8,4},{12,8},{1,13},{5,1},{9,5},{13,9},{2,14},{6,2},{... | collective-permute-start | bytes 786440 | tf_op jit(solution)/shard_map/ppermute | solution.py:328
  110.1 13.9 %collective-permute-start.14 = (bf16[2,2,256,128]{3,2,1,0:T(8,128)(2,1)S(1)}, bf16[2,2,256,128]{3,2,1,0:T(8,128)(2,1)S(1)}, u32[]{:S(2)}, u32[]{:S(2)}) collective-permute-start(bf16[2,2,256,128]{3,2,1,0:T(8,128)(2,1)S(1)} %pad_maximum_fusion.1.refs_0_), channel_id=1, source_target_pairs={{0,4},{4,8},{8,12},{12,0},{1,5},{5,9},{9,13},{13,1},{2,6},{6,10},{... | collective-permute-start | bytes 786440 | tf_op jit(solution)/shard_map/ppermute | solution.py:328
  110.1 8.3 %collective-permute-start.20 = (bf16[2,256,512]{2,1,0:T(8,128)(2,1)S(1)}, bf16[2,256,512]{2,1,0:T(8,128)(2,1)S(1)}, u32[]{:S(2)}, u32[]{:S(2)}) collective-permute-start(bf16[2,256,512]{2,1,0:T(8,128)(2,1)S(1)} %collective-permute-done.18.refs_10_), channel_id=1, source_target_pairs={{0,96},{32,0},{64,32},{96,64},{1,97},{33,1},{65,33},{97,65},{2,98}... | collective-permute-start | bytes 1572872 | tf_op jit(solution)/shard_map/ppermute | solution.py:328
  111.7 13.9 %collective-permute-start.27 = (bf16[2,256,128]{2,1,0:T(8,128)(2,1)S(1)}, bf16[2,256,128]{2,1,0:T(8,128)(2,1)S(1)}, u32[]{:S(2)}, u32[]{:S(2)}) collective-permute-start(bf16[2,256,128]{2,1,0:T(8,128)(2,1)S(1)} %slice_bitcast_fusion.4), channel_id=1, source_target_pairs={{0,12},{4,0},{8,4},{12,8},{1,13},{5,1},{9,5},{13,9},{2,14},{6,2},{... | collective-permute-start | bytes 393224 | tf_op jit(solution)/shard_map/ppermute | solution.py:328
  114.5 9.5 %collective-permute-start.19 = (bf16[2,256,512]{2,1,0:T(8,128)(2,1)S(1)}, bf16[2,256,512]{2,1,0:T(8,128)(2,1)S(1)}, u32[]{:S(2)}, u32[]{:S(2)}) collective-permute-start(bf16[2,256,512]{2,1,0:T(8,128)(2,1)S(1)} %collective-permute-done.18.refs_10_), channel_id=1, source_target_pairs={{0,32},{32,64},{64,96},{96,0},{1,33},{33,65},{65,97},{97,1},{2,34}... | collective-permute-start | bytes 1572872 | tf_op jit(solution)/shard_map/ppermute | solution.py:328
  115.4 10.5 %collective-permute-start.26 = (bf16[2,256,128]{2,1,0:T(8,128)(2,1)S(1)}, bf16[2,256,128]{2,1,0:T(8,128)(2,1)S(1)}, u32[]{:S(2)}, u32[]{:S(2)}) collective-permute-start(bf16[2,256,128]{2,1,0:T(8,128)(2,1)S(1)} %slice_bitcast_fusion.5), channel_id=1, source_target_pairs={{0,4},{4,8},{8,12},{12,0},{1,5},{5,9},{9,13},{13,1},{2,6},{6,10},{... | collective-permute-start | bytes 393224 | tf_op jit(solution)/shard_map/ppermute | solution.py:328
  118.5 19.3 %collective-permute-start.17 = (bf16[2,256,128]{2,1,0:T(8,128)(2,1)S(1)}, bf16[2,256,128]{2,1,0:T(8,128)(2,1)S(1)}, u32[]{:S(2)}, u32[]{:S(2)}) collective-permute-start(bf16[2,256,128]{2,1,0:T(8,128)(2,1)S(1)} %slice_bitcast_fusion.6), channel_id=1, source_target_pairs={{0,12},{4,0},{8,4},{12,8},{1,13},{5,1},{9,5},{13,9},{2,14},{6,2},{... | collective-permute-start | bytes 393224 | tf_op jit(solution)/shard_map/ppermute | solution.py:328
  124.0 7.1 %collective-permute-start.22 = (bf16[256,512]{1,0:T(8,128)(2,1)S(1)}, bf16[256,512]{1,0:T(8,128)(2,1)S(1)}, u32[]{:S(2)}, u32[]{:S(2)}) collective-permute-start(bf16[256,512]{1,0:T(8,128)(2,1)S(1)} %slice_bitcast_fusion), channel_id=1, source_target_pairs={{0,96},{32,0},{64,32},{96,64},{1,97},{33,1},{65,33},{97,65},{2,98}... | collective-permute-start | bytes 786440 | tf_op jit(solution)/shard_map/ppermute | solution.py:328
  124.0 9.6 %collective-permute-start.21 = (bf16[256,512]{1,0:T(8,128)(2,1)S(1)}, bf16[256,512]{1,0:T(8,128)(2,1)S(1)}, u32[]{:S(2)}, u32[]{:S(2)}) collective-permute-start(bf16[256,512]{1,0:T(8,128)(2,1)S(1)} %slice_bitcast_fusion.1), channel_id=1, source_target_pairs={{0,32},{32,64},{64,96},{96,0},{1,33},{33,65},{65,97},{97,1},{2,34}... | collective-permute-start | bytes 786440 | tf_op jit(solution)/shard_map/ppermute | solution.py:328
  125.6 12.1 %collective-permute-start.16 = (bf16[2,256,128]{2,1,0:T(8,128)(2,1)S(1)}, bf16[2,256,128]{2,1,0:T(8,128)(2,1)S(1)}, u32[]{:S(2)}, u32[]{:S(2)}) collective-permute-start(bf16[2,256,128]{2,1,0:T(8,128)(2,1)S(1)} %slice_bitcast_fusion.7), channel_id=1, source_target_pairs={{0,4},{4,8},{8,12},{12,0},{1,5},{5,9},{9,13},{13,1},{2,6},{6,10},{... | collective-permute-start | bytes 393224 | tf_op jit(solution)/shard_map/ppermute | solution.py:328
  143.6 13.4 %collective-permute-start.28 = (f32[256,1024]{1,0:T(8,128)}, f32[256,1024]{1,0:T(8,128)S(1)}, u32[]{:S(2)}, u32[]{:S(2)}) collective-permute-start(f32[256,1024]{1,0:T(8,128)} %get-tuple-element.42), channel_id=1, source_target_pairs={{0,16},{16,0},{1,17},{17,1},{2,18},{18,2},{3,19},{19,3},{4,20},{20... | collective-permute-start | bytes 3145736 | tf_op jit(solution)/shard_map/ppermute | solution.py:328
  158.4 7.6 %collective-permute-start.29 = (bf16[256,512]{1,0:T(8,128)(2,1)S(1)}, bf16[256,512]{1,0:T(8,128)(2,1)S(1)}, u32[]{:S(2)}, u32[]{:S(2)}) collective-permute-start(bf16[256,512]{1,0:T(8,128)(2,1)S(1)} %slice.123), channel_id=1, source_target_pairs={{0,1},{1,0},{2,3},{3,2},{4,5},{5,4},{6,7},{7,6},{8,9},{9,8},{10,11... | collective-permute-start | bytes 786440 | tf_op jit(solution)/shard_map/ppermute | solution.py:374
  (12 other events, 123.3 us)

commit v3 on v2

v3 whole, which is shorter than its diff:
```python
import functools

import jax
import jax.numpy as jnp
import numpy as np
from jax import lax
from jax.experimental import pallas as pl
from jax.experimental.pallas import tpu as pltpu
from jax.sharding import Mesh
from jax.sharding import PartitionSpec as P

bf16 = jnp.bfloat16
f32 = jnp.float32
AXES = ("h", "y", "k", "x", "l")
SEQ = ("h", "y", "k")
CHAN = ("x", "l")
N = 1024
STEPS = 4
FREQS = 128
MIB = 1 << 20
LARGE = 60 * MIB


def transform_tables():
    k = np.arange(N // 2)[:, None]
    a = np.arange(N // 2)[None, :]
    angle = 2.0 * np.pi * ((k * a) % N) / N
    re, im = np.cos(angle), -np.sin(angle)
    im[0] = 1.0 - 2.0 * (np.arange(N // 2) % 2)
    weight = np.full((N // 2, 1), 2.0 / N)
    weight[0] = 1.0 / N
    forward = np.concatenate([re.reshape(STEPS, FREQS, -1), im.reshape(STEPS, FREQS, -1)], 1)
    back = np.concatenate(
        [(re * weight).reshape(STEPS, FREQS, -1), (im * weight).reshape(STEPS, FREQS, -1)], 1
    ).transpose(0, 2, 1)

    def split(m):
        high = m.astype(np.float32).astype(jnp.bfloat16)
        low = (m - high.astype(np.float64)).astype(np.float32).astype(jnp.bfloat16)
        return np.stack([high, low], 1)

    return split(forward), split(back)


def lanes(rows):
    return lax.broadcasted_iota(jnp.int32, (rows, 128), 1)


def swap_groups(blocks):
    a0, a1, a2, a3 = blocks
    lane = lanes(a0.shape[0])
    low, even = lane < 64, (lane & 32) == 0
    roll = lambda v, n: pltpu.roll(v, n, 1)
    b0, b2 = jnp.where(low, a0, roll(a2, 64)), jnp.where(low, roll(a0, 64), a2)
    b1, b3 = jnp.where(low, a1, roll(a3, 64)), jnp.where(low, roll(a1, 64), a3)
    c0, c1 = jnp.where(even, b0, roll(b1, 32)), jnp.where(even, roll(b0, 96), b1)
    c2, c3 = jnp.where(even, b2, roll(b3, 32)), jnp.where(even, roll(b2, 96), b3)
    return c0, c1, c2, c3


def fetch(pairs, sems):
    copies = [pltpu.make_async_copy(src, dst, sems.at[i]) for i, (src, dst) in enumerate(pairs)]
    for copy in copies:
        copy.start()
    return copies


def pack_kernel(query_hbm, key_hbm, value_hbm, taps_hbm, out_ref, keep_ref, give_ref, *scratch):
    query_ref, key_ref, value_ref, taps_ref, sems = scratch
    pairs = (
        (taps_hbm, taps_ref),
        (key_hbm, key_ref),
        (value_hbm, value_ref),
        (query_hbm, query_ref),
    )
    copies = fetch(pairs, sems)
    core = lax.axis_index("k")

    def scatter(which, read):
        for v in range(4):
            cols = slice(v * 128, (v + 1) * 128)
            blocks = swap_groups([read(slice(r * 64, (r + 1) * 64), cols) for r in range(4)])
            for y, block in enumerate(blocks):
                out_ref[v % 2, y, v // 2, which] = block.astype(bf16)

    copies[0].wait()
    scatter(1, lambda rows, cols: taps_ref[rows, cols])
    copies[1].wait()
    copies[2].wait()
    scatter(0, lambda rows, cols: key_ref[rows, cols].astype(f32) * value_ref[rows, cols].astype(f32))
    copies[3].wait()
    for i, ref in enumerate((query_ref, key_ref, value_ref)):
        for dst, half in ((keep_ref, core), (give_ref, 1 - core)):
            dst[i] = ref[:, pl.ds(pl.multiple_of(half * 256, 256), 256)]


def pick(position, choices):
    return jnp.where(
        position == 0,
        choices[0],
        jnp.where(position == 1, choices[1], jnp.where(position == 2, choices[2], choices[3])),
    )


def conv_kernel(in_ref, fwd_hbm, back_hbm, *refs):
    out_ref, fwd, back, both, spec, prod, acc, sems = refs
    tables = []
    for i in range(STEPS):
        tables += [(fwd_hbm.at[i], fwd.at[i]), (back_hbm.at[i], back.at[i])]
    copies = fetch(tables, sems)
    for which in range(2):
        for h in range(2):
            for kk in range(2):
                blocks = [in_ref[h * 8 + y * 2 + kk, which].astype(f32) for y in range(4)]
                for r, block in enumerate(swap_groups(blocks)):
                    row, col = kk * 256 + r * 64, which * 256 + h * 128
                    both[row : row + 64, col : col + 128] = block.astype(bf16)

    dot = functools.partial(jnp.dot, preferred_element_type=f32)
    rows = 8
    position = lanes(rows) // 32
    row_id = lax.broadcasted_iota(jnp.int32, (rows, 128), 0)
    sign = (1 - 2 * (row_id & 1)).astype(f32)
    first_row = row_id == 0

    def rolled(v):
        return [v] + [pltpu.roll(v, 32 * i, 1) for i in (1, 2, 3)]

    for step in range(STEPS):
        copies[2 * step].wait()
        spec[...] = dot(fwd[step, 0], both[...]) + dot(fwd[step, 1], both[...])

        def body(i, carry, step=step):
            base = pl.multiple_of(i * rows, rows)
            re, im = pl.ds(base, rows), pl.ds(base + FREQS, rows)
            left, right = slice(0, 128), slice(128, 256)
            s = [rolled(spec[part, side]) for side in (left, right) for part in (re, im)]
            left_t, right_t = slice(256, 384), slice(384, 512)
            t = [rolled(spec[part, side]) for side in (left_t, right_t) for part in (re, im)]
            total = [[None] * 4 for _ in range(2)]

            def add(tile, tap, src):
                terms = (tap[0] * src[0], tap[1] * src[1], tap[1] * src[0], tap[0] * src[1])
                for n, term in enumerate(terms):
                    total[tile][n] = term if total[tile][n] is None else total[tile][n] + term

            for j in range(4):
                near = [pick(position, [t[part][(p - j) % 4] for p in range(4)]) for part in (0, 1)]
                far = [pick(position, [t[part][(p - j) % 4] for p in range(4)]) for part in (2, 3)]
                here = position >= j
                shifted = [jnp.where(here, s[part][j], 0.0) for part in (0, 1)]
                mixed = [jnp.where(here, s[part + 2][j], s[part][j]) for part in (0, 1)]
                add(0, near, shifted)
                add(1, near, mixed)
                add(1, far, shifted)
            prods = []
            for rr, ii, ri, ir in total:
                if step == 0:
                    special = jnp.logical_and(first_row, i == 0)
                    pair = (rr - jnp.where(special, 0.0, ii), jnp.where(special, ii, ri + ir))
                else:
                    pair = (rr - ii, ri + ir)
                prods.append(pair)
            for part, dst in enumerate((re, im)):
                p0, p1 = prods[0][part], prods[1][part]
                q0, q1 = pltpu.roll(p0, 32, 1), pltpu.roll(p1, 32, 1)
                prod[dst, left] = p0 + sign * jnp.where(position >= 1, q0, 0.0)
                prod[dst, right] = p1 + sign * jnp.where(position >= 1, q1, q0)
            return carry

        lax.fori_loop(0, FREQS // rows, body, 0, unroll=16)
        whole = prod[...]
        high = whole.astype(bf16)
        low = (whole - high.astype(f32)).astype(bf16)
        copies[2 * step + 1].wait()
        part = dot(back[step, 0], high) + dot(back[step, 1], high) + dot(back[step, 0], low)
        acc[...] = part if step == 0 else acc[...] + part

    for h in range(2):
        for kk in range(2):
            blocks = [
                acc[kk * 256 + r * 64 : kk * 256 + (r + 1) * 64, h * 128 : (h + 1) * 128]
                for r in range(4)
            ]
            for y, block in enumerate(swap_groups(blocks)):
                out_ref[h * 4 + y, kk] = block.astype(bf16)


def gate_kernel(in_ref, own_ref, partner_ref, bias_ref, out_ref):
    core = lax.axis_index("k")
    for h in range(2):
        cols = slice(h * 128, (h + 1) * 128)
        bias = bias_ref[:, pl.ds(pl.multiple_of(core * 256 + h * 128, 128), 128)]
        for other, ref in enumerate((own_ref, partner_ref)):
            kk = (core + other) % 2
            blocks = swap_groups([in_ref[h * 4 + y, kk].astype(f32) for y in range(4)])
            for r, conv in enumerate(blocks):
                rows = slice(r * 64, (r + 1) * 64)
                q, k, v = [ref[i, rows, cols].astype(f32) for i in range(3)]
                out_ref[other, rows, cols] = (q * (conv + bias * (k * v))).astype(bf16)


PIECES = [(0, dy, p) for dy in (0, 3, 1, 2) for p in (0, 1)]
PIECES += [(1, dy, p) for dy in (0, 3, 1) for p in (0, 1)] + [(1, 2, 0), (1, 2, 1)]


def beside(blocks, p):
    return jnp.concatenate([block[p] for block in blocks], axis=1)


def first_kernel(*refs):
    gated, weights, outs = refs[:4], refs[4:13], refs[13:]
    mine_ref, other_ref, rest_mine, rest_other, rhs, sems = outs
    at = {a: lax.axis_index(a) for a in AXES}
    swapped = (at["k"] + at["l"]) % 2
    pairs = []
    for i, (dh, dy, p) in enumerate(PIECES):
        h, y = (at["h"] + dh) % 2, (at["y"] + dy) % 4
        rest = (y + at["l"] // 2) % 2
        x = (2 * h + y // 2 - at["x"] + 4) % 4
        rows = pl.ds(pl.multiple_of(rest * 1024 + x * 256, 256), 256)
        cols = pl.ds(pl.multiple_of(((swapped + p) % 2) * 512, 512), 512)
        piece = weights[7 + p] if i >= 14 else weights[i // 2].at[p]
        pairs.append((piece, rhs.at[rows, cols]))
    for copy in fetch(pairs, sems):
        copy.wait()
    for p in range(2):
        lhs = beside(gated, p)
        for col, ref in enumerate((mine_ref, other_ref)):
            cols = slice(col * 512, (col + 1) * 512)
            ref[p] = jnp.dot(lhs, rhs[:1024, cols], preferred_element_type=f32)
    rest_mine[...] = rhs[1024:, :512]
    rest_other[...] = rhs[1024:, 512:]


def rest_kernel(g0, g1, g2, g3, before, rhs, own_ref, other_ref):
    for p, ref in enumerate((own_ref, other_ref)):
        lhs = beside((g0, g1, g2, g3), p)
        ref[...] = before[p] + jnp.dot(lhs, rhs[...], preferred_element_type=f32)


VMEM = pl.BlockSpec(memory_space=pltpu.VMEM)
ANY = pl.BlockSpec(memory_space=pl.ANY)


def params(limit=48 * MIB, **kw):
    return pltpu.CompilerParams(vmem_limit_bytes=limit, **kw)


def cost(microseconds):
    rate = 1 << 30
    return pl.CostEstimate(flops=int(microseconds * rate), bytes_accessed=0, transcendentals=0)


def pack(query, key_in, value_in, taps):
    half = jax.ShapeDtypeStruct((3, 256, 256), bf16)
    return pl.pallas_call(
        pack_kernel,
        out_shape=[jax.ShapeDtypeStruct((2, 4, 2, 2, 64, 128), bf16), half, half],
        in_specs=[ANY] * 4,
        out_specs=[VMEM] * 3,
        scratch_shapes=[
            pltpu.VMEM((256, 512), bf16),
            pltpu.VMEM((256, 512), bf16),
            pltpu.VMEM((256, 512), bf16),
            pltpu.VMEM((256, 512), f32),
            pltpu.SemaphoreType.DMA((4,)),
        ],
        compiler_params=params(LARGE),
        cost_estimate=cost(2),
        name="pack",
    )(query, key_in, value_in, taps)


def convolve(received):
    fwd, back = transform_tables()
    return pl.pallas_call(
        conv_kernel,
        out_shape=jax.ShapeDtypeStruct((8, 2, 64, 128), bf16),
        in_specs=[VMEM, ANY, ANY],
        out_specs=VMEM,
        scratch_shapes=[
            pltpu.VMEM(fwd.shape, bf16),
            pltpu.VMEM(back.shape, bf16),
            pltpu.VMEM((512, 512), bf16),
            pltpu.VMEM((2 * FREQS, 512), f32),
            pltpu.VMEM((2 * FREQS, 256), f32),
            pltpu.VMEM((512, 256), f32),
            pltpu.SemaphoreType.DMA((2 * STEPS,)),
        ],
        compiler_params=params(LARGE),
        cost_estimate=cost(10),
        name="convolve",
    )(received, jnp.asarray(fwd), jnp.asarray(back))


def gate(conv, own, partner, bias):
    return pl.pallas_call(
        gate_kernel,
        out_shape=jax.ShapeDtypeStruct((2, 256, 256), bf16),
        in_specs=[VMEM] * 4,
        out_specs=VMEM,
        compiler_params=params(),
        cost_estimate=cost(1),
        name="gate",
    )(conv, own, partner, bias)


def project_first(gated, weights):
    part = jax.ShapeDtypeStruct((2, 256, 512), f32)
    rest = jax.ShapeDtypeStruct((1024, 512), bf16)
    return pl.pallas_call(
        first_kernel,
        out_shape=[part, part, rest, rest],
        in_specs=[VMEM] * 4 + [ANY] * 9,
        out_specs=[VMEM] * 4,
        scratch_shapes=[pltpu.VMEM((2048, 1024), bf16), pltpu.SemaphoreType.DMA((16,))],
        compiler_params=params(32 * MIB),
        cost_estimate=cost(5),
        name="project_first",
    )(*gated, *weights)


def project_rest(gated, before, rhs):
    half = jax.ShapeDtypeStruct((256, 512), f32)
    return pl.pallas_call(
        rest_kernel,
        out_shape=[half] * 2,
        in_specs=[VMEM] * 6,
        out_specs=[VMEM] * 2,
        compiler_params=params(32 * MIB),
        cost_estimate=cost(3),
        name="project_rest",
    )(*gated, before, rhs)


def shift(v, axis, by):
    n = lax.axis_size(axis)
    return lax.ppermute(v, axis, [(i, (i + by) % n) for i in range(n)])


def around(v, axis):
    return v, shift(v, axis, -1), shift(v, axis, 2), shift(v, axis, 1)


def body(query, key_in, value_in, filter_taps, conv_bias, out_weight):
    core = lax.axis_index("k")
    tie = lax.optimization_barrier
    bias = conv_bias.reshape(1, 512)
    packed, own, give = pack(query, key_in, value_in, filter_taps)
    received = lax.all_to_all(
        packed.reshape(16, 2, 64, 128), SEQ, split_axis=0, concat_axis=0, tiled=True
    )
    partner = shift(give, "k", 1)

    swaps = []
    for k in range(2):
        for l in range(4):
            to = (k, l) if k == l % 2 else (1 - k, l ^ 1)
            swaps.append((k * 4 + l, to[0] * 4 + to[1]))
    out_weight = lax.ppermute(out_weight, ("k", "l"), swaps)
    keep = lax.dynamic_slice(out_weight, (core * 256, 0), (256, 512))
    give = lax.dynamic_slice(out_weight, ((1 - core) * 256, 0), (256, 512))
    weight = jnp.stack([keep, shift(give, "k", 1)])
    down, two, up = around(weight, "y")[1:]
    across = shift(weight, "h", 1)
    received, partner, weight = tie((received, partner, weight))

    conv, up, down, two, across = tie((convolve(received), up, down, two, across))
    weights = (weight, up, down, two, across)
    conv = lax.all_to_all(conv, ("h", "y"), split_axis=0, concat_axis=0, tiled=True)
    up, down = shift(across, "y", 1), shift(across, "y", -1)
    mine = gate(conv, own, partner, bias)
    other = lax.ppermute(mine, "l", [(i, i ^ 2) for i in range(4)])
    mine, other, up, down = tie((around(mine, "x"), other, up, down))

    other = around(other, "x")
    weights += (up, down, shift(up[0], "y", 1), shift(down[1], "y", -1))
    half_mine, half_other, rest_mine, rest_other = project_first(mine, weights)
    other, half_mine, rest_mine = tie((other, half_mine, rest_mine))
    own, partner = project_rest(other, half_other, rest_other)
    send = (own + shift(partner, "k", 1)).astype(bf16)
    send, other, half_mine = tie((send, other, half_mine))
    from_pair = lax.ppermute(send, "l", [(i, i ^ 1) for i in range(4)])
    own, partner = project_rest(other, half_mine, rest_mine)
    return (own + shift(partner, "k", 1) + from_pair.astype(f32)).astype(bf16)


def solution(mesh):
    fine = Mesh(mesh.devices.reshape(2, 4, 2, 4, 4), AXES)
    block = P(SEQ, CHAN)
    return jax.shard_map(
        body,
        mesh=fine,
        in_specs=(block, block, block, block, P(CHAN), block),
        out_specs=block,
        check_vma=False,
    )
```

time: 167 us -> 123 us (0.74)
  waiting for transfers between devices: 73 us -> 48.8 us
  starting transfers between devices: 61.6 us -> 54.4 us
  Pallas kernels: 22.7 us -> 15.8 us
  local copies, waits for them, and re-layouts: 6.94 us -> 2.86 us
    ppermute x26 -> x18, starting transfers between devices: 41.4 us -> 28.4 us  [shift(): return lax.ppermute(v, axis, [(i, (i + by) % n) for i in range(n)])]
    ppermute x3 -> x2, waiting for transfers between devices: 26.1 us -> 15.2 us  [the longest x1 7.76 us: body(): from_pair = lax.ppermute(send, 'l', [(i, i ^ 1) for i in range(4)])]
    ppermute x26 -> x18, waiting for transfers between devices: 32 us -> 22.5 us  [shift(): return lax.ppermute(v, axis, [(i, (i + by) % n) for i in range(n)])]
    ppermute x1, waiting for transfers between devices: 7.05 us -> 0.01 us  [body(): out_weight = lax.ppermute(out_weight, ('k', 'l'), swaps)]
    pallas_call x6, Pallas kernels: 22.7 us -> 15.8 us  [the longest x1 9.23 us: convolve(): pl.pallas_call(conv_kernel, out_shape=jax.ShapeDtypeStruct((8, 2, 64, 128...]
    all_to_all x1 -> x2, starting transfers between devices: 11.1 us -> 14.4 us  [the longest x1 10.3 us: body(): lax.all_to_all(packed.reshape(16, 2, 64, 128), SEQ, split_axis=0, concat_...]
    all_to_all x1 -> x2, waiting for transfers between devices: 7.98 us -> 11 us  [the longest x1 7.42 us: body(): lax.all_to_all(conv, ('h', 'y'), split_axis=0, concat_axis=0, tiled=True)]
    ppermute x3 -> x2, starting transfers between devices: 4.02 us -> 6.72 us  [the longest x1 6.72 us: body(): other = lax.ppermute(mine, 'l', [(i, i ^ 2) for i in range(4)])]
  transfers between devices with their start and end apart: 31 -> 23, of which waited for: 15 -> 13; matrix products, arithmetic and copies ran while one was open for 1% -> 0% of each run, Pallas kernels for 4% -> 12%
where the time goes in v3:
time: 123 us
  starting transfers between devices  54.4 us (44%)
  waiting for transfers between devices  48.8 us (40%)
  Pallas kernels  15.8 us (13%)
  local copies, waits for them, and re-layouts  2.86 us (2%)
    ppermute x18, starting transfers between devices, shift(): return lax.ppermute(v, axis, [(i, (i + by) % n) for i in range(n)])  28.4 us
    ppermute x18, waiting for transfers between devices, shift(): return lax.ppermute(v, axis, [(i, (i + by) % n) for i in range(n)])  22.5 us
    all_to_all x1, starting transfers between devices, body(): lax.all_to_all(packed.reshape(16, 2, 64, 128), SEQ, split_axis=0, concat_...  10.3 us
    pallas_call x1, Pallas kernels, convolve(): pl.pallas_call(conv_kernel, out_shape=jax.ShapeDtypeStruct((8, 2, 64, 128...  9.23 us
    ppermute x1, waiting for transfers between devices, body(): from_pair = lax.ppermute(send, 'l', [(i, i ^ 1) for i in range(4)])  7.76 us
    ppermute x1, waiting for transfers between devices, body(): other = lax.ppermute(mine, 'l', [(i, i ^ 2) for i in range(4)])  7.45 us
    all_to_all x1, waiting for transfers between devices, body(): lax.all_to_all(conv, ('h', 'y'), split_axis=0, concat_axis=0, tiled=True)  7.42 us
    ppermute x1, starting transfers between devices, body(): other = lax.ppermute(mine, 'l', [(i, i ^ 2) for i in range(4)])  6.72 us
  transfers between devices with their start and end apart: 23, of which 13 were waited for; matrix products, arithmetic and copies ran while one was open for 0% of the time, Pallas kernels for 12%

profile of v3, /device:TPU:1, one launch (start us, length us, event | category | flops | bytes accessed | tf_op | source)
XLA Modules:
  0.0 123.0 jit_solution(2574768965777841908)
XLA Ops:
  0.0 4.9 %collective-permute-start.1 = (bf16[512,512]{1,0:T(8,128)(2,1)}, bf16[512,512]{1,0:T(8,128)(2,1)S(1)}, u32[]{:S(2)}, u32[]{:S(2)}) collective-permute-start(bf16[512,512]{1,0:T(8,128)(2,1)} %param.13), channel_id=1, source_target_pairs={{0,0},{1,16},{2,2},{3,18},{16,1},{17,17},{18,3},{19,19},{4,4},{5,2... | collective-permute-start | bytes 1572872 | tf_op jit(solution)/shard_map/ppermute | solution.py:361
  4.9 2.9 %pack.1 = (bf16[2,4,2,2,64,128]{5,4,3,2,1,0:T(8,128)(2,1)}, bf16[3,256,256]{2,1,0:T(8,128)(2,1)}, bf16[3,256,256]{2,1,0:T(8,128)(2,1)}) custom-call(bf16[256,512]{1,0:T(8,128)(2,1)} %query_hbm.1, bf16[256,512]{1,0:T(8,128)(2,1)} %key_hbm.1, bf16[256,512]{1,0:T(8,128)(2,1)} %value_hbm.1, f32[256,512]{1,0:T(8,128)} %taps_hbm.1), custom_call_target="tpu_custom_call" | custom-call | flops 2147483648 | tf_op jit(solution)/shard_map/pack/pallas_call | solution.py:257
  7.9 10.3 %all-to-all-start = ((bf16[16,2,64,128]{3,2,1,0:T(8,128)(2,1)}), bf16[16,2,64,128]{3,2,1,0:T(8,128)(2,1)}, u32[]{:S(2)}, u32[]{:S(2)}) async-start(bf16[16,2,64,128]{3,2,1,0:T(8,128)(2,1)} %bitcast.10), calls=%async_computation | async-start | bytes 1048576 | tf_op jit(solution)/shard_map/all_to_all | solution.py:351
  18.9 1.5 %collective-permute-done.2 = bf16[256,512]{1,0:T(8,128)(2,1)S(1)} collective-permute-done((bf16[256,512]{1,0:T(8,128)(2,1)S(1)}, bf16[256,512]{1,0:T(8,128)(2,1)S(1)}, u32[]{:S(2)}, u32[]{:S(2)}) %collective-permute-start.2) | collective-permute-done | bytes 262176 | tf_op jit(solution)/shard_map/ppermute | solution.py:339
  20.4 5.4 %collective-permute-start.6 = (bf16[2,256,512]{2,1,0:T(8,128)(2,1)S(1)}, bf16[2,256,512]{2,1,0:T(8,128)(2,1)S(1)}, u32[]{:S(2)}, u32[]{:S(2)}) collective-permute-start(bf16[2,256,512]{2,1,0:T(8,128)(2,1)S(1)} %pad_maximum_fusion.refs_4_), channel_id=1, source_target_pairs={{0,128},{128,0},{1,129},{129,1},{2,130},{130,2},{3,131},{131,3},{4... | collective-permute-start | bytes 1572872 | tf_op jit(solution)/shard_map/ppermute | solution.py:339
  25.8 2.7 %collective-permute-start.5 = (bf16[2,256,512]{2,1,0:T(8,128)(2,1)S(1)}, bf16[2,256,512]{2,1,0:T(8,128)(2,1)S(1)}, u32[]{:S(2)}, u32[]{:S(2)}) collective-permute-start(bf16[2,256,512]{2,1,0:T(8,128)(2,1)S(1)} %pad_maximum_fusion.refs_4_), channel_id=1, source_target_pairs={{0,64},{32,96},{64,0},{96,32},{1,65},{33,97},{65,1},{97,33},{2,66}... | collective-permute-start | bytes 1572872 | tf_op jit(solution)/shard_map/ppermute | solution.py:339
  28.5 0.9 collective-permute-start.4
  29.9 3.6 %all-to-all-done.in_ref = bf16[16,2,64,128]{3,2,1,0:T(8,128)(2,1)} async-done(((bf16[16,2,64,128]{3,2,1,0:T(8,128)(2,1)}), bf16[16,2,64,128]{3,2,1,0:T(8,128)(2,1)}, u32[]{:S(2)}, u32[]{:S(2)}) %all-to-all-start) | async-done | bytes 524320 | tf_op jit(solution)/shard_map/all_to_all | solution.py:351
  33.5 9.2 %convolve.1 = bf16[8,2,64,128]{3,2,1,0:T(8,128)(2,1)} custom-call(bf16[16,2,64,128]{3,2,1,0:T(8,128)(2,1)} %all-to-all-done.in_ref, bf16[4,2,256,512]{3,2,1,0:T(8,128)(2,1)} %constant.18.clone.fwd_hbm, bf16[4,2,512,256]{3,2,1,0:T(8,128)(2,1)} %constant.19.clone.back_hbm), custom_call_target="tpu_custom_call" | custom-call | flops 10737418240 | tf_op jit(solution)/shard_map/convolve/pallas_call | solution.py:277
  42.8 6.8 %collective-permute-done.6.refs_8_ = bf16[2,256,512]{2,1,0:T(8,128)(2,1)S(1)} collective-permute-done((bf16[2,256,512]{2,1,0:T(8,128)(2,1)S(1)}, bf16[2,256,512]{2,1,0:T(8,128)(2,1)S(1)}, u32[]{:S(2)}, u32[]{:S(2)}) %collective-permute-start.6) | collective-permute-done | bytes 524320 | tf_op jit(solution)/shard_map/ppermute | solution.py:339
  49.6 3.2 %collective-permute-done.4.refs_6_ = bf16[2,256,512]{2,1,0:T(8,128)(2,1)S(1)} collective-permute-done((bf16[2,256,512]{2,1,0:T(8,128)(2,1)S(1)}, bf16[2,256,512]{2,1,0:T(8,128)(2,1)S(1)}, u32[]{:S(2)}, u32[]{:S(2)}) %collective-permute-start.4) | collective-permute-done | bytes 524320 | tf_op jit(solution)/shard_map/ppermute | solution.py:339
  52.8 1.3 %collective-permute-done.3.refs_5_ = bf16[2,256,512]{2,1,0:T(8,128)(2,1)S(1)} collective-permute-done((bf16[2,256,512]{2,1,0:T(8,128)(2,1)S(1)}, bf16[2,256,512]{2,1,0:T(8,128)(2,1)S(1)}, u32[]{:S(2)}, u32[]{:S(2)}) %collective-permute-start.3) | collective-permute-done | bytes 524320 | tf_op jit(solution)/shard_map/ppermute | solution.py:339
  54.8 4.1 %all-to-all-start.1 = ((bf16[8,2,64,128]{3,2,1,0:T(8,128)(2,1)}), bf16[8,2,64,128]{3,2,1,0:T(8,128)(2,1)S(1)}, u32[]{:S(2)}, u32[]{:S(2)}) async-start(bf16[8,2,64,128]{3,2,1,0:T(8,128)(2,1)} %convolve.1), calls=%async_computation.1 | async-start | bytes 524288 | tf_op jit(solution)/shard_map/all_to_all | solution.py:371
  58.9 2.7 %collective-permute-start.12 = (bf16[2,256,512]{2,1,0:T(8,128)(2,1)S(1)}, bf16[2,256,512]{2,1,0:T(8,128)(2,1)S(1)}, u32[]{:S(2)}, u32[]{:S(2)}) collective-permute-start(bf16[2,256,512]{2,1,0:T(8,128)(2,1)S(1)} %collective-permute-done.6.refs_8_), channel_id=1, source_target_pairs={{0,96},{32,0},{64,32},{96,64},{1,97},{33,1},{65,33},{97,65},{2,98}... | collective-permute-start | bytes 1572872 | tf_op jit(solution)/shard_map/ppermute | solution.py:339
  61.6 7.4 %all-to-all-done.1.in_ref = bf16[8,2,64,128]{3,2,1,0:T(8,128)(2,1)S(1)} async-done(((bf16[8,2,64,128]{3,2,1,0:T(8,128)(2,1)}), bf16[8,2,64,128]{3,2,1,0:T(8,128)(2,1)S(1)}, u32[]{:S(2)}, u32[]{:S(2)}) %all-to-all-start.1) | async-done | bytes 262176 | tf_op jit(solution)/shard_map/all_to_all | solution.py:371
  69.0 1.0 copy-done.3
  70.0 1.0 copy-done.5
  71.4 6.7 %collective-permute-start.10 = (bf16[2,256,256]{2,1,0:T(8,128)(2,1)S(1)}, bf16[2,256,256]{2,1,0:T(8,128)(2,1)S(1)}, u32[]{:S(2)}, u32[]{:S(2)}) collective-permute-start(bf16[2,256,256]{2,1,0:T(8,128)(2,1)S(1)} %gate.1.refs_0_), channel_id=1, source_target_pairs={{0,2},{1,3},{2,0},{3,1},{4,6},{5,7},{6,4},{7,5},{8,10},{9,11},{10,... | collective-permute-start | bytes 786440 | tf_op jit(solution)/shard_map/ppermute | solution.py:374
  78.1 1.2 collective-permute-start.9
  79.3 2.5 %collective-permute-start.8 = (bf16[2,256,256]{2,1,0:T(8,128)(2,1)S(1)}, bf16[2,256,256]{2,1,0:T(8,128)(2,1)S(1)}, u32[]{:S(2)}, u32[]{:S(2)}) collective-permute-start(bf16[2,256,256]{2,1,0:T(8,128)(2,1)S(1)} %gate.1.refs_0_), channel_id=1, source_target_pairs={{0,8},{4,12},{8,0},{12,4},{1,9},{5,13},{9,1},{13,5},{2,10},{6,14},... | collective-permute-start | bytes 786440 | tf_op jit(solution)/shard_map/ppermute | solution.py:339
  81.8 1.2 collective-permute-start.7
  82.9 7.5 %collective-permute-done.10.g0 = bf16[2,256,256]{2,1,0:T(8,128)(2,1)S(1)} collective-permute-done((bf16[2,256,256]{2,1,0:T(8,128)(2,1)S(1)}, bf16[2,256,256]{2,1,0:T(8,128)(2,1)S(1)}, u32[]{:S(2)}, u32[]{:S(2)}) %collective-permute-start.10) | collective-permute-done | bytes 262176 | tf_op jit(solution)/shard_map/ppermute | solution.py:374
  91.2 2.1 %collective-permute-start.17 = (bf16[256,512]{1,0:T(8,128)(2,1)S(1)}, bf16[256,512]{1,0:T(8,128)(2,1)S(1)}, u32[]{:S(2)}, u32[]{:S(2)}) collective-permute-start(bf16[256,512]{1,0:T(8,128)(2,1)S(1)} %slice_bitcast_fusion), channel_id=1, source_target_pairs={{0,96},{32,0},{64,32},{96,64},{1,97},{33,1},{65,33},{97,65},{2,98}... | collective-permute-start | bytes 786440 | tf_op jit(solution)/shard_map/ppermute | solution.py:339
  93.3 2.8 %collective-permute-start.15 = (bf16[2,256,256]{2,1,0:T(8,128)(2,1)S(1)}, bf16[2,256,256]{2,1,0:T(8,128)(2,1)S(1)}, u32[]{:S(2)}, u32[]{:S(2)}) collective-permute-start(bf16[2,256,256]{2,1,0:T(8,128)(2,1)S(1)} %collective-permute-done.10.g0), channel_id=1, source_target_pairs={{0,4},{4,8},{8,12},{12,0},{1,5},{5,9},{9,13},{13,1},{2,6},{6,10},{... | collective-permute-start | bytes 786440 | tf_op jit(solution)/shard_map/ppermute | solution.py:339
  96.0 1.8 %collective-permute-start.14 = (bf16[2,256,256]{2,1,0:T(8,128)(2,1)S(1)}, bf16[2,256,256]{2,1,0:T(8,128)(2,1)S(1)}, u32[]{:S(2)}, u32[]{:S(2)}) collective-permute-start(bf16[2,256,256]{2,1,0:T(8,128)(2,1)S(1)} %collective-permute-done.10.g0), channel_id=1, source_target_pairs={{0,8},{4,12},{8,0},{12,4},{1,9},{5,13},{9,1},{13,5},{2,10},{6,14},... | collective-permute-start | bytes 786440 | tf_op jit(solution)/shard_map/ppermute | solution.py:339
  98.4 1.3 %collective-permute-done.16.refs_11_ = bf16[256,512]{1,0:T(8,128)(2,1)S(1)} collective-permute-done((bf16[256,512]{1,0:T(8,128)(2,1)S(1)}, bf16[256,512]{1,0:T(8,128)(2,1)S(1)}, u32[]{:S(2)}, u32[]{:S(2)}) %collective-permute-start.16) | collective-permute-done | bytes 262176 | tf_op jit(solution)/shard_map/ppermute | solution.py:339
  99.7 1.9 %project_first.1 = (f32[2,256,512]{2,1,0:T(8,128)S(1)}, f32[2,256,512]{2,1,0:T(8,128)S(1)}, bf16[1024,512]{1,0:T(8,128)(2,1)S(1)}, bf16[1024,512]{1,0:T(8,128)(2,1)S(1)}) custom-call(bf16[2,256,256]{2,1,0:T(8,128)(2,1)S(1)} %gate.1.refs_0_, bf16[2,256,256]{2,1,0:T(8,128)(2,1)S(1)} %collective-permute-done.7.refs_1_, ...), custom_call_target="tpu_custom_call" | custom-call | flops 5368709120 | tf_op jit(solution)/shard_map/project_first/pallas_call | solution.py:312
  101.6 6.2 %collective-permute-done.14.g2 = bf16[2,256,256]{2,1,0:T(8,128)(2,1)S(1)} collective-permute-done((bf16[2,256,256]{2,1,0:T(8,128)(2,1)S(1)}, bf16[2,256,256]{2,1,0:T(8,128)(2,1)S(1)}, u32[]{:S(2)}, u32[]{:S(2)}) %collective-permute-start.14) | collective-permute-done | bytes 262176 | tf_op jit(solution)/shard_map/ppermute | solution.py:339
  108.5 3.1 %collective-permute-start.18 = (f32[256,512]{1,0:T(8,128)S(1)}, f32[256,512]{1,0:T(8,128)S(1)}, u32[]{:S(2)}, u32[]{:S(2)}) collective-permute-start(f32[256,512]{1,0:T(8,128)S(1)} %get-tuple-element.70), channel_id=1, source_target_pairs={{0,16},{16,0},{1,17},{17,1},{2,18},{18,2},{3,19},{19,3},{4,20},{20... | collective-permute-start | bytes 1572872 | tf_op jit(solution)/shard_map/ppermute | solution.py:339
  111.6 1.5 %collective-permute-done.18 = f32[256,512]{1,0:T(8,128)S(1)} collective-permute-done((f32[256,512]{1,0:T(8,128)S(1)}, f32[256,512]{1,0:T(8,128)S(1)}, u32[]{:S(2)}, u32[]{:S(2)}) %collective-permute-start.18) | collective-permute-done | bytes 524320 | tf_op jit(solution)/shard_map/ppermute | solution.py:339
  114.4 7.8 %collective-permute-done.20 = bf16[256,512]{1,0:T(8,128)(2,1)S(1)} collective-permute-done((bf16[256,512]{1,0:T(8,128)(2,1)S(1)}, bf16[256,512]{1,0:T(8,128)(2,1)S(1)}, u32[]{:S(2)}, u32[]{:S(2)}) %collective-permute-start.20) | collective-permute-done | bytes 262176 | tf_op jit(solution)/shard_map/ppermute | solution.py:384
  122.1 0.8 add_convert_fusion
  (38 shorter events, 5.8 us)
Async XLA Ops:
  0.0 18.5 %collective-permute-start.1 = (bf16[512,512]{1,0:T(8,128)(2,1)}, bf16[512,512]{1,0:T(8,128)(2,1)S(1)}, u32[]{:S(2)}, u32[]{:S(2)}) collective-permute-start(bf16[512,512]{1,0:T(8,128)(2,1)} %param.13), channel_id=1, source_target_pairs={{0,0},{1,16},{2,2},{3,18},{16,1},{17,17},{18,3},{19,19},{4,4},{5,2... | collective-permute-start | bytes 1572872 | tf_op jit(solution)/shard_map/ppermute | solution.py:361
  7.9 25.6 %all-to-all-start = ((bf16[16,2,64,128]{3,2,1,0:T(8,128)(2,1)}), bf16[16,2,64,128]{3,2,1,0:T(8,128)(2,1)}, u32[]{:S(2)}, u32[]{:S(2)}) async-start(bf16[16,2,64,128]{3,2,1,0:T(8,128)(2,1)} %bitcast.10), calls=%async_computation | async-start | bytes 1048576 | tf_op jit(solution)/shard_map/all_to_all | solution.py:351
  18.2 11.7 %collective-permute-start = (bf16[3,256,256]{2,1,0:T(8,128)(2,1)}, bf16[3,256,256]{2,1,0:T(8,128)(2,1)S(1)}, u32[]{:S(2)}, u32[]{:S(2)}) collective-permute-start(bf16[3,256,256]{2,1,0:T(8,128)(2,1)} %get-tuple-element.44), channel_id=1, source_target_pairs={{0,16},{16,0},{1,17},{17,1},{2,18},{18,2},{3,19},{19,3},{4,20},{20... | collective-permute-start | bytes 1179656 | tf_op jit(solution)/shard_map/ppermute | solution.py:339
  18.5 1.8 %collective-permute-start.2 = (bf16[256,512]{1,0:T(8,128)(2,1)S(1)}, bf16[256,512]{1,0:T(8,128)(2,1)S(1)}, u32[]{:S(2)}, u32[]{:S(2)}) collective-permute-start(bf16[256,512]{1,0:T(8,128)(2,1)S(1)} %get-tuple-element.82), channel_id=1, source_target_pairs={{0,16},{16,0},{1,17},{17,1},{2,18},{18,2},{3,19},{19,3},{4,20},{20... | collective-permute-start | bytes 786440 | tf_op jit(solution)/shard_map/ppermute | solution.py:339
  20.4 48.6 %copy-start.4 = (f32[512]{0:T(512)S(1)}, f32[512]{0:T(512)}, u32[]{:S(2)}) copy-start(f32[512]{0:T(512)} %param.12) | copy-start | bytes 6148
  20.4 29.2 %collective-permute-start.6 = (bf16[2,256,512]{2,1,0:T(8,128)(2,1)S(1)}, bf16[2,256,512]{2,1,0:T(8,128)(2,1)S(1)}, u32[]{:S(2)}, u32[]{:S(2)}) collective-permute-start(bf16[2,256,512]{2,1,0:T(8,128)(2,1)S(1)} %pad_maximum_fusion.refs_4_), channel_id=1, source_target_pairs={{0,128},{128,0},{1,129},{129,1},{2,130},{130,2},{3,131},{131,3},{4... | collective-permute-start | bytes 1572872 | tf_op jit(solution)/shard_map/ppermute | solution.py:339
  25.8 23.8 %collective-permute-start.5 = (bf16[2,256,512]{2,1,0:T(8,128)(2,1)S(1)}, bf16[2,256,512]{2,1,0:T(8,128)(2,1)S(1)}, u32[]{:S(2)}, u32[]{:S(2)}) collective-permute-start(bf16[2,256,512]{2,1,0:T(8,128)(2,1)S(1)} %pad_maximum_fusion.refs_4_), channel_id=1, source_target_pairs={{0,64},{32,96},{64,0},{96,32},{1,65},{33,97},{65,1},{97,33},{2,66}... | collective-permute-start | bytes 1572872 | tf_op jit(solution)/shard_map/ppermute | solution.py:339
  28.5 24.3 %collective-permute-start.4 = (bf16[2,256,512]{2,1,0:T(8,128)(2,1)S(1)}, bf16[2,256,512]{2,1,0:T(8,128)(2,1)S(1)}, u32[]{:S(2)}, u32[]{:S(2)}) collective-permute-start(bf16[2,256,512]{2,1,0:T(8,128)(2,1)S(1)} %pad_maximum_fusion.refs_4_), channel_id=1, source_target_pairs={{0,96},{32,0},{64,32},{96,64},{1,97},{33,1},{65,33},{97,65},{2,98}... | collective-permute-start | bytes 1572872 | tf_op jit(solution)/shard_map/ppermute | solution.py:339
  29.3 24.7 %collective-permute-start.3 = (bf16[2,256,512]{2,1,0:T(8,128)(2,1)S(1)}, bf16[2,256,512]{2,1,0:T(8,128)(2,1)S(1)}, u32[]{:S(2)}, u32[]{:S(2)}) collective-permute-start(bf16[2,256,512]{2,1,0:T(8,128)(2,1)S(1)} %pad_maximum_fusion.refs_4_), channel_id=1, source_target_pairs={{0,32},{32,64},{64,96},{96,0},{1,33},{33,65},{65,97},{97,1},{2,34}... | collective-permute-start | bytes 1572872 | tf_op jit(solution)/shard_map/ppermute | solution.py:339
  29.9 12.8 %copy-start.2 = (bf16[3,256,256]{2,1,0:T(8,128)(2,1)}, bf16[3,256,256]{2,1,0:T(8,128)(2,1)S(1)}, u32[]{:S(2)}) copy-start(bf16[3,256,256]{2,1,0:T(8,128)(2,1)S(1)} %collective-permute-done.partner_ref) | copy-start | bytes 1179652
  54.1 0.8 copy-start
  54.8 14.2 %all-to-all-start.1 = ((bf16[8,2,64,128]{3,2,1,0:T(8,128)(2,1)}), bf16[8,2,64,128]{3,2,1,0:T(8,128)(2,1)S(1)}, u32[]{:S(2)}, u32[]{:S(2)}) async-start(bf16[8,2,64,128]{3,2,1,0:T(8,128)(2,1)} %convolve.1), calls=%async_computation.1 | async-start | bytes 524288 | tf_op jit(solution)/shard_map/all_to_all | solution.py:371
  58.9 22.8 %collective-permute-start.12 = (bf16[2,256,512]{2,1,0:T(8,128)(2,1)S(1)}, bf16[2,256,512]{2,1,0:T(8,128)(2,1)S(1)}, u32[]{:S(2)}, u32[]{:S(2)}) collective-permute-start(bf16[2,256,512]{2,1,0:T(8,128)(2,1)S(1)} %collective-permute-done.6.refs_8_), channel_id=1, source_target_pairs={{0,96},{32,0},{64,32},{96,64},{1,97},{33,1},{65,33},{97,65},{2,98}... | collective-permute-start | bytes 1572872 | tf_op jit(solution)/shard_map/ppermute | solution.py:339
  61.6 21.3 %collective-permute-start.11 = (bf16[2,256,512]{2,1,0:T(8,128)(2,1)S(1)}, bf16[2,256,512]{2,1,0:T(8,128)(2,1)S(1)}, u32[]{:S(2)}, u32[]{:S(2)}) collective-permute-start(bf16[2,256,512]{2,1,0:T(8,128)(2,1)S(1)} %collective-permute-done.6.refs_8_), channel_id=1, source_target_pairs={{0,32},{32,64},{64,96},{96,0},{1,33},{33,65},{65,97},{97,1},{2,34}... | collective-permute-start | bytes 1572872 | tf_op jit(solution)/shard_map/ppermute | solution.py:339
  69.0 1.0 copy-start.3
  70.0 1.0 copy-start.5
  71.0 28.7 %copy-start.1 = (bf16[2,256,512]{2,1,0:T(8,128)(2,1)S(1)}, bf16[2,256,512]{2,1,0:T(8,128)(2,1)}, u32[]{:S(2)}) copy-start(bf16[2,256,512]{2,1,0:T(8,128)(2,1)} %copy-done) | copy-start | bytes 1572868
  71.4 19.0 %collective-permute-start.10 = (bf16[2,256,256]{2,1,0:T(8,128)(2,1)S(1)}, bf16[2,256,256]{2,1,0:T(8,128)(2,1)S(1)}, u32[]{:S(2)}, u32[]{:S(2)}) collective-permute-start(bf16[2,256,256]{2,1,0:T(8,128)(2,1)S(1)} %gate.1.refs_0_), channel_id=1, source_target_pairs={{0,2},{1,3},{2,0},{3,1},{4,6},{5,7},{6,4},{7,5},{8,10},{9,11},{10,... | collective-permute-start | bytes 786440 | tf_op jit(solution)/shard_map/ppermute | solution.py:374
  78.1 12.3 %collective-permute-start.9 = (bf16[2,256,256]{2,1,0:T(8,128)(2,1)S(1)}, bf16[2,256,256]{2,1,0:T(8,128)(2,1)S(1)}, u32[]{:S(2)}, u32[]{:S(2)}) collective-permute-start(bf16[2,256,256]{2,1,0:T(8,128)(2,1)S(1)} %gate.1.refs_0_), channel_id=1, source_target_pairs={{0,4},{4,8},{8,12},{12,0},{1,5},{5,9},{9,13},{13,1},{2,6},{6,10},{... | collective-permute-start | bytes 786440 | tf_op jit(solution)/shard_map/ppermute | solution.py:339
  79.3 11.7 %collective-permute-start.8 = (bf16[2,256,256]{2,1,0:T(8,128)(2,1)S(1)}, bf16[2,256,256]{2,1,0:T(8,128)(2,1)S(1)}, u32[]{:S(2)}, u32[]{:S(2)}) collective-permute-start(bf16[2,256,256]{2,1,0:T(8,128)(2,1)S(1)} %gate.1.refs_0_), channel_id=1, source_target_pairs={{0,8},{4,12},{8,0},{12,4},{1,9},{5,13},{9,1},{13,5},{2,10},{6,14},... | collective-permute-start | bytes 786440 | tf_op jit(solution)/shard_map/ppermute | solution.py:339
  81.8 9.4 %collective-permute-start.7 = (bf16[2,256,256]{2,1,0:T(8,128)(2,1)S(1)}, bf16[2,256,256]{2,1,0:T(8,128)(2,1)S(1)}, u32[]{:S(2)}, u32[]{:S(2)}) collective-permute-start(bf16[2,256,256]{2,1,0:T(8,128)(2,1)S(1)} %gate.1.refs_0_), channel_id=1, source_target_pairs={{0,12},{4,0},{8,4},{12,8},{1,13},{5,1},{9,5},{13,9},{2,14},{6,2},{... | collective-permute-start | bytes 786440 | tf_op jit(solution)/shard_map/ppermute | solution.py:339
  91.2 7.2 %collective-permute-start.17 = (bf16[256,512]{1,0:T(8,128)(2,1)S(1)}, bf16[256,512]{1,0:T(8,128)(2,1)S(1)}, u32[]{:S(2)}, u32[]{:S(2)}) collective-permute-start(bf16[256,512]{1,0:T(8,128)(2,1)S(1)} %slice_bitcast_fusion), channel_id=1, source_target_pairs={{0,96},{32,0},{64,32},{96,64},{1,97},{33,1},{65,33},{97,65},{2,98}... | collective-permute-start | bytes 786440 | tf_op jit(solution)/shard_map/ppermute | solution.py:339
  93.3 6.4 %collective-permute-start.16 = (bf16[256,512]{1,0:T(8,128)(2,1)S(1)}, bf16[256,512]{1,0:T(8,128)(2,1)S(1)}, u32[]{:S(2)}, u32[]{:S(2)}) collective-permute-start(bf16[256,512]{1,0:T(8,128)(2,1)S(1)} %slice_bitcast_fusion.1), channel_id=1, source_target_pairs={{0,32},{32,64},{64,96},{96,0},{1,33},{33,65},{65,97},{97,1},{2,34}... | collective-permute-start | bytes 786440 | tf_op jit(solution)/shard_map/ppermute | solution.py:339
  93.3 8.3 %collective-permute-start.15 = (bf16[2,256,256]{2,1,0:T(8,128)(2,1)S(1)}, bf16[2,256,256]{2,1,0:T(8,128)(2,1)S(1)}, u32[]{:S(2)}, u32[]{:S(2)}) collective-permute-start(bf16[2,256,256]{2,1,0:T(8,128)(2,1)S(1)} %collective-permute-done.10.g0), channel_id=1, source_target_pairs={{0,4},{4,8},{8,12},{12,0},{1,5},{5,9},{9,13},{13,1},{2,6},{6,10},{... | collective-permute-start | bytes 786440 | tf_op jit(solution)/shard_map/ppermute | solution.py:339
  96.0 11.7 %collective-permute-start.14 = (bf16[2,256,256]{2,1,0:T(8,128)(2,1)S(1)}, bf16[2,256,256]{2,1,0:T(8,128)(2,1)S(1)}, u32[]{:S(2)}, u32[]{:S(2)}) collective-permute-start(bf16[2,256,256]{2,1,0:T(8,128)(2,1)S(1)} %collective-permute-done.10.g0), channel_id=1, source_target_pairs={{0,8},{4,12},{8,0},{12,4},{1,9},{5,13},{9,1},{13,5},{2,10},{6,14},... | collective-permute-start | bytes 786440 | tf_op jit(solution)/shard_map/ppermute | solution.py:339
  97.9 9.9 %collective-permute-start.13 = (bf16[2,256,256]{2,1,0:T(8,128)(2,1)S(1)}, bf16[2,256,256]{2,1,0:T(8,128)(2,1)S(1)}, u32[]{:S(2)}, u32[]{:S(2)}) collective-permute-start(bf16[2,256,256]{2,1,0:T(8,128)(2,1)S(1)} %collective-permute-done.10.g0), channel_id=1, source_target_pairs={{0,12},{4,0},{8,4},{12,8},{1,13},{5,1},{9,5},{13,9},{2,14},{6,2},{... | collective-permute-start | bytes 786440 | tf_op jit(solution)/shard_map/ppermute | solution.py:339
  108.5 4.6 %collective-permute-start.18 = (f32[256,512]{1,0:T(8,128)S(1)}, f32[256,512]{1,0:T(8,128)S(1)}, u32[]{:S(2)}, u32[]{:S(2)}) collective-permute-start(f32[256,512]{1,0:T(8,128)S(1)} %get-tuple-element.70), channel_id=1, source_target_pairs={{0,16},{16,0},{1,17},{17,1},{2,18},{18,2},{3,19},{19,3},{4,20},{20... | collective-permute-start | bytes 1572872 | tf_op jit(solution)/shard_map/ppermute | solution.py:339
  113.9 8.2 %collective-permute-start.19 = (f32[256,512]{1,0:T(8,128)S(1)}, f32[256,512]{1,0:T(8,128)S(1)}, u32[]{:S(2)}, u32[]{:S(2)}) collective-permute-start(f32[256,512]{1,0:T(8,128)S(1)} %get-tuple-element.79), channel_id=1, source_target_pairs={{0,16},{16,0},{1,17},{17,1},{2,18},{18,2},{3,19},{19,3},{4,20},{20... | collective-permute-start | bytes 1572872 | tf_op jit(solution)/shard_map/ppermute | solution.py:339
  114.4 7.8 %collective-permute-start.20 = (bf16[256,512]{1,0:T(8,128)(2,1)S(1)}, bf16[256,512]{1,0:T(8,128)(2,1)S(1)}, u32[]{:S(2)}, u32[]{:S(2)}) collective-permute-start(bf16[256,512]{1,0:T(8,128)(2,1)S(1)} %add_convert_fusion.1), channel_id=1, source_target_pairs={{0,1},{1,0},{2,3},{3,2},{4,5},{5,4},{6,7},{7,6},{8,9},{9,8},{10,11... | collective-permute-start | bytes 786440 | tf_op jit(solution)/shard_map/ppermute | solution.py:384

commit v4 on v3

--- a/solution.py
+++ b/solution.py
@@ -65,16 +65,9 @@
     return copies
 
 
-def pack_kernel(query_hbm, key_hbm, value_hbm, taps_hbm, out_ref, keep_ref, give_ref, *scratch):
-    query_ref, key_ref, value_ref, taps_ref, sems = scratch
-    pairs = (
-        (taps_hbm, taps_ref),
-        (key_hbm, key_ref),
-        (value_hbm, value_ref),
-        (query_hbm, query_ref),
-    )
+def pack_kernel(key_hbm, value_hbm, taps_hbm, out_ref, key_ref, value_ref, taps_ref, sems):
+    pairs = ((taps_hbm, taps_ref), (key_hbm, key_ref), (value_hbm, value_ref))
     copies = fetch(pairs, sems)
-    core = lax.axis_index("k")
 
     def scatter(which, read):
         for v in range(4):
@@ -88,10 +81,6 @@
     copies[1].wait()
     copies[2].wait()
     scatter(0, lambda rows, cols: key_ref[rows, cols].astype(f32) * value_ref[rows, cols].astype(f32))
-    copies[3].wait()
-    for i, ref in enumerate((query_ref, key_ref, value_ref)):
-        for dst, half in ((keep_ref, core), (give_ref, 1 - core)):
-            dst[i] = ref[:, pl.ds(pl.multiple_of(half * 256, 256), 256)]
 
 
 def pick(position, choices):
@@ -102,7 +91,7 @@
     )
 
 
-def conv_kernel(in_ref, fwd_hbm, back_hbm, *refs):
+def conv_kernel(in_ref, bias_ref, fwd_hbm, back_hbm, *refs):
     out_ref, fwd, back, both, spec, prod, acc, sems = refs
     tables = []
     for i in range(STEPS):
@@ -126,9 +115,17 @@
     def rolled(v):
         return [v] + [pltpu.roll(v, 32 * i, 1) for i in (1, 2, 3)]
 
+    start = lax.axis_index("k") * 256 + (lax.axis_index("h") * 4 + lax.axis_index("y")) * 32
+    tile = pl.multiple_of(start // 128 * 128, 128)
+    bias = pltpu.roll(bias_ref[:, pl.ds(tile, 128)], 128 - start % 128, 1)
+    bias = jnp.where(lanes(1) < 32, bias, 0.0)
+
     for step in range(STEPS):
         copies[2 * step].wait()
         spec[...] = dot(fwd[step, 0], both[...]) + dot(fwd[step, 1], both[...])
+        spec[:FREQS, 256:384] += bias
+        if step == 0:
+            spec[FREQS : FREQS + 1, 256:384] += bias
 
         def body(i, carry, step=step):
             base = pl.multiple_of(i * rows, rows)
@@ -186,22 +183,20 @@
                 out_ref[h * 4 + y, kk] = block.astype(bf16)
 
 
-def gate_kernel(in_ref, own_ref, partner_ref, bias_ref, out_ref):
+def gate_kernel(in_ref, own_ref, partner_ref, out_ref):
     core = lax.axis_index("k")
     for h in range(2):
         cols = slice(h * 128, (h + 1) * 128)
-        bias = bias_ref[:, pl.ds(pl.multiple_of(core * 256 + h * 128, 128), 128)]
-        for other, ref in enumerate((own_ref, partner_ref)):
+        own_cols = pl.ds(pl.multiple_of(core * 256 + h * 128, 128), 128)
+        for other, (ref, at) in enumerate(((own_ref, own_cols), (partner_ref, cols))):
             kk = (core + other) % 2
             blocks = swap_groups([in_ref[h * 4 + y, kk].astype(f32) for y in range(4)])
             for r, conv in enumerate(blocks):
                 rows = slice(r * 64, (r + 1) * 64)
-                q, k, v = [ref[i, rows, cols].astype(f32) for i in range(3)]
-                out_ref[other, rows, cols] = (q * (conv + bias * (k * v))).astype(bf16)
-
-
-PIECES = [(0, dy, p) for dy in (0, 3, 1, 2) for p in (0, 1)]
-PIECES += [(1, dy, p) for dy in (0, 3, 1) for p in (0, 1)] + [(1, 2, 0), (1, 2, 1)]
+                out_ref[other, rows, cols] = (ref[rows, at].astype(f32) * conv).astype(bf16)
+
+
+PIECES = [(dh, dy, p) for dh in (0, 1) for dy in (0, 1, 2, 3) for p in (0, 1)]
 
 
 def beside(blocks, p):
@@ -209,7 +204,7 @@
 
 
 def first_kernel(*refs):
-    gated, weights, outs = refs[:4], refs[4:13], refs[13:]
+    gated, weights, outs = refs[:4], refs[4:12], refs[12:]
     mine_ref, other_ref, rest_mine, rest_other, rhs, sems = outs
     at = {a: lax.axis_index(a) for a in AXES}
     swapped = (at["k"] + at["l"]) % 2
@@ -220,8 +215,7 @@
         x = (2 * h + y // 2 - at["x"] + 4) % 4
         rows = pl.ds(pl.multiple_of(rest * 1024 + x * 256, 256), 256)
         cols = pl.ds(pl.multiple_of(((swapped + p) % 2) * 512, 512), 512)
-        piece = weights[7 + p] if i >= 14 else weights[i // 2].at[p]
-        pairs.append((piece, rhs.at[rows, cols]))
+        pairs.append((weights[i // 2].at[p], rhs.at[rows, cols]))
     for copy in fetch(pairs, sems):
         copy.wait()
     for p in range(2):
@@ -252,32 +246,30 @@
     return pl.CostEstimate(flops=int(microseconds * rate), bytes_accessed=0, transcendentals=0)
 
 
-def pack(query, key_in, value_in, taps):
-    half = jax.ShapeDtypeStruct((3, 256, 256), bf16)
+def pack(key_in, value_in, taps):
     return pl.pallas_call(
         pack_kernel,
-        out_shape=[jax.ShapeDtypeStruct((2, 4, 2, 2, 64, 128), bf16), half, half],
-        in_specs=[ANY] * 4,
-        out_specs=[VMEM] * 3,
+        out_shape=jax.ShapeDtypeStruct((2, 4, 2, 2, 64, 128), bf16),
+        in_specs=[ANY] * 3,
+        out_specs=VMEM,
         scratch_shapes=[
             pltpu.VMEM((256, 512), bf16),
             pltpu.VMEM((256, 512), bf16),
-            pltpu.VMEM((256, 512), bf16),
             pltpu.VMEM((256, 512), f32),
-            pltpu.SemaphoreType.DMA((4,)),
+            pltpu.SemaphoreType.DMA((3,)),
         ],
         compiler_params=params(LARGE),
         cost_estimate=cost(2),
         name="pack",
-    )(query, key_in, value_in, taps)
-
-
-def convolve(received):
+    )(key_in, value_in, taps)
+
+
+def convolve(received, bias):
     fwd, back = transform_tables()
     return pl.pallas_call(
         conv_kernel,
         out_shape=jax.ShapeDtypeStruct((8, 2, 64, 128), bf16),
-        in_specs=[VMEM, ANY, ANY],
+        in_specs=[VMEM, VMEM, ANY, ANY],
         out_specs=VMEM,
         scratch_shapes=[
             pltpu.VMEM(fwd.shape, bf16),
@@ -291,19 +283,19 @@
         compiler_params=params(LARGE),
         cost_estimate=cost(10),
         name="convolve",
-    )(received, jnp.asarray(fwd), jnp.asarray(back))
-
-
-def gate(conv, own, partner, bias):
+    )(received, bias, jnp.asarray(fwd), jnp.asarray(back))
+
+
+def gate(conv, own, partner):
     return pl.pallas_call(
         gate_kernel,
         out_shape=jax.ShapeDtypeStruct((2, 256, 256), bf16),
-        in_specs=[VMEM] * 4,
+        in_specs=[VMEM] * 3,
         out_specs=VMEM,
         compiler_params=params(),
         cost_estimate=cost(1),
         name="gate",
-    )(conv, own, partner, bias)
+    )(conv, own, partner)
 
 
 def project_first(gated, weights):
@@ -312,7 +304,7 @@
     return pl.pallas_call(
         first_kernel,
         out_shape=[part, part, rest, rest],
-        in_specs=[VMEM] * 4 + [ANY] * 9,
+        in_specs=[VMEM] * 4 + [ANY] * 8,
         out_specs=[VMEM] * 4,
         scratch_shapes=[pltpu.VMEM((2048, 1024), bf16), pltpu.SemaphoreType.DMA((16,))],
         compiler_params=params(32 * MIB),
@@ -347,11 +339,12 @@
     core = lax.axis_index("k")
     tie = lax.optimization_barrier
     bias = conv_bias.reshape(1, 512)
-    packed, own, give = pack(query, key_in, value_in, filter_taps)
+    packed = pack(key_in, value_in, filter_taps)
     received = lax.all_to_all(
         packed.reshape(16, 2, 64, 128), SEQ, split_axis=0, concat_axis=0, tiled=True
     )
-    partner = shift(give, "k", 1)
+    other_half = lax.dynamic_slice(query, (0, (1 - core) * 256), (256, 256))
+    partner = shift(other_half, "k", 1)
 
     swaps = []
     for k in range(2):
@@ -362,28 +355,30 @@
     keep = lax.dynamic_slice(out_weight, (core * 256, 0), (256, 512))
     give = lax.dynamic_slice(out_weight, ((1 - core) * 256, 0), (256, 512))
     weight = jnp.stack([keep, shift(give, "k", 1)])
-    down, two, up = around(weight, "y")[1:]
+    up, down = shift(weight, "y", 1), shift(weight, "y", -1)
+    received, partner, weight = tie((received, partner, weight))
+
     across = shift(weight, "h", 1)
-    received, partner, weight = tie((received, partner, weight))
-
-    conv, up, down, two, across = tie((convolve(received), up, down, two, across))
-    weights = (weight, up, down, two, across)
+    conv, up, down, weight = tie((convolve(received, bias), up, down, weight))
+    two = shift(weight, "y", 2)
     conv = lax.all_to_all(conv, ("h", "y"), split_axis=0, concat_axis=0, tiled=True)
-    up, down = shift(across, "y", 1), shift(across, "y", -1)
-    mine = gate(conv, own, partner, bias)
+    two_over = shift(across, "y", 2)
+    conv, across, two = tie((conv, across, two))
+    weights = (weight, down, two, up)
+
+    mine = gate(conv, query, partner)
     other = lax.ppermute(mine, "l", [(i, i ^ 2) for i in range(4)])
-    mine, other, up, down = tie((around(mine, "x"), other, up, down))
-
+    mine, other, across, two = tie((around(mine, "x"), other, across, two_over))
     other = around(other, "x")
-    weights += (up, down, shift(up[0], "y", 1), shift(down[1], "y", -1))
+    weights += (across, shift(across, "y", -1), two, shift(across, "y", 1))
     half_mine, half_other, rest_mine, rest_other = project_first(mine, weights)
     other, half_mine, rest_mine = tie((other, half_mine, rest_mine))
     own, partner = project_rest(other, half_other, rest_other)
     send = (own + shift(partner, "k", 1)).astype(bf16)
-    send, other, half_mine = tie((send, other, half_mine))
     from_pair = lax.ppermute(send, "l", [(i, i ^ 1) for i in range(4)])
     own, partner = project_rest(other, half_mine, rest_mine)
-    return (own + shift(partner, "k", 1) + from_pair.astype(f32)).astype(bf16)
+    total, from_pair = tie((own + shift(partner, "k", 1), from_pair))
+    return (total + from_pair.astype(f32)).astype(bf16)
 
 
 def solution(mesh):

time: 123 us -> 119 us (0.967)
  starting transfers between devices: 54.4 us -> 43.2 us
  waiting for transfers between devices: 48.8 us -> 56.6 us
  local copies, waits for them, and re-layouts: 2.86 us -> 0.78 us
    ppermute x18 -> x17, starting transfers between devices: 28.4 us -> 17 us  [shift(): return lax.ppermute(v, axis, [(i, (i + by) % n) for i in range(n)])]
    ppermute x18 -> x17, waiting for transfers between devices: 22.5 us -> 15.2 us  [shift(): return lax.ppermute(v, axis, [(i, (i + by) % n) for i in range(n)])]
    all_to_all x1, waiting for transfers between devices: 7.42 us -> 14.6 us  [body(): lax.all_to_all(conv, ('h', 'y'), split_axis=0, concat_axis=0, tiled=True)]
    all_to_all x1, waiting for transfers between devices: 3.59 us -> 10.5 us  [body(): lax.all_to_all(packed.reshape(16, 2, 64, 128), SEQ, split_axis=0, concat_...]
    ppermute x1, starting transfers between devices: 6.72 us -> 0.09 us  [body(): other = lax.ppermute(mine, 'l', [(i, i ^ 2) for i in range(4)])]
    all_to_all x1, starting transfers between devices: 4.08 us -> 7.83 us  [body(): lax.all_to_all(conv, ('h', 'y'), split_axis=0, concat_axis=0, tiled=True)]
    ppermute x1, starting transfers between devices: 0.01 us -> 2.89 us  [body(): from_pair = lax.ppermute(send, 'l', [(i, i ^ 1) for i in range(4)])]
    ppermute x1, waiting for transfers between devices: 7.45 us -> 9.98 us  [body(): other = lax.ppermute(mine, 'l', [(i, i ^ 2) for i in range(4)])]
  transfers between devices with their start and end apart: 23 -> 22, of which waited for: 13 -> 9; matrix products, arithmetic and copies ran while one was open for 0% -> 0% of each run, Pallas kernels for 12% -> 13%
where the time goes in v4:
time: 119 us; the launch traced here: 118 us
  waiting for transfers between devices  56.6 us (48%)
  starting transfers between devices  43.2 us (36%)
  Pallas kernels  16.5 us (14%)
    ppermute x17, starting transfers between devices, shift(): return lax.ppermute(v, axis, [(i, (i + by) % n) for i in range(n)])  17 us
    ppermute x17, waiting for transfers between devices, shift(): return lax.ppermute(v, axis, [(i, (i + by) % n) for i in range(n)])  15.2 us
    all_to_all x1, waiting for transfers between devices, body(): lax.all_to_all(conv, ('h', 'y'), split_axis=0, concat_axis=0, tiled=True)  14.6 us
    all_to_all x1, waiting for transfers between devices, body(): lax.all_to_all(packed.reshape(16, 2, 64, 128), SEQ, split_axis=0, concat_...  10.5 us
    all_to_all x1, starting transfers between devices, body(): lax.all_to_all(packed.reshape(16, 2, 64, 128), SEQ, split_axis=0, concat_...  10.5 us
    ppermute x1, waiting for transfers between devices, body(): other = lax.ppermute(mine, 'l', [(i, i ^ 2) for i in range(4)])  9.98 us
    pallas_call x1, Pallas kernels, convolve(): pl.pallas_call(conv_kernel, out_shape=jax.ShapeDtypeStruct((8, 2, 64, 128...  9.4 us
    all_to_all x1, starting transfers between devices, body(): lax.all_to_all(conv, ('h', 'y'), split_axis=0, concat_axis=0, tiled=True)  7.83 us
  transfers between devices with their start and end apart: 22, of which 9 were waited for; matrix products, arithmetic and copies ran while one was open for 0% of the time, Pallas kernels for 13%

profile of v4, /device:TPU:1, one launch (start us, length us, event | category | flops | bytes accessed | tf_op | source)
XLA Modules:
  0.0 118.3 jit_solution(7166502043307768212)
XLA Ops:
  0.0 4.9 %collective-permute-start.1 = (bf16[512,512]{1,0:T(8,128)(2,1)}, bf16[512,512]{1,0:T(8,128)(2,1)S(1)}, u32[]{:S(2)}, u32[]{:S(2)}) collective-permute-start(bf16[512,512]{1,0:T(8,128)(2,1)} %param.13), channel_id=1, source_target_pairs={{0,0},{1,16},{2,2},{3,18},{16,1},{17,17},{18,3},{19,19},{4,4},{5,2... | collective-permute-start | bytes 1572872 | tf_op jit(solution)/shard_map/ppermute | solution.py:354
  4.9 2.6 %pack.1 = bf16[2,4,2,2,64,128]{5,4,3,2,1,0:T(8,128)(2,1)} custom-call(bf16[256,512]{1,0:T(8,128)(2,1)} %key_hbm.1, bf16[256,512]{1,0:T(8,128)(2,1)} %value_hbm.1, f32[256,512]{1,0:T(8,128)} %taps_hbm.1), custom_call_target="tpu_custom_call" | custom-call | flops 2147483648 | tf_op jit(solution)/shard_map/pack/pallas_call | solution.py:250
  7.6 10.5 %all-to-all-start = ((bf16[16,2,64,128]{3,2,1,0:T(8,128)(2,1)}), bf16[16,2,64,128]{3,2,1,0:T(8,128)(2,1)S(1)}, u32[]{:S(2)}, u32[]{:S(2)}) async-start(bf16[16,2,64,128]{3,2,1,0:T(8,128)(2,1)} %bitcast.5), calls=%async_computation | async-start | bytes 1048576 | tf_op jit(solution)/shard_map/all_to_all | solution.py:343
  18.3 0.5 collective-permute-start
  18.8 0.9 collective-permute-done.2
  19.8 1.5 %collective-permute-start.3 = (bf16[2,256,512]{2,1,0:T(8,128)(2,1)S(1)}, bf16[2,256,512]{2,1,0:T(8,128)(2,1)S(1)}, u32[]{:S(2)}, u32[]{:S(2)}) collective-permute-start(bf16[2,256,512]{2,1,0:T(8,128)(2,1)S(1)} %pad_maximum_fusion.refs_4_), channel_id=1, source_target_pairs={{0,32},{32,64},{64,96},{96,0},{1,33},{33,65},{65,97},{97,1},{2,34}... | collective-permute-start | bytes 1572872 | tf_op jit(solution)/shard_map/ppermute | solution.py:331
  21.2 1.3 %collective-permute-start.4 = (bf16[2,256,512]{2,1,0:T(8,128)(2,1)S(1)}, bf16[2,256,512]{2,1,0:T(8,128)(2,1)S(1)}, u32[]{:S(2)}, u32[]{:S(2)}) collective-permute-start(bf16[2,256,512]{2,1,0:T(8,128)(2,1)S(1)} %pad_maximum_fusion.refs_4_), channel_id=1, source_target_pairs={{0,96},{32,0},{64,32},{96,64},{1,97},{33,1},{65,33},{97,65},{2,98}... | collective-permute-start | bytes 1572872 | tf_op jit(solution)/shard_map/ppermute | solution.py:331
  22.5 10.5 %all-to-all-done.in_ref = bf16[16,2,64,128]{3,2,1,0:T(8,128)(2,1)S(1)} async-done(((bf16[16,2,64,128]{3,2,1,0:T(8,128)(2,1)}), bf16[16,2,64,128]{3,2,1,0:T(8,128)(2,1)S(1)}, u32[]{:S(2)}, u32[]{:S(2)}) %all-to-all-start) | async-done | bytes 524320 | tf_op jit(solution)/shard_map/all_to_all | solution.py:343
  33.2 0.7 copy-done.1
  33.9 9.4 %convolve.1 = bf16[8,2,64,128]{3,2,1,0:T(8,128)(2,1)} custom-call(bf16[16,2,64,128]{3,2,1,0:T(8,128)(2,1)} %copy-done.1, f32[1,512]{1,0:T(1,128)} %bitcast.7, bf16[4,2,256,512]{3,2,1,0:T(8,128)(2,1)} %constant.18.clone.fwd_hbm, bf16[4,2,512,256]{3,2,1,0:T(8,128)(2,1)} %constant.19.clone.back_hbm), custom_call_target="tpu_custom_call" | custom-call | flops 10737418240 | tf_op jit(solution)/shard_map/convolve/pallas_call | solution.py:269
  43.3 0.8 collective-permute-start.6
  44.1 7.8 %all-to-all-start.1 = ((bf16[8,2,64,128]{3,2,1,0:T(8,128)(2,1)}), bf16[8,2,64,128]{3,2,1,0:T(8,128)(2,1)S(1)}, u32[]{:S(2)}, u32[]{:S(2)}) async-start(bf16[8,2,64,128]{3,2,1,0:T(8,128)(2,1)} %convolve.1), calls=%async_computation.1 | async-start | bytes 524288 | tf_op jit(solution)/shard_map/all_to_all | solution.py:364
  51.9 3.0 %collective-permute-start.11 = (bf16[2,256,512]{2,1,0:T(8,128)(2,1)S(1)}, bf16[2,256,512]{2,1,0:T(8,128)(2,1)}, u32[]{:S(2)}, u32[]{:S(2)}) collective-permute-start(bf16[2,256,512]{2,1,0:T(8,128)(2,1)S(1)} %collective-permute-done.5.refs_8_), channel_id=1, source_target_pairs={{0,64},{32,96},{64,0},{96,32},{1,65},{33,97},{65,1},{97,33},{2,66}... | collective-permute-start | bytes 1572872 | tf_op jit(solution)/shard_map/ppermute | solution.py:331
  54.9 14.6 %all-to-all-done.1.in_ref = bf16[8,2,64,128]{3,2,1,0:T(8,128)(2,1)S(1)} async-done(((bf16[8,2,64,128]{3,2,1,0:T(8,128)(2,1)}), bf16[8,2,64,128]{3,2,1,0:T(8,128)(2,1)S(1)}, u32[]{:S(2)}, u32[]{:S(2)}) %all-to-all-start.1) | async-done | bytes 262176 | tf_op jit(solution)/shard_map/all_to_all | solution.py:364
  69.9 2.6 %collective-permute-start.7 = (bf16[2,256,256]{2,1,0:T(8,128)(2,1)S(1)}, bf16[2,256,256]{2,1,0:T(8,128)(2,1)S(1)}, u32[]{:S(2)}, u32[]{:S(2)}) collective-permute-start(bf16[2,256,256]{2,1,0:T(8,128)(2,1)S(1)} %gate.1.refs_0_), channel_id=1, source_target_pairs={{0,12},{4,0},{8,4},{12,8},{1,13},{5,1},{9,5},{13,9},{2,14},{6,2},{... | collective-permute-start | bytes 786440 | tf_op jit(solution)/shard_map/ppermute | solution.py:331
  72.5 0.5 collective-permute-start.8
  73.0 0.6 collective-permute-start.9
  73.6 10.0 %collective-permute-done.10.g0 = bf16[2,256,256]{2,1,0:T(8,128)(2,1)S(1)} collective-permute-done((bf16[2,256,256]{2,1,0:T(8,128)(2,1)S(1)}, bf16[2,256,256]{2,1,0:T(8,128)(2,1)S(1)}, u32[]{:S(2)}, u32[]{:S(2)}) %collective-permute-start.10) | collective-permute-done | bytes 262176 | tf_op jit(solution)/shard_map/ppermute | solution.py:370
  83.6 3.0 %collective-permute-done.9.refs_3_ = bf16[2,256,256]{2,1,0:T(8,128)(2,1)S(1)} collective-permute-done((bf16[2,256,256]{2,1,0:T(8,128)(2,1)S(1)}, bf16[2,256,256]{2,1,0:T(8,128)(2,1)S(1)}, u32[]{:S(2)}, u32[]{:S(2)}) %collective-permute-start.9) | collective-permute-done | bytes 262176 | tf_op jit(solution)/shard_map/ppermute | solution.py:331
  86.6 0.8 collective-permute-start.15
  87.4 0.7 collective-permute-start.16
  88.3 1.3 %collective-permute-start.14 = (bf16[2,256,256]{2,1,0:T(8,128)(2,1)S(1)}, bf16[2,256,256]{2,1,0:T(8,128)(2,1)S(1)}, u32[]{:S(2)}, u32[]{:S(2)}) collective-permute-start(bf16[2,256,256]{2,1,0:T(8,128)(2,1)S(1)} %collective-permute-done.10.g0), channel_id=1, source_target_pairs={{0,4},{4,8},{8,12},{12,0},{1,5},{5,9},{9,13},{13,1},{2,6},{6,10},{... | collective-permute-start | bytes 786440 | tf_op jit(solution)/shard_map/ppermute | solution.py:331
  89.5 8.8 %collective-permute-done.15.refs_9_ = bf16[2,256,512]{2,1,0:T(8,128)(2,1)S(1)} collective-permute-done((bf16[2,256,512]{2,1,0:T(8,128)(2,1)S(1)}, bf16[2,256,512]{2,1,0:T(8,128)(2,1)S(1)}, u32[]{:S(2)}, u32[]{:S(2)}) %collective-permute-start.15) | collective-permute-done | bytes 524320 | tf_op jit(solution)/shard_map/ppermute | solution.py:331
  98.3 1.7 %collective-permute-done.16.refs_11_ = bf16[2,256,512]{2,1,0:T(8,128)(2,1)S(1)} collective-permute-done((bf16[2,256,512]{2,1,0:T(8,128)(2,1)S(1)}, bf16[2,256,512]{2,1,0:T(8,128)(2,1)S(1)}, u32[]{:S(2)}, u32[]{:S(2)}) %collective-permute-start.16) | collective-permute-done | bytes 524320 | tf_op jit(solution)/shard_map/ppermute | solution.py:331
  100.0 2.8 %project_first.1 = (f32[2,256,512]{2,1,0:T(8,128)S(1)}, f32[2,256,512]{2,1,0:T(8,128)S(1)}, bf16[1024,512]{1,0:T(8,128)(2,1)S(1)}, bf16[1024,512]{1,0:T(8,128)(2,1)S(1)}) custom-call(bf16[2,256,256]{2,1,0:T(8,128)(2,1)S(1)} %gate.1.refs_0_, bf16[2,256,256]{2,1,0:T(8,128)(2,1)S(1)} %collective-permute-done.7.refs_1_, ...), custom_call_target="tpu_custom_call" | custom-call | flops 5368709120 | tf_op jit(solution)/shard_map/project_first/pallas_call | solution.py:304
  102.9 0.7 project_rest.3
  103.6 3.0 %collective-permute-start.18 = (f32[256,512]{1,0:T(8,128)S(1)}, f32[256,512]{1,0:T(8,128)S(1)}, u32[]{:S(2)}, u32[]{:S(2)}) collective-permute-start(f32[256,512]{1,0:T(8,128)S(1)} %get-tuple-element.68), channel_id=1, source_target_pairs={{0,16},{16,0},{1,17},{17,1},{2,18},{18,2},{3,19},{19,3},{4,20},{20... | collective-permute-start | bytes 1572872 | tf_op jit(solution)/shard_map/ppermute | solution.py:331
  106.6 0.7 project_rest.2
  107.4 0.7 collective-permute-done.18
  108.2 2.9 %collective-permute-start.19 = (bf16[256,512]{1,0:T(8,128)(2,1)S(1)}, bf16[256,512]{1,0:T(8,128)(2,1)S(1)}, u32[]{:S(2)}, u32[]{:S(2)}) collective-permute-start(bf16[256,512]{1,0:T(8,128)(2,1)S(1)} %add_convert_fusion.1), channel_id=1, source_target_pairs={{0,1},{1,0},{2,3},{3,2},{4,5},{5,4},{6,7},{7,6},{8,9},{9,8},{10,11... | collective-permute-start | bytes 786440 | tf_op jit(solution)/shard_map/ppermute | solution.py:378
  111.2 6.3 %collective-permute-done.19 = bf16[256,512]{1,0:T(8,128)(2,1)S(1)} collective-permute-done((bf16[256,512]{1,0:T(8,128)(2,1)S(1)}, bf16[256,512]{1,0:T(8,128)(2,1)S(1)}, u32[]{:S(2)}, u32[]{:S(2)}) %collective-permute-start.19) | collective-permute-done | bytes 262176 | tf_op jit(solution)/shard_map/ppermute | solution.py:378
  117.5 0.8 add_convert_fusion
  (28 shorter events, 1.3 us)
Async XLA Ops:
  0.0 18.0 %collective-permute-start.1 = (bf16[512,512]{1,0:T(8,128)(2,1)}, bf16[512,512]{1,0:T(8,128)(2,1)S(1)}, u32[]{:S(2)}, u32[]{:S(2)}) collective-permute-start(bf16[512,512]{1,0:T(8,128)(2,1)} %param.13), channel_id=1, source_target_pairs={{0,0},{1,16},{2,2},{3,18},{16,1},{17,17},{18,3},{19,19},{4,4},{5,2... | collective-permute-start | bytes 1572872 | tf_op jit(solution)/shard_map/ppermute | solution.py:354
  7.6 10.7 %copy-start = (bf16[256,512]{1,0:T(8,128)(2,1)S(1)}, bf16[256,512]{1,0:T(8,128)(2,1)}, u32[]{:S(2)}) copy-start(bf16[256,512]{1,0:T(8,128)(2,1)} %own_ref.1) | copy-start | bytes 786436
  7.6 25.5 %all-to-all-start = ((bf16[16,2,64,128]{3,2,1,0:T(8,128)(2,1)}), bf16[16,2,64,128]{3,2,1,0:T(8,128)(2,1)S(1)}, u32[]{:S(2)}, u32[]{:S(2)}) async-start(bf16[16,2,64,128]{3,2,1,0:T(8,128)(2,1)} %bitcast.5), calls=%async_computation | async-start | bytes 1048576 | tf_op jit(solution)/shard_map/all_to_all | solution.py:343
  18.1 1.6 %collective-permute-start.2 = (bf16[256,512]{1,0:T(8,128)(2,1)S(1)}, bf16[256,512]{1,0:T(8,128)(2,1)S(1)}, u32[]{:S(2)}, u32[]{:S(2)}) collective-permute-start(bf16[256,512]{1,0:T(8,128)(2,1)S(1)} %get-tuple-element.72), channel_id=1, source_target_pairs={{0,16},{16,0},{1,17},{17,1},{2,18},{18,2},{3,19},{19,3},{4,20},{20... | collective-permute-start | bytes 786440 | tf_op jit(solution)/shard_map/ppermute | solution.py:331
  18.3 4.2 %collective-permute-start = (bf16[256,256]{1,0:T(8,128)(2,1)S(1)}, bf16[256,256]{1,0:T(8,128)(2,1)S(1)}, u32[]{:S(2)}, u32[]{:S(2)}) collective-permute-start(bf16[256,256]{1,0:T(8,128)(2,1)S(1)} %constant_dynamic-slice_fusion.1), channel_id=1, source_target_pairs={{0,16},{16,0},{1,17},{17,1},{2,18},{18,2},{3,19},{19,3},{4,20},{20... | collective-permute-start | bytes 393224 | tf_op jit(solution)/shard_map/ppermute | solution.py:331
  19.8 23.5 %collective-permute-start.3 = (bf16[2,256,512]{2,1,0:T(8,128)(2,1)S(1)}, bf16[2,256,512]{2,1,0:T(8,128)(2,1)S(1)}, u32[]{:S(2)}, u32[]{:S(2)}) collective-permute-start(bf16[2,256,512]{2,1,0:T(8,128)(2,1)S(1)} %pad_maximum_fusion.refs_4_), channel_id=1, source_target_pairs={{0,32},{32,64},{64,96},{96,0},{1,33},{33,65},{65,97},{97,1},{2,34}... | collective-permute-start | bytes 1572872 | tf_op jit(solution)/shard_map/ppermute | solution.py:331
  21.2 22.1 %collective-permute-start.4 = (bf16[2,256,512]{2,1,0:T(8,128)(2,1)S(1)}, bf16[2,256,512]{2,1,0:T(8,128)(2,1)S(1)}, u32[]{:S(2)}, u32[]{:S(2)}) collective-permute-start(bf16[2,256,512]{2,1,0:T(8,128)(2,1)S(1)} %pad_maximum_fusion.refs_4_), channel_id=1, source_target_pairs={{0,96},{32,0},{64,32},{96,64},{1,97},{33,1},{65,33},{97,65},{2,98}... | collective-permute-start | bytes 1572872 | tf_op jit(solution)/shard_map/ppermute | solution.py:331
  33.1 0.8 copy-start.1
  33.1 18.9 %collective-permute-start.5 = (bf16[2,256,512]{2,1,0:T(8,128)(2,1)S(1)}, bf16[2,256,512]{2,1,0:T(8,128)(2,1)S(1)}, u32[]{:S(2)}, u32[]{:S(2)}) collective-permute-start(bf16[2,256,512]{2,1,0:T(8,128)(2,1)S(1)} %pad_maximum_fusion.refs_4_), channel_id=1, source_target_pairs={{0,128},{128,0},{1,129},{129,1},{2,130},{130,2},{3,131},{131,3},{4... | collective-permute-start | bytes 1572872 | tf_op jit(solution)/shard_map/ppermute | solution.py:331
  43.3 26.2 %collective-permute-start.6 = (bf16[2,256,512]{2,1,0:T(8,128)(2,1)S(1)}, bf16[2,256,512]{2,1,0:T(8,128)(2,1)S(1)}, u32[]{:S(2)}, u32[]{:S(2)}) collective-permute-start(bf16[2,256,512]{2,1,0:T(8,128)(2,1)S(1)} %pad_maximum_fusion.refs_4_), channel_id=1, source_target_pairs={{0,64},{32,96},{64,0},{96,32},{1,65},{33,97},{65,1},{97,33},{2,66}... | collective-permute-start | bytes 1572872 | tf_op jit(solution)/shard_map/ppermute | solution.py:331
  44.1 25.4 %all-to-all-start.1 = ((bf16[8,2,64,128]{3,2,1,0:T(8,128)(2,1)}), bf16[8,2,64,128]{3,2,1,0:T(8,128)(2,1)S(1)}, u32[]{:S(2)}, u32[]{:S(2)}) async-start(bf16[8,2,64,128]{3,2,1,0:T(8,128)(2,1)} %convolve.1), calls=%async_computation.1 | async-start | bytes 524288 | tf_op jit(solution)/shard_map/all_to_all | solution.py:364
  51.9 21.7 %collective-permute-start.11 = (bf16[2,256,512]{2,1,0:T(8,128)(2,1)S(1)}, bf16[2,256,512]{2,1,0:T(8,128)(2,1)}, u32[]{:S(2)}, u32[]{:S(2)}) collective-permute-start(bf16[2,256,512]{2,1,0:T(8,128)(2,1)S(1)} %collective-permute-done.5.refs_8_), channel_id=1, source_target_pairs={{0,64},{32,96},{64,0},{96,32},{1,65},{33,97},{65,1},{97,33},{2,66}... | collective-permute-start | bytes 1572872 | tf_op jit(solution)/shard_map/ppermute | solution.py:331
  69.8 13.8 %collective-permute-start.10 = (bf16[2,256,256]{2,1,0:T(8,128)(2,1)S(1)}, bf16[2,256,256]{2,1,0:T(8,128)(2,1)S(1)}, u32[]{:S(2)}, u32[]{:S(2)}) collective-permute-start(bf16[2,256,256]{2,1,0:T(8,128)(2,1)S(1)} %gate.1.refs_0_), channel_id=1, source_target_pairs={{0,2},{1,3},{2,0},{3,1},{4,6},{5,7},{6,4},{7,5},{8,10},{9,11},{10,... | collective-permute-start | bytes 786440 | tf_op jit(solution)/shard_map/ppermute | solution.py:370
  69.9 13.7 %collective-permute-start.7 = (bf16[2,256,256]{2,1,0:T(8,128)(2,1)S(1)}, bf16[2,256,256]{2,1,0:T(8,128)(2,1)S(1)}, u32[]{:S(2)}, u32[]{:S(2)}) collective-permute-start(bf16[2,256,256]{2,1,0:T(8,128)(2,1)S(1)} %gate.1.refs_0_), channel_id=1, source_target_pairs={{0,12},{4,0},{8,4},{12,8},{1,13},{5,1},{9,5},{13,9},{2,14},{6,2},{... | collective-permute-start | bytes 786440 | tf_op jit(solution)/shard_map/ppermute | solution.py:331
  72.5 11.1 %collective-permute-start.8 = (bf16[2,256,256]{2,1,0:T(8,128)(2,1)S(1)}, bf16[2,256,256]{2,1,0:T(8,128)(2,1)S(1)}, u32[]{:S(2)}, u32[]{:S(2)}) collective-permute-start(bf16[2,256,256]{2,1,0:T(8,128)(2,1)S(1)} %gate.1.refs_0_), channel_id=1, source_target_pairs={{0,8},{4,12},{8,0},{12,4},{1,9},{5,13},{9,1},{13,5},{2,10},{6,14},... | collective-permute-start | bytes 786440 | tf_op jit(solution)/shard_map/ppermute | solution.py:331
  73.0 13.6 %collective-permute-start.9 = (bf16[2,256,256]{2,1,0:T(8,128)(2,1)S(1)}, bf16[2,256,256]{2,1,0:T(8,128)(2,1)S(1)}, u32[]{:S(2)}, u32[]{:S(2)}) collective-permute-start(bf16[2,256,256]{2,1,0:T(8,128)(2,1)S(1)} %gate.1.refs_0_), channel_id=1, source_target_pairs={{0,4},{4,8},{8,12},{12,0},{1,5},{5,9},{9,13},{13,1},{2,6},{6,10},{... | collective-permute-start | bytes 786440 | tf_op jit(solution)/shard_map/ppermute | solution.py:331
  86.6 11.7 %collective-permute-start.15 = (bf16[2,256,512]{2,1,0:T(8,128)(2,1)S(1)}, bf16[2,256,512]{2,1,0:T(8,128)(2,1)S(1)}, u32[]{:S(2)}, u32[]{:S(2)}) collective-permute-start(bf16[2,256,512]{2,1,0:T(8,128)(2,1)S(1)} %collective-permute-done.5.refs_8_), channel_id=1, source_target_pairs={{0,96},{32,0},{64,32},{96,64},{1,97},{33,1},{65,33},{97,65},{2,98}... | collective-permute-start | bytes 1572872 | tf_op jit(solution)/shard_map/ppermute | solution.py:331
  87.4 12.6 %collective-permute-start.16 = (bf16[2,256,512]{2,1,0:T(8,128)(2,1)S(1)}, bf16[2,256,512]{2,1,0:T(8,128)(2,1)S(1)}, u32[]{:S(2)}, u32[]{:S(2)}) collective-permute-start(bf16[2,256,512]{2,1,0:T(8,128)(2,1)S(1)} %collective-permute-done.5.refs_8_), channel_id=1, source_target_pairs={{0,32},{32,64},{64,96},{96,0},{1,33},{33,65},{65,97},{97,1},{2,34}... | collective-permute-start | bytes 1572872 | tf_op jit(solution)/shard_map/ppermute | solution.py:331
  88.1 14.8 %collective-permute-start.12 = (bf16[2,256,256]{2,1,0:T(8,128)(2,1)S(1)}, bf16[2,256,256]{2,1,0:T(8,128)(2,1)S(1)}, u32[]{:S(2)}, u32[]{:S(2)}) collective-permute-start(bf16[2,256,256]{2,1,0:T(8,128)(2,1)S(1)} %collective-permute-done.10.g0), channel_id=1, source_target_pairs={{0,12},{4,0},{8,4},{12,8},{1,13},{5,1},{9,5},{13,9},{2,14},{6,2},{... | collective-permute-start | bytes 786440 | tf_op jit(solution)/shard_map/ppermute | solution.py:331
  88.1 14.8 %collective-permute-start.13 = (bf16[2,256,256]{2,1,0:T(8,128)(2,1)S(1)}, bf16[2,256,256]{2,1,0:T(8,128)(2,1)S(1)}, u32[]{:S(2)}, u32[]{:S(2)}) collective-permute-start(bf16[2,256,256]{2,1,0:T(8,128)(2,1)S(1)} %collective-permute-done.10.g0), channel_id=1, source_target_pairs={{0,8},{4,12},{8,0},{12,4},{1,9},{5,13},{9,1},{13,5},{2,10},{6,14},... | collective-permute-start | bytes 786440 | tf_op jit(solution)/shard_map/ppermute | solution.py:331
  88.3 14.6 %collective-permute-start.14 = (bf16[2,256,256]{2,1,0:T(8,128)(2,1)S(1)}, bf16[2,256,256]{2,1,0:T(8,128)(2,1)S(1)}, u32[]{:S(2)}, u32[]{:S(2)}) collective-permute-start(bf16[2,256,256]{2,1,0:T(8,128)(2,1)S(1)} %collective-permute-done.10.g0), channel_id=1, source_target_pairs={{0,4},{4,8},{8,12},{12,0},{1,5},{5,9},{9,13},{13,1},{2,6},{6,10},{... | collective-permute-start | bytes 786440 | tf_op jit(solution)/shard_map/ppermute | solution.py:331
  103.6 4.6 %collective-permute-start.18 = (f32[256,512]{1,0:T(8,128)S(1)}, f32[256,512]{1,0:T(8,128)S(1)}, u32[]{:S(2)}, u32[]{:S(2)}) collective-permute-start(f32[256,512]{1,0:T(8,128)S(1)} %get-tuple-element.68), channel_id=1, source_target_pairs={{0,16},{16,0},{1,17},{17,1},{2,18},{18,2},{3,19},{19,3},{4,20},{20... | collective-permute-start | bytes 1572872 | tf_op jit(solution)/shard_map/ppermute | solution.py:331
  107.3 3.8 %collective-permute-start.17 = (f32[256,512]{1,0:T(8,128)S(1)}, f32[256,512]{1,0:T(8,128)S(1)}, u32[]{:S(2)}, u32[]{:S(2)}) collective-permute-start(f32[256,512]{1,0:T(8,128)S(1)} %get-tuple-element.64), channel_id=1, source_target_pairs={{0,16},{16,0},{1,17},{17,1},{2,18},{18,2},{3,19},{19,3},{4,20},{20... | collective-permute-start | bytes 1572872 | tf_op jit(solution)/shard_map/ppermute | solution.py:331
  108.2 9.3 %collective-permute-start.19 = (bf16[256,512]{1,0:T(8,128)(2,1)S(1)}, bf16[256,512]{1,0:T(8,128)(2,1)S(1)}, u32[]{:S(2)}, u32[]{:S(2)}) collective-permute-start(bf16[256,512]{1,0:T(8,128)(2,1)S(1)} %add_convert_fusion.1), channel_id=1, source_target_pairs={{0,1},{1,0},{2,3},{3,2},{4,5},{5,4},{6,7},{7,6},{8,9},{9,8},{10,11... | collective-permute-start | bytes 786440 | tf_op jit(solution)/shard_map/ppermute | solution.py:378

commit v5 on v4

--- a/solution.py
+++ b/solution.py
@@ -293,7 +293,7 @@
         in_specs=[VMEM] * 3,
         out_specs=VMEM,
         compiler_params=params(),
-        cost_estimate=cost(1),
+        cost_estimate=cost(40),
         name="gate",
     )(conv, own, partner)
 
@@ -363,12 +363,13 @@
     two = shift(weight, "y", 2)
     conv = lax.all_to_all(conv, ("h", "y"), split_axis=0, concat_axis=0, tiled=True)
     two_over = shift(across, "y", 2)
-    conv, across, two = tie((conv, across, two))
-    weights = (weight, down, two, up)
+    conv, across = tie((conv, across))
 
     mine = gate(conv, query, partner)
     other = lax.ppermute(mine, "l", [(i, i ^ 2) for i in range(4)])
-    mine, other, across, two = tie((around(mine, "x"), other, across, two_over))
+    two, two_over, across, other, mine = tie((two, two_over, across, other, around(mine, "x")))
+    weights = (weight, down, two, up)
+    two = two_over
     other = around(other, "x")
     weights += (across, shift(across, "y", -1), two, shift(across, "y", 1))
     half_mine, half_other, rest_mine, rest_other = project_first(mine, weights)

time: 119 us -> 117 us (0.983)
  starting transfers between devices: 43.2 us -> 40.3 us
  waiting for transfers between devices: 56.6 us -> 58.1 us
    ppermute x17, waiting for transfers between devices: 15.2 us -> 23.8 us  [shift(): return lax.ppermute(v, axis, [(i, (i + by) % n) for i in range(n)])]
    ppermute x1, waiting for transfers between devices: 9.98 us -> 1.51 us  [body(): other = lax.ppermute(mine, 'l', [(i, i ^ 2) for i in range(4)])]
    ppermute x1, starting transfers between devices: 2.89 us -> 0.09 us  [body(): from_pair = lax.ppermute(send, 'l', [(i, i ^ 1) for i in range(4)])]
  transfers between devices with their start and end apart: 22 -> 22, of which waited for: 9 -> 12; matrix products, arithmetic and copies ran while one was open for 0% -> 0% of each run, Pallas kernels for 13% -> 14%
where the time goes in v5:
time: 117 us
  waiting for transfers between devices  58.1 us (50%)
  starting transfers between devices  40.3 us (34%)
  Pallas kernels  16.5 us (14%)
    ppermute x17, waiting for transfers between devices, shift(): return lax.ppermute(v, axis, [(i, (i + by) % n) for i in range(n)])  23.8 us
    ppermute x17, starting transfers between devices, shift(): return lax.ppermute(v, axis, [(i, (i + by) % n) for i in range(n)])  17.6 us
    all_to_all x1, waiting for transfers between devices, body(): lax.all_to_all(conv, ('h', 'y'), split_axis=0, concat_axis=0, tiled=True)  15.7 us
    all_to_all x1, waiting for transfers between devices, body(): lax.all_to_all(packed.reshape(16, 2, 64, 128), SEQ, split_axis=0, concat_...  10.5 us
    all_to_all x1, starting transfers between devices, body(): lax.all_to_all(packed.reshape(16, 2, 64, 128), SEQ, split_axis=0, concat_...  10.5 us
    pallas_call x1, Pallas kernels, convolve(): pl.pallas_call(conv_kernel, out_shape=jax.ShapeDtypeStruct((8, 2, 64, 128...  9.4 us
    all_to_all x1, starting transfers between devices, body(): lax.all_to_all(conv, ('h', 'y'), split_axis=0, concat_axis=0, tiled=True)  7.27 us
    ppermute x1, waiting for transfers between devices, body(): from_pair = lax.ppermute(send, 'l', [(i, i ^ 1) for i in range(4)])  6.44 us
  transfers between devices with their start and end apart: 22, of which 12 were waited for; matrix products, arithmetic and copies ran while one was open for 0% of the time, Pallas kernels for 14%

profile of v5, /device:TPU:1, one launch (start us, length us, event | category | flops | bytes accessed | tf_op | source)
XLA Modules:
  0.0 116.9 jit_solution(957068599715470747)
XLA Ops:
  0.0 4.9 %collective-permute-start.1 = (bf16[512,512]{1,0:T(8,128)(2,1)}, bf16[512,512]{1,0:T(8,128)(2,1)S(1)}, u32[]{:S(2)}, u32[]{:S(2)}) collective-permute-start(bf16[512,512]{1,0:T(8,128)(2,1)} %param.13), channel_id=1, source_target_pairs={{0,0},{1,16},{2,2},{3,18},{16,1},{17,17},{18,3},{19,19},{4,4},{5,2... | collective-permute-start | bytes 1572872 | tf_op jit(solution)/shard_map/ppermute | solution.py:354
  4.9 2.6 %pack.1 = bf16[2,4,2,2,64,128]{5,4,3,2,1,0:T(8,128)(2,1)} custom-call(bf16[256,512]{1,0:T(8,128)(2,1)} %key_hbm.1, bf16[256,512]{1,0:T(8,128)(2,1)} %value_hbm.1, f32[256,512]{1,0:T(8,128)} %taps_hbm.1), custom_call_target="tpu_custom_call" | custom-call | flops 2147483648 | tf_op jit(solution)/shard_map/pack/pallas_call | solution.py:250
  7.6 10.5 %all-to-all-start = ((bf16[16,2,64,128]{3,2,1,0:T(8,128)(2,1)}), bf16[16,2,64,128]{3,2,1,0:T(8,128)(2,1)S(1)}, u32[]{:S(2)}, u32[]{:S(2)}) async-start(bf16[16,2,64,128]{3,2,1,0:T(8,128)(2,1)} %bitcast.5), calls=%async_computation | async-start | bytes 1048576 | tf_op jit(solution)/shard_map/all_to_all | solution.py:343
  18.8 0.9 collective-permute-done.2
  19.8 1.5 %collective-permute-start.3 = (bf16[2,256,512]{2,1,0:T(8,128)(2,1)S(1)}, bf16[2,256,512]{2,1,0:T(8,128)(2,1)S(1)}, u32[]{:S(2)}, u32[]{:S(2)}) collective-permute-start(bf16[2,256,512]{2,1,0:T(8,128)(2,1)S(1)} %pad_maximum_fusion.refs_4_), channel_id=1, source_target_pairs={{0,32},{32,64},{64,96},{96,0},{1,33},{33,65},{65,97},{97,1},{2,34}... | collective-permute-start | bytes 1572872 | tf_op jit(solution)/shard_map/ppermute | solution.py:331
  21.2 1.3 %collective-permute-start.4 = (bf16[2,256,512]{2,1,0:T(8,128)(2,1)S(1)}, bf16[2,256,512]{2,1,0:T(8,128)(2,1)S(1)}, u32[]{:S(2)}, u32[]{:S(2)}) collective-permute-start(bf16[2,256,512]{2,1,0:T(8,128)(2,1)S(1)} %pad_maximum_fusion.refs_4_), channel_id=1, source_target_pairs={{0,96},{32,0},{64,32},{96,64},{1,97},{33,1},{65,33},{97,65},{2,98}... | collective-permute-start | bytes 1572872 | tf_op jit(solution)/shard_map/ppermute | solution.py:331
  22.5 10.5 %all-to-all-done.in_ref = bf16[16,2,64,128]{3,2,1,0:T(8,128)(2,1)S(1)} async-done(((bf16[16,2,64,128]{3,2,1,0:T(8,128)(2,1)}), bf16[16,2,64,128]{3,2,1,0:T(8,128)(2,1)S(1)}, u32[]{:S(2)}, u32[]{:S(2)}) %all-to-all-start) | async-done | bytes 524320 | tf_op jit(solution)/shard_map/all_to_all | solution.py:343
  33.2 0.7 copy-done.1
  33.9 9.4 %convolve.1 = bf16[8,2,64,128]{3,2,1,0:T(8,128)(2,1)} custom-call(bf16[16,2,64,128]{3,2,1,0:T(8,128)(2,1)} %copy-done.1, f32[1,512]{1,0:T(1,128)} %bitcast.7, bf16[4,2,256,512]{3,2,1,0:T(8,128)(2,1)} %constant.18.clone.fwd_hbm, bf16[4,2,512,256]{3,2,1,0:T(8,128)(2,1)} %constant.19.clone.back_hbm), custom_call_target="tpu_custom_call" | custom-call | flops 10737418240 | tf_op jit(solution)/shard_map/convolve/pallas_call | solution.py:269
  43.3 7.3 %all-to-all-start.1 = ((bf16[8,2,64,128]{3,2,1,0:T(8,128)(2,1)}), bf16[8,2,64,128]{3,2,1,0:T(8,128)(2,1)S(1)}, u32[]{:S(2)}, u32[]{:S(2)}) async-start(bf16[8,2,64,128]{3,2,1,0:T(8,128)(2,1)} %convolve.1), calls=%async_computation.1 | async-start | bytes 524288 | tf_op jit(solution)/shard_map/all_to_all | solution.py:364
  50.6 3.0 %collective-permute-start.5 = (bf16[2,256,512]{2,1,0:T(8,128)(2,1)S(1)}, bf16[2,256,512]{2,1,0:T(8,128)(2,1)S(1)}, u32[]{:S(2)}, u32[]{:S(2)}) collective-permute-start(bf16[2,256,512]{2,1,0:T(8,128)(2,1)S(1)} %pad_maximum_fusion.refs_4_), channel_id=1, source_target_pairs={{0,64},{32,96},{64,0},{96,32},{1,65},{33,97},{65,1},{97,33},{2,66}... | collective-permute-start | bytes 1572872 | tf_op jit(solution)/shard_map/ppermute | solution.py:331
  53.6 15.7 %all-to-all-done.1.in_ref = bf16[8,2,64,128]{3,2,1,0:T(8,128)(2,1)S(1)} async-done(((bf16[8,2,64,128]{3,2,1,0:T(8,128)(2,1)}), bf16[8,2,64,128]{3,2,1,0:T(8,128)(2,1)S(1)}, u32[]{:S(2)}, u32[]{:S(2)}) %all-to-all-start.1) | async-done | bytes 262176 | tf_op jit(solution)/shard_map/all_to_all | solution.py:364
  69.7 2.8 %collective-permute-start.10 = (bf16[2,256,256]{2,1,0:T(8,128)(2,1)S(1)}, bf16[2,256,256]{2,1,0:T(8,128)(2,1)S(1)}, u32[]{:S(2)}, u32[]{:S(2)}) collective-permute-start(bf16[2,256,256]{2,1,0:T(8,128)(2,1)S(1)} %gate.1.refs_0_), channel_id=1, source_target_pairs={{0,8},{4,12},{8,0},{12,4},{1,9},{5,13},{9,1},{13,5},{2,10},{6,14},... | collective-permute-start | bytes 786440 | tf_op jit(solution)/shard_map/ppermute | solution.py:331
  72.9 2.4 %collective-permute-start.9 = (bf16[2,256,256]{2,1,0:T(8,128)(2,1)S(1)}, bf16[2,256,256]{2,1,0:T(8,128)(2,1)S(1)}, u32[]{:S(2)}, u32[]{:S(2)}) collective-permute-start(bf16[2,256,256]{2,1,0:T(8,128)(2,1)S(1)} %gate.1.refs_0_), channel_id=1, source_target_pairs={{0,12},{4,0},{8,4},{12,8},{1,13},{5,1},{9,5},{13,9},{2,14},{6,2},{... | collective-permute-start | bytes 786440 | tf_op jit(solution)/shard_map/ppermute | solution.py:331
  75.2 3.3 %collective-permute-done.10.refs_2_ = bf16[2,256,256]{2,1,0:T(8,128)(2,1)S(1)} collective-permute-done((bf16[2,256,256]{2,1,0:T(8,128)(2,1)S(1)}, bf16[2,256,256]{2,1,0:T(8,128)(2,1)S(1)}, u32[]{:S(2)}, u32[]{:S(2)}) %collective-permute-start.10) | collective-permute-done | bytes 262176 | tf_op jit(solution)/shard_map/ppermute | solution.py:331
  78.5 6.7 %collective-permute-done.11.refs_3_ = bf16[2,256,256]{2,1,0:T(8,128)(2,1)S(1)} collective-permute-done((bf16[2,256,256]{2,1,0:T(8,128)(2,1)S(1)}, bf16[2,256,256]{2,1,0:T(8,128)(2,1)S(1)}, u32[]{:S(2)}, u32[]{:S(2)}) %collective-permute-start.11) | collective-permute-done | bytes 262176 | tf_op jit(solution)/shard_map/ppermute | solution.py:331
  85.1 1.5 %collective-permute-done.8.g0 = bf16[2,256,256]{2,1,0:T(8,128)(2,1)S(1)} collective-permute-done((bf16[2,256,256]{2,1,0:T(8,128)(2,1)S(1)}, bf16[2,256,256]{2,1,0:T(8,128)(2,1)S(1)}, u32[]{:S(2)}, u32[]{:S(2)}) %collective-permute-start.8) | collective-permute-done | bytes 262176 | tf_op jit(solution)/shard_map/ppermute | solution.py:369
  86.7 0.9 collective-permute-start.15
  87.5 0.6 collective-permute-start.16
  88.1 2.4 %collective-permute-start.12 = (bf16[2,256,256]{2,1,0:T(8,128)(2,1)S(1)}, bf16[2,256,256]{2,1,0:T(8,128)(2,1)S(1)}, u32[]{:S(2)}, u32[]{:S(2)}) collective-permute-start(bf16[2,256,256]{2,1,0:T(8,128)(2,1)S(1)} %collective-permute-done.8.g0), channel_id=1, source_target_pairs={{0,12},{4,0},{8,4},{12,8},{1,13},{5,1},{9,5},{13,9},{2,14},{6,2},{... | collective-permute-start | bytes 786440 | tf_op jit(solution)/shard_map/ppermute | solution.py:331
  90.5 0.6 collective-permute-start.14
  91.1 8.6 %collective-permute-done.15.refs_9_ = bf16[2,256,512]{2,1,0:T(8,128)(2,1)S(1)} collective-permute-done((bf16[2,256,512]{2,1,0:T(8,128)(2,1)S(1)}, bf16[2,256,512]{2,1,0:T(8,128)(2,1)S(1)}, u32[]{:S(2)}, u32[]{:S(2)}) %collective-permute-start.15) | collective-permute-done | bytes 524320 | tf_op jit(solution)/shard_map/ppermute | solution.py:331
  99.7 1.7 %collective-permute-done.16.refs_11_ = bf16[2,256,512]{2,1,0:T(8,128)(2,1)S(1)} collective-permute-done((bf16[2,256,512]{2,1,0:T(8,128)(2,1)S(1)}, bf16[2,256,512]{2,1,0:T(8,128)(2,1)S(1)}, u32[]{:S(2)}, u32[]{:S(2)}) %collective-permute-start.16) | collective-permute-done | bytes 524320 | tf_op jit(solution)/shard_map/ppermute | solution.py:331
  101.4 2.8 %project_first.1 = (f32[2,256,512]{2,1,0:T(8,128)S(1)}, f32[2,256,512]{2,1,0:T(8,128)S(1)}, bf16[1024,512]{1,0:T(8,128)(2,1)S(1)}, bf16[1024,512]{1,0:T(8,128)(2,1)S(1)}) custom-call(bf16[2,256,256]{2,1,0:T(8,128)(2,1)S(1)} %gate.1.refs_0_, bf16[2,256,256]{2,1,0:T(8,128)(2,1)S(1)} %collective-permute-done.9.refs_1_, ...), custom_call_target="tpu_custom_call" | custom-call | flops 5368709120 | tf_op jit(solution)/shard_map/project_first/pallas_call | solution.py:304
  104.2 1.0 collective-permute-done.14.g3
  105.2 0.7 project_rest.3
  105.9 0.9 collective-permute-start.18
  106.8 0.7 project_rest.2
  107.7 0.7 collective-permute-done.18
  108.6 1.0 collective-permute-done.17
  109.6 6.4 %collective-permute-done.19 = bf16[256,512]{1,0:T(8,128)(2,1)S(1)} collective-permute-done((bf16[256,512]{1,0:T(8,128)(2,1)S(1)}, bf16[256,512]{1,0:T(8,128)(2,1)S(1)}, u32[]{:S(2)}, u32[]{:S(2)}) %collective-permute-start.19) | collective-permute-done | bytes 262176 | tf_op jit(solution)/shard_map/ppermute | solution.py:379
  116.1 0.8 add_convert_fusion
  (28 shorter events, 2.0 us)
Async XLA Ops:
  0.0 18.0 %collective-permute-start.1 = (bf16[512,512]{1,0:T(8,128)(2,1)}, bf16[512,512]{1,0:T(8,128)(2,1)S(1)}, u32[]{:S(2)}, u32[]{:S(2)}) collective-permute-start(bf16[512,512]{1,0:T(8,128)(2,1)} %param.13), channel_id=1, source_target_pairs={{0,0},{1,16},{2,2},{3,18},{16,1},{17,17},{18,3},{19,19},{4,4},{5,2... | collective-permute-start | bytes 1572872 | tf_op jit(solution)/shard_map/ppermute | solution.py:354
  7.6 10.7 %copy-start = (bf16[256,512]{1,0:T(8,128)(2,1)S(1)}, bf16[256,512]{1,0:T(8,128)(2,1)}, u32[]{:S(2)}) copy-start(bf16[256,512]{1,0:T(8,128)(2,1)} %own_ref.1) | copy-start | bytes 786436
  7.6 25.5 %all-to-all-start = ((bf16[16,2,64,128]{3,2,1,0:T(8,128)(2,1)}), bf16[16,2,64,128]{3,2,1,0:T(8,128)(2,1)S(1)}, u32[]{:S(2)}, u32[]{:S(2)}) async-start(bf16[16,2,64,128]{3,2,1,0:T(8,128)(2,1)} %bitcast.5), calls=%async_computation | async-start | bytes 1048576 | tf_op jit(solution)/shard_map/all_to_all | solution.py:343
  18.1 1.6 %collective-permute-start.2 = (bf16[256,512]{1,0:T(8,128)(2,1)S(1)}, bf16[256,512]{1,0:T(8,128)(2,1)S(1)}, u32[]{:S(2)}, u32[]{:S(2)}) collective-permute-start(bf16[256,512]{1,0:T(8,128)(2,1)S(1)} %get-tuple-element.72), channel_id=1, source_target_pairs={{0,16},{16,0},{1,17},{17,1},{2,18},{18,2},{3,19},{19,3},{4,20},{20... | collective-permute-start | bytes 786440 | tf_op jit(solution)/shard_map/ppermute | solution.py:331
  18.3 4.2 %collective-permute-start = (bf16[256,256]{1,0:T(8,128)(2,1)S(1)}, bf16[256,256]{1,0:T(8,128)(2,1)S(1)}, u32[]{:S(2)}, u32[]{:S(2)}) collective-permute-start(bf16[256,256]{1,0:T(8,128)(2,1)S(1)} %constant_dynamic-slice_fusion.1), channel_id=1, source_target_pairs={{0,16},{16,0},{1,17},{17,1},{2,18},{18,2},{3,19},{19,3},{4,20},{20... | collective-permute-start | bytes 393224 | tf_op jit(solution)/shard_map/ppermute | solution.py:331
  19.8 23.5 %collective-permute-start.3 = (bf16[2,256,512]{2,1,0:T(8,128)(2,1)S(1)}, bf16[2,256,512]{2,1,0:T(8,128)(2,1)S(1)}, u32[]{:S(2)}, u32[]{:S(2)}) collective-permute-start(bf16[2,256,512]{2,1,0:T(8,128)(2,1)S(1)} %pad_maximum_fusion.refs_4_), channel_id=1, source_target_pairs={{0,32},{32,64},{64,96},{96,0},{1,33},{33,65},{65,97},{97,1},{2,34}... | collective-permute-start | bytes 1572872 | tf_op jit(solution)/shard_map/ppermute | solution.py:331
  21.2 22.1 %collective-permute-start.4 = (bf16[2,256,512]{2,1,0:T(8,128)(2,1)S(1)}, bf16[2,256,512]{2,1,0:T(8,128)(2,1)S(1)}, u32[]{:S(2)}, u32[]{:S(2)}) collective-permute-start(bf16[2,256,512]{2,1,0:T(8,128)(2,1)S(1)} %pad_maximum_fusion.refs_4_), channel_id=1, source_target_pairs={{0,96},{32,0},{64,32},{96,64},{1,97},{33,1},{65,33},{97,65},{2,98}... | collective-permute-start | bytes 1572872 | tf_op jit(solution)/shard_map/ppermute | solution.py:331
  33.1 0.8 copy-start.1
  33.1 20.5 %collective-permute-start.6 = (bf16[2,256,512]{2,1,0:T(8,128)(2,1)S(1)}, bf16[2,256,512]{2,1,0:T(8,128)(2,1)S(1)}, u32[]{:S(2)}, u32[]{:S(2)}) collective-permute-start(bf16[2,256,512]{2,1,0:T(8,128)(2,1)S(1)} %pad_maximum_fusion.refs_4_), channel_id=1, source_target_pairs={{0,128},{128,0},{1,129},{129,1},{2,130},{130,2},{3,131},{131,3},{4... | collective-permute-start | bytes 1572872 | tf_op jit(solution)/shard_map/ppermute | solution.py:331
  43.3 26.1 %all-to-all-start.1 = ((bf16[8,2,64,128]{3,2,1,0:T(8,128)(2,1)}), bf16[8,2,64,128]{3,2,1,0:T(8,128)(2,1)S(1)}, u32[]{:S(2)}, u32[]{:S(2)}) async-start(bf16[8,2,64,128]{3,2,1,0:T(8,128)(2,1)} %convolve.1), calls=%async_computation.1 | async-start | bytes 524288 | tf_op jit(solution)/shard_map/all_to_all | solution.py:364
  50.6 22.3 %collective-permute-start.5 = (bf16[2,256,512]{2,1,0:T(8,128)(2,1)S(1)}, bf16[2,256,512]{2,1,0:T(8,128)(2,1)S(1)}, u32[]{:S(2)}, u32[]{:S(2)}) collective-permute-start(bf16[2,256,512]{2,1,0:T(8,128)(2,1)S(1)} %pad_maximum_fusion.refs_4_), channel_id=1, source_target_pairs={{0,64},{32,96},{64,0},{96,32},{1,65},{33,97},{65,1},{97,33},{2,66}... | collective-permute-start | bytes 1572872 | tf_op jit(solution)/shard_map/ppermute | solution.py:331
  53.5 33.1 %collective-permute-start.7 = (bf16[2,256,512]{2,1,0:T(8,128)(2,1)S(1)}, bf16[2,256,512]{2,1,0:T(8,128)(2,1)}, u32[]{:S(2)}, u32[]{:S(2)}) collective-permute-start(bf16[2,256,512]{2,1,0:T(8,128)(2,1)S(1)} %collective-permute-done.6.refs_8_), channel_id=1, source_target_pairs={{0,64},{32,96},{64,0},{96,32},{1,65},{33,97},{65,1},{97,33},{2,66}... | collective-permute-start | bytes 1572872 | tf_op jit(solution)/shard_map/ppermute | solution.py:331
  69.7 8.8 %collective-permute-start.10 = (bf16[2,256,256]{2,1,0:T(8,128)(2,1)S(1)}, bf16[2,256,256]{2,1,0:T(8,128)(2,1)S(1)}, u32[]{:S(2)}, u32[]{:S(2)}) collective-permute-start(bf16[2,256,256]{2,1,0:T(8,128)(2,1)S(1)} %gate.1.refs_0_), channel_id=1, source_target_pairs={{0,8},{4,12},{8,0},{12,4},{1,9},{5,13},{9,1},{13,5},{2,10},{6,14},... | collective-permute-start | bytes 786440 | tf_op jit(solution)/shard_map/ppermute | solution.py:331
  72.5 12.6 %collective-permute-start.11 = (bf16[2,256,256]{2,1,0:T(8,128)(2,1)S(1)}, bf16[2,256,256]{2,1,0:T(8,128)(2,1)S(1)}, u32[]{:S(2)}, u32[]{:S(2)}) collective-permute-start(bf16[2,256,256]{2,1,0:T(8,128)(2,1)S(1)} %gate.1.refs_0_), channel_id=1, source_target_pairs={{0,4},{4,8},{8,12},{12,0},{1,5},{5,9},{9,13},{13,1},{2,6},{6,10},{... | collective-permute-start | bytes 786440 | tf_op jit(solution)/shard_map/ppermute | solution.py:331
  72.8 13.8 %collective-permute-start.8 = (bf16[2,256,256]{2,1,0:T(8,128)(2,1)S(1)}, bf16[2,256,256]{2,1,0:T(8,128)(2,1)S(1)}, u32[]{:S(2)}, u32[]{:S(2)}) collective-permute-start(bf16[2,256,256]{2,1,0:T(8,128)(2,1)S(1)} %gate.1.refs_0_), channel_id=1, source_target_pairs={{0,2},{1,3},{2,0},{3,1},{4,6},{5,7},{6,4},{7,5},{8,10},{9,11},{10,... | collective-permute-start | bytes 786440 | tf_op jit(solution)/shard_map/ppermute | solution.py:369
  72.9 13.8 %collective-permute-start.9 = (bf16[2,256,256]{2,1,0:T(8,128)(2,1)S(1)}, bf16[2,256,256]{2,1,0:T(8,128)(2,1)S(1)}, u32[]{:S(2)}, u32[]{:S(2)}) collective-permute-start(bf16[2,256,256]{2,1,0:T(8,128)(2,1)S(1)} %gate.1.refs_0_), channel_id=1, source_target_pairs={{0,12},{4,0},{8,4},{12,8},{1,13},{5,1},{9,5},{13,9},{2,14},{6,2},{... | collective-permute-start | bytes 786440 | tf_op jit(solution)/shard_map/ppermute | solution.py:331
  86.7 13.0 %collective-permute-start.15 = (bf16[2,256,512]{2,1,0:T(8,128)(2,1)S(1)}, bf16[2,256,512]{2,1,0:T(8,128)(2,1)S(1)}, u32[]{:S(2)}, u32[]{:S(2)}) collective-permute-start(bf16[2,256,512]{2,1,0:T(8,128)(2,1)S(1)} %collective-permute-done.6.refs_8_), channel_id=1, source_target_pairs={{0,96},{32,0},{64,32},{96,64},{1,97},{33,1},{65,33},{97,65},{2,98}... | collective-permute-start | bytes 1572872 | tf_op jit(solution)/shard_map/ppermute | solution.py:331
  87.5 13.9 %collective-permute-start.16 = (bf16[2,256,512]{2,1,0:T(8,128)(2,1)S(1)}, bf16[2,256,512]{2,1,0:T(8,128)(2,1)S(1)}, u32[]{:S(2)}, u32[]{:S(2)}) collective-permute-start(bf16[2,256,512]{2,1,0:T(8,128)(2,1)S(1)} %collective-permute-done.6.refs_8_), channel_id=1, source_target_pairs={{0,32},{32,64},{64,96},{96,0},{1,33},{33,65},{65,97},{97,1},{2,34}... | collective-permute-start | bytes 1572872 | tf_op jit(solution)/shard_map/ppermute | solution.py:331
  88.1 16.1 %collective-permute-start.12 = (bf16[2,256,256]{2,1,0:T(8,128)(2,1)S(1)}, bf16[2,256,256]{2,1,0:T(8,128)(2,1)S(1)}, u32[]{:S(2)}, u32[]{:S(2)}) collective-permute-start(bf16[2,256,256]{2,1,0:T(8,128)(2,1)S(1)} %collective-permute-done.8.g0), channel_id=1, source_target_pairs={{0,12},{4,0},{8,4},{12,8},{1,13},{5,1},{9,5},{13,9},{2,14},{6,2},{... | collective-permute-start | bytes 786440 | tf_op jit(solution)/shard_map/ppermute | solution.py:331
  90.5 13.7 %collective-permute-start.13 = (bf16[2,256,256]{2,1,0:T(8,128)(2,1)S(1)}, bf16[2,256,256]{2,1,0:T(8,128)(2,1)S(1)}, u32[]{:S(2)}, u32[]{:S(2)}) collective-permute-start(bf16[2,256,256]{2,1,0:T(8,128)(2,1)S(1)} %collective-permute-done.8.g0), channel_id=1, source_target_pairs={{0,8},{4,12},{8,0},{12,4},{1,9},{5,13},{9,1},{13,5},{2,10},{6,14},... | collective-permute-start | bytes 786440 | tf_op jit(solution)/shard_map/ppermute | solution.py:331
  90.5 14.7 %collective-permute-start.14 = (bf16[2,256,256]{2,1,0:T(8,128)(2,1)S(1)}, bf16[2,256,256]{2,1,0:T(8,128)(2,1)S(1)}, u32[]{:S(2)}, u32[]{:S(2)}) collective-permute-start(bf16[2,256,256]{2,1,0:T(8,128)(2,1)S(1)} %collective-permute-done.8.g0), channel_id=1, source_target_pairs={{0,4},{4,8},{8,12},{12,0},{1,5},{5,9},{9,13},{13,1},{2,6},{6,10},{... | collective-permute-start | bytes 786440 | tf_op jit(solution)/shard_map/ppermute | solution.py:331
  105.9 2.5 %collective-permute-start.18 = (f32[256,512]{1,0:T(8,128)S(1)}, f32[256,512]{1,0:T(8,128)S(1)}, u32[]{:S(2)}, u32[]{:S(2)}) collective-permute-start(f32[256,512]{1,0:T(8,128)S(1)} %get-tuple-element.68), channel_id=1, source_target_pairs={{0,16},{16,0},{1,17},{17,1},{2,18},{18,2},{3,19},{19,3},{4,20},{20... | collective-permute-start | bytes 1572872 | tf_op jit(solution)/shard_map/ppermute | solution.py:331
  107.6 2.0 %collective-permute-start.17 = (f32[256,512]{1,0:T(8,128)S(1)}, f32[256,512]{1,0:T(8,128)S(1)}, u32[]{:S(2)}, u32[]{:S(2)}) collective-permute-start(f32[256,512]{1,0:T(8,128)S(1)} %get-tuple-element.64), channel_id=1, source_target_pairs={{0,16},{16,0},{1,17},{17,1},{2,18},{18,2},{3,19},{19,3},{4,20},{20... | collective-permute-start | bytes 1572872 | tf_op jit(solution)/shard_map/ppermute | solution.py:331
  108.5 7.6 %collective-permute-start.19 = (bf16[256,512]{1,0:T(8,128)(2,1)S(1)}, bf16[256,512]{1,0:T(8,128)(2,1)S(1)}, u32[]{:S(2)}, u32[]{:S(2)}) collective-permute-start(bf16[256,512]{1,0:T(8,128)(2,1)S(1)} %add_convert_fusion.1), channel_id=1, source_target_pairs={{0,1},{1,0},{2,3},{3,2},{4,5},{5,4},{6,7},{7,6},{8,9},{9,8},{10,11... | collective-permute-start | bytes 786440 | tf_op jit(solution)/shard_map/ppermute | solution.py:379

commit v6 on v5

--- a/solution.py
+++ b/solution.py
@@ -367,7 +367,7 @@
 
     mine = gate(conv, query, partner)
     other = lax.ppermute(mine, "l", [(i, i ^ 2) for i in range(4)])
-    two, two_over, across, other, mine = tie((two, two_over, across, other, around(mine, "x")))
+    two, across, other, mine = tie((two, across, other, around(mine, "x")))
     weights = (weight, down, two, up)
     two = two_over
     other = around(other, "x")

time: 117 us -> 115 us (0.983)
  waiting for transfers between devices: 58.1 us -> 54.7 us
  starting transfers between devices: 40.3 us -> 42.2 us
    ppermute x17, waiting for transfers between devices: 23.8 us -> 15.3 us  [shift(): return lax.ppermute(v, axis, [(i, (i + by) % n) for i in range(n)])]
    ppermute x1, waiting for transfers between devices: 1.51 us -> 6.79 us  [body(): other = lax.ppermute(mine, 'l', [(i, i ^ 2) for i in range(4)])]
  transfers between devices with their start and end apart: 22 -> 22, of which waited for: 12 -> 10; matrix products, arithmetic and copies ran while one was open for 0% -> 0% of each run, Pallas kernels for 14% -> 13%
where the time goes in v6:
time: 115 us; the launch traced here: 114 us
  waiting for transfers between devices  54.7 us (48%)
  starting transfers between devices  42.2 us (37%)
  Pallas kernels  15.6 us (14%)
    ppermute x17, starting transfers between devices, shift(): return lax.ppermute(v, axis, [(i, (i + by) % n) for i in range(n)])  18.3 us
    all_to_all x1, waiting for transfers between devices, body(): lax.all_to_all(conv, ('h', 'y'), split_axis=0, concat_axis=0, tiled=True)  15.8 us
    ppermute x17, waiting for transfers between devices, shift(): return lax.ppermute(v, axis, [(i, (i + by) % n) for i in range(n)])  15.3 us
    all_to_all x1, waiting for transfers between devices, body(): lax.all_to_all(packed.reshape(16, 2, 64, 128), SEQ, split_axis=0, concat_...  10.5 us
    all_to_all x1, starting transfers between devices, body(): lax.all_to_all(packed.reshape(16, 2, 64, 128), SEQ, split_axis=0, concat_...  10.5 us
    pallas_call x1, Pallas kernels, convolve(): pl.pallas_call(conv_kernel, out_shape=jax.ShapeDtypeStruct((8, 2, 64, 128...  9.4 us
    all_to_all x1, starting transfers between devices, body(): lax.all_to_all(conv, ('h', 'y'), split_axis=0, concat_axis=0, tiled=True)  7.27 us
    ppermute x1, waiting for transfers between devices, body(): other = lax.ppermute(mine, 'l', [(i, i ^ 2) for i in range(4)])  6.79 us
  transfers between devices with their start and end apart: 22, of which 10 were waited for; matrix products, arithmetic and copies ran while one was open for 0% of the time, Pallas kernels for 13%

profile of v6, /device:TPU:1, one launch (start us, length us, event | category | flops | bytes accessed | tf_op | source)
XLA Modules:
  0.0 114.4 jit_solution(10441162797261170978)
XLA Ops:
  0.0 4.9 %collective-permute-start.1 = (bf16[512,512]{1,0:T(8,128)(2,1)}, bf16[512,512]{1,0:T(8,128)(2,1)S(1)}, u32[]{:S(2)}, u32[]{:S(2)}) collective-permute-start(bf16[512,512]{1,0:T(8,128)(2,1)} %param.13), channel_id=1, source_target_pairs={{0,0},{1,16},{2,2},{3,18},{16,1},{17,17},{18,3},{19,19},{4,4},{5,2... | collective-permute-start | bytes 1572872 | tf_op jit(solution)/shard_map/ppermute | solution.py:354
  4.9 2.6 %pack.1 = bf16[2,4,2,2,64,128]{5,4,3,2,1,0:T(8,128)(2,1)} custom-call(bf16[256,512]{1,0:T(8,128)(2,1)} %key_hbm.1, bf16[256,512]{1,0:T(8,128)(2,1)} %value_hbm.1, f32[256,512]{1,0:T(8,128)} %taps_hbm.1), custom_call_target="tpu_custom_call" | custom-call | flops 2147483648 | tf_op jit(solution)/shard_map/pack/pallas_call | solution.py:250
  7.6 10.5 %all-to-all-start = ((bf16[16,2,64,128]{3,2,1,0:T(8,128)(2,1)}), bf16[16,2,64,128]{3,2,1,0:T(8,128)(2,1)S(1)}, u32[]{:S(2)}, u32[]{:S(2)}) async-start(bf16[16,2,64,128]{3,2,1,0:T(8,128)(2,1)} %bitcast.5), calls=%async_computation | async-start | bytes 1048576 | tf_op jit(solution)/shard_map/all_to_all | solution.py:343
  18.8 0.9 collective-permute-done.2
  19.8 1.5 %collective-permute-start.3 = (bf16[2,256,512]{2,1,0:T(8,128)(2,1)S(1)}, bf16[2,256,512]{2,1,0:T(8,128)(2,1)S(1)}, u32[]{:S(2)}, u32[]{:S(2)}) collective-permute-start(bf16[2,256,512]{2,1,0:T(8,128)(2,1)S(1)} %pad_maximum_fusion.refs_4_), channel_id=1, source_target_pairs={{0,32},{32,64},{64,96},{96,0},{1,33},{33,65},{65,97},{97,1},{2,34}... | collective-permute-start | bytes 1572872 | tf_op jit(solution)/shard_map/ppermute | solution.py:331
  21.2 1.3 %collective-permute-start.4 = (bf16[2,256,512]{2,1,0:T(8,128)(2,1)S(1)}, bf16[2,256,512]{2,1,0:T(8,128)(2,1)S(1)}, u32[]{:S(2)}, u32[]{:S(2)}) collective-permute-start(bf16[2,256,512]{2,1,0:T(8,128)(2,1)S(1)} %pad_maximum_fusion.refs_4_), channel_id=1, source_target_pairs={{0,96},{32,0},{64,32},{96,64},{1,97},{33,1},{65,33},{97,65},{2,98}... | collective-permute-start | bytes 1572872 | tf_op jit(solution)/shard_map/ppermute | solution.py:331
  22.5 10.5 %all-to-all-done.in_ref = bf16[16,2,64,128]{3,2,1,0:T(8,128)(2,1)S(1)} async-done(((bf16[16,2,64,128]{3,2,1,0:T(8,128)(2,1)}), bf16[16,2,64,128]{3,2,1,0:T(8,128)(2,1)S(1)}, u32[]{:S(2)}, u32[]{:S(2)}) %all-to-all-start) | async-done | bytes 524320 | tf_op jit(solution)/shard_map/all_to_all | solution.py:343
  33.2 0.7 copy-done.1
  33.9 9.4 %convolve.1 = bf16[8,2,64,128]{3,2,1,0:T(8,128)(2,1)} custom-call(bf16[16,2,64,128]{3,2,1,0:T(8,128)(2,1)} %copy-done.1, f32[1,512]{1,0:T(1,128)} %bitcast.7, bf16[4,2,256,512]{3,2,1,0:T(8,128)(2,1)} %constant.18.clone.fwd_hbm, bf16[4,2,512,256]{3,2,1,0:T(8,128)(2,1)} %constant.19.clone.back_hbm), custom_call_target="tpu_custom_call" | custom-call | flops 10737418240 | tf_op jit(solution)/shard_map/convolve/pallas_call | solution.py:269
  43.3 7.3 %all-to-all-start.1 = ((bf16[8,2,64,128]{3,2,1,0:T(8,128)(2,1)}), bf16[8,2,64,128]{3,2,1,0:T(8,128)(2,1)S(1)}, u32[]{:S(2)}, u32[]{:S(2)}) async-start(bf16[8,2,64,128]{3,2,1,0:T(8,128)(2,1)} %convolve.1), calls=%async_computation.1 | async-start | bytes 524288 | tf_op jit(solution)/shard_map/all_to_all | solution.py:364
  50.6 3.0 %collective-permute-start.5 = (bf16[2,256,512]{2,1,0:T(8,128)(2,1)S(1)}, bf16[2,256,512]{2,1,0:T(8,128)(2,1)S(1)}, u32[]{:S(2)}, u32[]{:S(2)}) collective-permute-start(bf16[2,256,512]{2,1,0:T(8,128)(2,1)S(1)} %pad_maximum_fusion.refs_4_), channel_id=1, source_target_pairs={{0,64},{32,96},{64,0},{96,32},{1,65},{33,97},{65,1},{97,33},{2,66}... | collective-permute-start | bytes 1572872 | tf_op jit(solution)/shard_map/ppermute | solution.py:331
  53.5 15.8 %all-to-all-done.1.in_ref = bf16[8,2,64,128]{3,2,1,0:T(8,128)(2,1)S(1)} async-done(((bf16[8,2,64,128]{3,2,1,0:T(8,128)(2,1)}), bf16[8,2,64,128]{3,2,1,0:T(8,128)(2,1)S(1)}, u32[]{:S(2)}, u32[]{:S(2)}) %all-to-all-start.1) | async-done | bytes 262176 | tf_op jit(solution)/shard_map/all_to_all | solution.py:364
  69.7 1.3 %collective-permute-start.10 = (bf16[2,256,256]{2,1,0:T(8,128)(2,1)S(1)}, bf16[2,256,256]{2,1,0:T(8,128)(2,1)S(1)}, u32[]{:S(2)}, u32[]{:S(2)}) collective-permute-start(bf16[2,256,256]{2,1,0:T(8,128)(2,1)S(1)} %gate.1.refs_0_), channel_id=1, source_target_pairs={{0,4},{4,8},{8,12},{12,0},{1,5},{5,9},{9,13},{13,1},{2,6},{6,10},{... | collective-permute-start | bytes 786440 | tf_op jit(solution)/shard_map/ppermute | solution.py:331
  71.0 1.6 %collective-permute-start.8 = (bf16[2,256,256]{2,1,0:T(8,128)(2,1)S(1)}, bf16[2,256,256]{2,1,0:T(8,128)(2,1)S(1)}, u32[]{:S(2)}, u32[]{:S(2)}) collective-permute-start(bf16[2,256,256]{2,1,0:T(8,128)(2,1)S(1)} %gate.1.refs_0_), channel_id=1, source_target_pairs={{0,12},{4,0},{8,4},{12,8},{1,13},{5,1},{9,5},{13,9},{2,14},{6,2},{... | collective-permute-start | bytes 786440 | tf_op jit(solution)/shard_map/ppermute | solution.py:331
  72.6 1.4 %collective-permute-start.9 = (bf16[2,256,256]{2,1,0:T(8,128)(2,1)S(1)}, bf16[2,256,256]{2,1,0:T(8,128)(2,1)S(1)}, u32[]{:S(2)}, u32[]{:S(2)}) collective-permute-start(bf16[2,256,256]{2,1,0:T(8,128)(2,1)S(1)} %gate.1.refs_0_), channel_id=1, source_target_pairs={{0,8},{4,12},{8,0},{12,4},{1,9},{5,13},{9,1},{13,5},{2,10},{6,14},... | collective-permute-start | bytes 786440 | tf_op jit(solution)/shard_map/ppermute | solution.py:331
  74.0 1.3 %collective-permute-start.15 = (bf16[2,256,512]{2,1,0:T(8,128)(2,1)S(1)}, bf16[2,256,512]{2,1,0:T(8,128)(2,1)S(1)}, u32[]{:S(2)}, u32[]{:S(2)}) collective-permute-start(bf16[2,256,512]{2,1,0:T(8,128)(2,1)S(1)} %collective-permute-done.6.refs_8_), channel_id=1, source_target_pairs={{0,64},{32,96},{64,0},{96,32},{1,65},{33,97},{65,1},{97,33},{2,66}... | collective-permute-start | bytes 1572872 | tf_op jit(solution)/shard_map/ppermute | solution.py:331
  75.2 2.8 %collective-permute-done.10.refs_3_ = bf16[2,256,256]{2,1,0:T(8,128)(2,1)S(1)} collective-permute-done((bf16[2,256,256]{2,1,0:T(8,128)(2,1)S(1)}, bf16[2,256,256]{2,1,0:T(8,128)(2,1)S(1)}, u32[]{:S(2)}, u32[]{:S(2)}) %collective-permute-start.10) | collective-permute-done | bytes 262176 | tf_op jit(solution)/shard_map/ppermute | solution.py:331
  78.0 6.8 %collective-permute-done.7.g0 = bf16[2,256,256]{2,1,0:T(8,128)(2,1)S(1)} collective-permute-done((bf16[2,256,256]{2,1,0:T(8,128)(2,1)S(1)}, bf16[2,256,256]{2,1,0:T(8,128)(2,1)S(1)}, u32[]{:S(2)}, u32[]{:S(2)}) %collective-permute-start.7) | collective-permute-done | bytes 262176 | tf_op jit(solution)/shard_map/ppermute | solution.py:369
  84.8 1.1 collective-permute-start.14
  86.3 1.5 %collective-permute-start.11 = (bf16[2,256,256]{2,1,0:T(8,128)(2,1)S(1)}, bf16[2,256,256]{2,1,0:T(8,128)(2,1)S(1)}, u32[]{:S(2)}, u32[]{:S(2)}) collective-permute-start(bf16[2,256,256]{2,1,0:T(8,128)(2,1)S(1)} %collective-permute-done.7.g0), channel_id=1, source_target_pairs={{0,12},{4,0},{8,4},{12,8},{1,13},{5,1},{9,5},{13,9},{2,14},{6,2},{... | collective-permute-start | bytes 786440 | tf_op jit(solution)/shard_map/ppermute | solution.py:331
  87.7 1.5 %collective-permute-start.12 = (bf16[2,256,256]{2,1,0:T(8,128)(2,1)S(1)}, bf16[2,256,256]{2,1,0:T(8,128)(2,1)S(1)}, u32[]{:S(2)}, u32[]{:S(2)}) collective-permute-start(bf16[2,256,256]{2,1,0:T(8,128)(2,1)S(1)} %collective-permute-done.7.g0), channel_id=1, source_target_pairs={{0,8},{4,12},{8,0},{12,4},{1,9},{5,13},{9,1},{13,5},{2,10},{6,14},... | collective-permute-start | bytes 786440 | tf_op jit(solution)/shard_map/ppermute | solution.py:331
  89.6 8.1 %collective-permute-done.14.refs_9_ = bf16[2,256,512]{2,1,0:T(8,128)(2,1)S(1)} collective-permute-done((bf16[2,256,512]{2,1,0:T(8,128)(2,1)S(1)}, bf16[2,256,512]{2,1,0:T(8,128)(2,1)S(1)}, u32[]{:S(2)}, u32[]{:S(2)}) %collective-permute-start.14) | collective-permute-done | bytes 524320 | tf_op jit(solution)/shard_map/ppermute | solution.py:331
  97.7 1.3 %collective-permute-done.16.refs_11_ = bf16[2,256,512]{2,1,0:T(8,128)(2,1)S(1)} collective-permute-done((bf16[2,256,512]{2,1,0:T(8,128)(2,1)S(1)}, bf16[2,256,512]{2,1,0:T(8,128)(2,1)S(1)}, u32[]{:S(2)}, u32[]{:S(2)}) %collective-permute-start.16) | collective-permute-done | bytes 524320 | tf_op jit(solution)/shard_map/ppermute | solution.py:331
  99.0 1.9 %project_first.1 = (f32[2,256,512]{2,1,0:T(8,128)S(1)}, f32[2,256,512]{2,1,0:T(8,128)S(1)}, bf16[1024,512]{1,0:T(8,128)(2,1)S(1)}, bf16[1024,512]{1,0:T(8,128)(2,1)S(1)}) custom-call(bf16[2,256,256]{2,1,0:T(8,128)(2,1)S(1)} %gate.1.refs_0_, bf16[2,256,256]{2,1,0:T(8,128)(2,1)S(1)} %collective-permute-done.8.refs_1_, ...), custom_call_target="tpu_custom_call" | custom-call | flops 5368709120 | tf_op jit(solution)/shard_map/project_first/pallas_call | solution.py:304
  100.9 1.4 %collective-permute-done.13.g3 = bf16[2,256,256]{2,1,0:T(8,128)(2,1)S(1)} collective-permute-done((bf16[2,256,256]{2,1,0:T(8,128)(2,1)S(1)}, bf16[2,256,256]{2,1,0:T(8,128)(2,1)S(1)}, u32[]{:S(2)}, u32[]{:S(2)}) %collective-permute-start.13) | collective-permute-done | bytes 262176 | tf_op jit(solution)/shard_map/ppermute | solution.py:331
  102.3 0.7 project_rest.3
  103.0 1.3 %collective-permute-start.18 = (f32[256,512]{1,0:T(8,128)S(1)}, f32[256,512]{1,0:T(8,128)S(1)}, u32[]{:S(2)}, u32[]{:S(2)}) collective-permute-start(f32[256,512]{1,0:T(8,128)S(1)} %get-tuple-element.66), channel_id=1, source_target_pairs={{0,16},{16,0},{1,17},{17,1},{2,18},{18,2},{3,19},{19,3},{4,20},{20... | collective-permute-start | bytes 1572872 | tf_op jit(solution)/shard_map/ppermute | solution.py:331
  104.4 0.7 project_rest.2
  105.2 0.7 collective-permute-done.18
  106.0 1.2 %collective-permute-start.19 = (bf16[256,512]{1,0:T(8,128)(2,1)S(1)}, bf16[256,512]{1,0:T(8,128)(2,1)S(1)}, u32[]{:S(2)}, u32[]{:S(2)}) collective-permute-start(bf16[256,512]{1,0:T(8,128)(2,1)S(1)} %add_convert_fusion.1), channel_id=1, source_target_pairs={{0,1},{1,0},{2,3},{3,2},{4,5},{5,4},{6,7},{7,6},{8,9},{9,8},{10,11... | collective-permute-start | bytes 786440 | tf_op jit(solution)/shard_map/ppermute | solution.py:379
  107.3 6.3 %collective-permute-done.19 = bf16[256,512]{1,0:T(8,128)(2,1)S(1)} collective-permute-done((bf16[256,512]{1,0:T(8,128)(2,1)S(1)}, bf16[256,512]{1,0:T(8,128)(2,1)S(1)}, u32[]{:S(2)}, u32[]{:S(2)}) %collective-permute-start.19) | collective-permute-done | bytes 262176 | tf_op jit(solution)/shard_map/ppermute | solution.py:379
  113.6 0.8 add_convert_fusion
  (28 shorter events, 2.2 us)
Async XLA Ops:
  0.0 18.0 %collective-permute-start.1 = (bf16[512,512]{1,0:T(8,128)(2,1)}, bf16[512,512]{1,0:T(8,128)(2,1)S(1)}, u32[]{:S(2)}, u32[]{:S(2)}) collective-permute-start(bf16[512,512]{1,0:T(8,128)(2,1)} %param.13), channel_id=1, source_target_pairs={{0,0},{1,16},{2,2},{3,18},{16,1},{17,17},{18,3},{19,19},{4,4},{5,2... | collective-permute-start | bytes 1572872 | tf_op jit(solution)/shard_map/ppermute | solution.py:354
  7.6 10.7 %copy-start = (bf16[256,512]{1,0:T(8,128)(2,1)S(1)}, bf16[256,512]{1,0:T(8,128)(2,1)}, u32[]{:S(2)}) copy-start(bf16[256,512]{1,0:T(8,128)(2,1)} %own_ref.1) | copy-start | bytes 786436
  7.6 25.5 %all-to-all-start = ((bf16[16,2,64,128]{3,2,1,0:T(8,128)(2,1)}), bf16[16,2,64,128]{3,2,1,0:T(8,128)(2,1)S(1)}, u32[]{:S(2)}, u32[]{:S(2)}) async-start(bf16[16,2,64,128]{3,2,1,0:T(8,128)(2,1)} %bitcast.5), calls=%async_computation | async-start | bytes 1048576 | tf_op jit(solution)/shard_map/all_to_all | solution.py:343
  18.1 1.6 %collective-permute-start.2 = (bf16[256,512]{1,0:T(8,128)(2,1)S(1)}, bf16[256,512]{1,0:T(8,128)(2,1)S(1)}, u32[]{:S(2)}, u32[]{:S(2)}) collective-permute-start(bf16[256,512]{1,0:T(8,128)(2,1)S(1)} %get-tuple-element.70), channel_id=1, source_target_pairs={{0,16},{16,0},{1,17},{17,1},{2,18},{18,2},{3,19},{19,3},{4,20},{20... | collective-permute-start | bytes 786440 | tf_op jit(solution)/shard_map/ppermute | solution.py:331
  18.3 4.2 %collective-permute-start = (bf16[256,256]{1,0:T(8,128)(2,1)S(1)}, bf16[256,256]{1,0:T(8,128)(2,1)S(1)}, u32[]{:S(2)}, u32[]{:S(2)}) collective-permute-start(bf16[256,256]{1,0:T(8,128)(2,1)S(1)} %constant_dynamic-slice_fusion.1), channel_id=1, source_target_pairs={{0,16},{16,0},{1,17},{17,1},{2,18},{18,2},{3,19},{19,3},{4,20},{20... | collective-permute-start | bytes 393224 | tf_op jit(solution)/shard_map/ppermute | solution.py:331
  19.8 23.5 %collective-permute-start.3 = (bf16[2,256,512]{2,1,0:T(8,128)(2,1)S(1)}, bf16[2,256,512]{2,1,0:T(8,128)(2,1)S(1)}, u32[]{:S(2)}, u32[]{:S(2)}) collective-permute-start(bf16[2,256,512]{2,1,0:T(8,128)(2,1)S(1)} %pad_maximum_fusion.refs_4_), channel_id=1, source_target_pairs={{0,32},{32,64},{64,96},{96,0},{1,33},{33,65},{65,97},{97,1},{2,34}... | collective-permute-start | bytes 1572872 | tf_op jit(solution)/shard_map/ppermute | solution.py:331
  21.2 22.1 %collective-permute-start.4 = (bf16[2,256,512]{2,1,0:T(8,128)(2,1)S(1)}, bf16[2,256,512]{2,1,0:T(8,128)(2,1)S(1)}, u32[]{:S(2)}, u32[]{:S(2)}) collective-permute-start(bf16[2,256,512]{2,1,0:T(8,128)(2,1)S(1)} %pad_maximum_fusion.refs_4_), channel_id=1, source_target_pairs={{0,96},{32,0},{64,32},{96,64},{1,97},{33,1},{65,33},{97,65},{2,98}... | collective-permute-start | bytes 1572872 | tf_op jit(solution)/shard_map/ppermute | solution.py:331
  33.1 0.8 copy-start.1
  33.1 20.5 %collective-permute-start.6 = (bf16[2,256,512]{2,1,0:T(8,128)(2,1)S(1)}, bf16[2,256,512]{2,1,0:T(8,128)(2,1)S(1)}, u32[]{:S(2)}, u32[]{:S(2)}) collective-permute-start(bf16[2,256,512]{2,1,0:T(8,128)(2,1)S(1)} %pad_maximum_fusion.refs_4_), channel_id=1, source_target_pairs={{0,128},{128,0},{1,129},{129,1},{2,130},{130,2},{3,131},{131,3},{4... | collective-permute-start | bytes 1572872 | tf_op jit(solution)/shard_map/ppermute | solution.py:331
  43.3 26.0 %all-to-all-start.1 = ((bf16[8,2,64,128]{3,2,1,0:T(8,128)(2,1)}), bf16[8,2,64,128]{3,2,1,0:T(8,128)(2,1)S(1)}, u32[]{:S(2)}, u32[]{:S(2)}) async-start(bf16[8,2,64,128]{3,2,1,0:T(8,128)(2,1)} %convolve.1), calls=%async_computation.1 | async-start | bytes 524288 | tf_op jit(solution)/shard_map/all_to_all | solution.py:364
  50.6 23.4 %collective-permute-start.5 = (bf16[2,256,512]{2,1,0:T(8,128)(2,1)S(1)}, bf16[2,256,512]{2,1,0:T(8,128)(2,1)S(1)}, u32[]{:S(2)}, u32[]{:S(2)}) collective-permute-start(bf16[2,256,512]{2,1,0:T(8,128)(2,1)S(1)} %pad_maximum_fusion.refs_4_), channel_id=1, source_target_pairs={{0,64},{32,96},{64,0},{96,32},{1,65},{33,97},{65,1},{97,33},{2,66}... | collective-permute-start | bytes 1572872 | tf_op jit(solution)/shard_map/ppermute | solution.py:331
  69.7 8.3 %collective-permute-start.10 = (bf16[2,256,256]{2,1,0:T(8,128)(2,1)S(1)}, bf16[2,256,256]{2,1,0:T(8,128)(2,1)S(1)}, u32[]{:S(2)}, u32[]{:S(2)}) collective-permute-start(bf16[2,256,256]{2,1,0:T(8,128)(2,1)S(1)} %gate.1.refs_0_), channel_id=1, source_target_pairs={{0,4},{4,8},{8,12},{12,0},{1,5},{5,9},{9,13},{13,1},{2,6},{6,10},{... | collective-permute-start | bytes 786440 | tf_op jit(solution)/shard_map/ppermute | solution.py:331
  71.0 13.8 %collective-permute-start.7 = (bf16[2,256,256]{2,1,0:T(8,128)(2,1)S(1)}, bf16[2,256,256]{2,1,0:T(8,128)(2,1)S(1)}, u32[]{:S(2)}, u32[]{:S(2)}) collective-permute-start(bf16[2,256,256]{2,1,0:T(8,128)(2,1)S(1)} %gate.1.refs_0_), channel_id=1, source_target_pairs={{0,2},{1,3},{2,0},{3,1},{4,6},{5,7},{6,4},{7,5},{8,10},{9,11},{10,... | collective-permute-start | bytes 786440 | tf_op jit(solution)/shard_map/ppermute | solution.py:369
  71.0 13.8 %collective-permute-start.8 = (bf16[2,256,256]{2,1,0:T(8,128)(2,1)S(1)}, bf16[2,256,256]{2,1,0:T(8,128)(2,1)S(1)}, u32[]{:S(2)}, u32[]{:S(2)}) collective-permute-start(bf16[2,256,256]{2,1,0:T(8,128)(2,1)S(1)} %gate.1.refs_0_), channel_id=1, source_target_pairs={{0,12},{4,0},{8,4},{12,8},{1,13},{5,1},{9,5},{13,9},{2,14},{6,2},{... | collective-permute-start | bytes 786440 | tf_op jit(solution)/shard_map/ppermute | solution.py:331
  72.6 12.2 %collective-permute-start.9 = (bf16[2,256,256]{2,1,0:T(8,128)(2,1)S(1)}, bf16[2,256,256]{2,1,0:T(8,128)(2,1)S(1)}, u32[]{:S(2)}, u32[]{:S(2)}) collective-permute-start(bf16[2,256,256]{2,1,0:T(8,128)(2,1)S(1)} %gate.1.refs_0_), channel_id=1, source_target_pairs={{0,8},{4,12},{8,0},{12,4},{1,9},{5,13},{9,1},{13,5},{2,10},{6,14},... | collective-permute-start | bytes 786440 | tf_op jit(solution)/shard_map/ppermute | solution.py:331
  74.0 15.3 %collective-permute-start.15 = (bf16[2,256,512]{2,1,0:T(8,128)(2,1)S(1)}, bf16[2,256,512]{2,1,0:T(8,128)(2,1)S(1)}, u32[]{:S(2)}, u32[]{:S(2)}) collective-permute-start(bf16[2,256,512]{2,1,0:T(8,128)(2,1)S(1)} %collective-permute-done.6.refs_8_), channel_id=1, source_target_pairs={{0,64},{32,96},{64,0},{96,32},{1,65},{33,97},{65,1},{97,33},{2,66}... | collective-permute-start | bytes 1572872 | tf_op jit(solution)/shard_map/ppermute | solution.py:331
  84.8 12.9 %collective-permute-start.14 = (bf16[2,256,512]{2,1,0:T(8,128)(2,1)S(1)}, bf16[2,256,512]{2,1,0:T(8,128)(2,1)S(1)}, u32[]{:S(2)}, u32[]{:S(2)}) collective-permute-start(bf16[2,256,512]{2,1,0:T(8,128)(2,1)S(1)} %collective-permute-done.6.refs_8_), channel_id=1, source_target_pairs={{0,96},{32,0},{64,32},{96,64},{1,97},{33,1},{65,33},{97,65},{2,98}... | collective-permute-start | bytes 1572872 | tf_op jit(solution)/shard_map/ppermute | solution.py:331
  85.9 13.1 %collective-permute-start.16 = (bf16[2,256,512]{2,1,0:T(8,128)(2,1)S(1)}, bf16[2,256,512]{2,1,0:T(8,128)(2,1)S(1)}, u32[]{:S(2)}, u32[]{:S(2)}) collective-permute-start(bf16[2,256,512]{2,1,0:T(8,128)(2,1)S(1)} %collective-permute-done.6.refs_8_), channel_id=1, source_target_pairs={{0,32},{32,64},{64,96},{96,0},{1,33},{33,65},{65,97},{97,1},{2,34}... | collective-permute-start | bytes 1572872 | tf_op jit(solution)/shard_map/ppermute | solution.py:331
  86.3 14.6 %collective-permute-start.11 = (bf16[2,256,256]{2,1,0:T(8,128)(2,1)S(1)}, bf16[2,256,256]{2,1,0:T(8,128)(2,1)S(1)}, u32[]{:S(2)}, u32[]{:S(2)}) collective-permute-start(bf16[2,256,256]{2,1,0:T(8,128)(2,1)S(1)} %collective-permute-done.7.g0), channel_id=1, source_target_pairs={{0,12},{4,0},{8,4},{12,8},{1,13},{5,1},{9,5},{13,9},{2,14},{6,2},{... | collective-permute-start | bytes 786440 | tf_op jit(solution)/shard_map/ppermute | solution.py:331
  87.7 13.2 %collective-permute-start.12 = (bf16[2,256,256]{2,1,0:T(8,128)(2,1)S(1)}, bf16[2,256,256]{2,1,0:T(8,128)(2,1)S(1)}, u32[]{:S(2)}, u32[]{:S(2)}) collective-permute-start(bf16[2,256,256]{2,1,0:T(8,128)(2,1)S(1)} %collective-permute-done.7.g0), channel_id=1, source_target_pairs={{0,8},{4,12},{8,0},{12,4},{1,9},{5,13},{9,1},{13,5},{2,10},{6,14},... | collective-permute-start | bytes 786440 | tf_op jit(solution)/shard_map/ppermute | solution.py:331
  89.3 13.0 %collective-permute-start.13 = (bf16[2,256,256]{2,1,0:T(8,128)(2,1)S(1)}, bf16[2,256,256]{2,1,0:T(8,128)(2,1)S(1)}, u32[]{:S(2)}, u32[]{:S(2)}) collective-permute-start(bf16[2,256,256]{2,1,0:T(8,128)(2,1)S(1)} %collective-permute-done.7.g0), channel_id=1, source_target_pairs={{0,4},{4,8},{8,12},{12,0},{1,5},{5,9},{9,13},{13,1},{2,6},{6,10},{... | collective-permute-start | bytes 786440 | tf_op jit(solution)/shard_map/ppermute | solution.py:331
  103.0 2.9 %collective-permute-start.18 = (f32[256,512]{1,0:T(8,128)S(1)}, f32[256,512]{1,0:T(8,128)S(1)}, u32[]{:S(2)}, u32[]{:S(2)}) collective-permute-start(f32[256,512]{1,0:T(8,128)S(1)} %get-tuple-element.66), channel_id=1, source_target_pairs={{0,16},{16,0},{1,17},{17,1},{2,18},{18,2},{3,19},{19,3},{4,20},{20... | collective-permute-start | bytes 1572872 | tf_op jit(solution)/shard_map/ppermute | solution.py:331
  105.1 2.1 %collective-permute-start.17 = (f32[256,512]{1,0:T(8,128)S(1)}, f32[256,512]{1,0:T(8,128)S(1)}, u32[]{:S(2)}, u32[]{:S(2)}) collective-permute-start(f32[256,512]{1,0:T(8,128)S(1)} %get-tuple-element.62), channel_id=1, source_target_pairs={{0,16},{16,0},{1,17},{17,1},{2,18},{18,2},{3,19},{19,3},{4,20},{20... | collective-permute-start | bytes 1572872 | tf_op jit(solution)/shard_map/ppermute | solution.py:331
  106.0 7.6 %collective-permute-start.19 = (bf16[256,512]{1,0:T(8,128)(2,1)S(1)}, bf16[256,512]{1,0:T(8,128)(2,1)S(1)}, u32[]{:S(2)}, u32[]{:S(2)}) collective-permute-start(bf16[256,512]{1,0:T(8,128)(2,1)S(1)} %add_convert_fusion.1), channel_id=1, source_target_pairs={{0,1},{1,0},{2,3},{3,2},{4,5},{5,4},{6,7},{7,6},{8,9},{9,8},{10,11... | collective-permute-start | bytes 786440 | tf_op jit(solution)/shard_map/ppermute | solution.py:379

commit v7 on v6

--- a/solution.py
+++ b/solution.py
@@ -15,8 +15,8 @@
 SEQ = ("h", "y", "k")
 CHAN = ("x", "l")
 N = 1024
-STEPS = 4
-FREQS = 128
+STEPS = 2
+FREQS = 256
 MIB = 1 << 20
 LARGE = 60 * MIB
 
@@ -122,7 +122,8 @@
 
     for step in range(STEPS):
         copies[2 * step].wait()
-        spec[...] = dot(fwd[step, 0], both[...]) + dot(fwd[step, 1], both[...])
+        pair = dot(fwd[step].reshape(4 * FREQS, 512), both[...])
+        spec[...] = pair[: 2 * FREQS] + pair[2 * FREQS :]
         spec[:FREQS, 256:384] += bias
         if step == 0:
             spec[FREQS : FREQS + 1, 256:384] += bias
@@ -165,7 +166,7 @@
                 prod[dst, right] = p1 + sign * jnp.where(position >= 1, q1, q0)
             return carry
 
-        lax.fori_loop(0, FREQS // rows, body, 0, unroll=16)
+        lax.fori_loop(0, FREQS // rows, body, 0, unroll=32)
         whole = prod[...]
         high = whole.astype(bf16)
         low = (whole - high.astype(f32)).astype(bf16)

time: 115 us -> 115 us (level)
  no operation moved by 1% of the time
where the time goes in v7:
time: 115 us; the launch traced here: 114 us
  waiting for transfers between devices  55.4 us (48%)
  starting transfers between devices  42 us (37%)
  Pallas kernels  15.1 us (13%)
    ppermute x17, starting transfers between devices, shift(): return lax.ppermute(v, axis, [(i, (i + by) % n) for i in range(n)])  18.1 us
    all_to_all x1, waiting for transfers between devices, body(): lax.all_to_all(conv, ('h', 'y'), split_axis=0, concat_axis=0, tiled=True)  16.3 us
    ppermute x17, waiting for transfers between devices, shift(): return lax.ppermute(v, axis, [(i, (i + by) % n) for i in range(n)])  15.4 us
    all_to_all x1, waiting for transfers between devices, body(): lax.all_to_all(packed.reshape(16, 2, 64, 128), SEQ, split_axis=0, concat_...  10.5 us
    all_to_all x1, starting transfers between devices, body(): lax.all_to_all(packed.reshape(16, 2, 64, 128), SEQ, split_axis=0, concat_...  10.5 us
    pallas_call x1, Pallas kernels, convolve(): pl.pallas_call(conv_kernel, out_shape=jax.ShapeDtypeStruct((8, 2, 64, 128...  8.93 us
    all_to_all x1, starting transfers between devices, body(): lax.all_to_all(conv, ('h', 'y'), split_axis=0, concat_axis=0, tiled=True)  7.27 us
    ppermute x1, waiting for transfers between devices, body(): other = lax.ppermute(mine, 'l', [(i, i ^ 2) for i in range(4)])  6.81 us
  transfers between devices with their start and end apart: 22, of which 10 were waited for; matrix products, arithmetic and copies ran while one was open for 0% of the time, Pallas kernels for 13%

profile of v7, /device:TPU:1, one launch (start us, length us, event | category | flops | bytes accessed | tf_op | source)
XLA Modules:
  0.0 114.4 jit_solution(2397296313428719342)
XLA Ops:
  0.0 4.9 %collective-permute-start.1 = (bf16[512,512]{1,0:T(8,128)(2,1)}, bf16[512,512]{1,0:T(8,128)(2,1)S(1)}, u32[]{:S(2)}, u32[]{:S(2)}) collective-permute-start(bf16[512,512]{1,0:T(8,128)(2,1)} %param.13), channel_id=1, source_target_pairs={{0,0},{1,16},{2,2},{3,18},{16,1},{17,17},{18,3},{19,19},{4,4},{5,2... | collective-permute-start | bytes 1572872 | tf_op jit(solution)/shard_map/ppermute | solution.py:355
  4.9 2.6 %pack.1 = bf16[2,4,2,2,64,128]{5,4,3,2,1,0:T(8,128)(2,1)} custom-call(bf16[256,512]{1,0:T(8,128)(2,1)} %key_hbm.1, bf16[256,512]{1,0:T(8,128)(2,1)} %value_hbm.1, f32[256,512]{1,0:T(8,128)} %taps_hbm.1), custom_call_target="tpu_custom_call" | custom-call | flops 2147483648 | tf_op jit(solution)/shard_map/pack/pallas_call | solution.py:251
  7.6 10.5 %all-to-all-start = ((bf16[16,2,64,128]{3,2,1,0:T(8,128)(2,1)}), bf16[16,2,64,128]{3,2,1,0:T(8,128)(2,1)S(1)}, u32[]{:S(2)}, u32[]{:S(2)}) async-start(bf16[16,2,64,128]{3,2,1,0:T(8,128)(2,1)} %bitcast.5), calls=%async_computation | async-start | bytes 1048576 | tf_op jit(solution)/shard_map/all_to_all | solution.py:344
  18.8 0.9 collective-permute-done.2
  19.8 1.5 %collective-permute-start.3 = (bf16[2,256,512]{2,1,0:T(8,128)(2,1)S(1)}, bf16[2,256,512]{2,1,0:T(8,128)(2,1)S(1)}, u32[]{:S(2)}, u32[]{:S(2)}) collective-permute-start(bf16[2,256,512]{2,1,0:T(8,128)(2,1)S(1)} %pad_maximum_fusion.refs_4_), channel_id=1, source_target_pairs={{0,32},{32,64},{64,96},{96,0},{1,33},{33,65},{65,97},{97,1},{2,34}... | collective-permute-start | bytes 1572872 | tf_op jit(solution)/shard_map/ppermute | solution.py:332
  21.2 1.3 %collective-permute-start.4 = (bf16[2,256,512]{2,1,0:T(8,128)(2,1)S(1)}, bf16[2,256,512]{2,1,0:T(8,128)(2,1)S(1)}, u32[]{:S(2)}, u32[]{:S(2)}) collective-permute-start(bf16[2,256,512]{2,1,0:T(8,128)(2,1)S(1)} %pad_maximum_fusion.refs_4_), channel_id=1, source_target_pairs={{0,96},{32,0},{64,32},{96,64},{1,97},{33,1},{65,33},{97,65},{2,98}... | collective-permute-start | bytes 1572872 | tf_op jit(solution)/shard_map/ppermute | solution.py:332
  22.5 10.5 %all-to-all-done.in_ref = bf16[16,2,64,128]{3,2,1,0:T(8,128)(2,1)S(1)} async-done(((bf16[16,2,64,128]{3,2,1,0:T(8,128)(2,1)}), bf16[16,2,64,128]{3,2,1,0:T(8,128)(2,1)S(1)}, u32[]{:S(2)}, u32[]{:S(2)}) %all-to-all-start) | async-done | bytes 524320 | tf_op jit(solution)/shard_map/all_to_all | solution.py:344
  33.2 0.7 copy-done.1
  33.9 8.9 %convolve.1 = bf16[8,2,64,128]{3,2,1,0:T(8,128)(2,1)} custom-call(bf16[16,2,64,128]{3,2,1,0:T(8,128)(2,1)} %copy-done.1, f32[1,512]{1,0:T(1,128)} %bitcast.7, bf16[2,2,512,512]{3,2,1,0:T(8,128)(2,1)} %constant.18.clone.fwd_hbm, bf16[2,2,512,512]{3,2,1,0:T(8,128)(2,1)} %constant.19.clone.back_hbm), custom_call_target="tpu_custom_call" | custom-call | flops 10737418240 | tf_op jit(solution)/shard_map/convolve/pallas_call | solution.py:270
  42.8 7.3 %all-to-all-start.1 = ((bf16[8,2,64,128]{3,2,1,0:T(8,128)(2,1)}), bf16[8,2,64,128]{3,2,1,0:T(8,128)(2,1)S(1)}, u32[]{:S(2)}, u32[]{:S(2)}) async-start(bf16[8,2,64,128]{3,2,1,0:T(8,128)(2,1)} %convolve.1), calls=%async_computation.1 | async-start | bytes 524288 | tf_op jit(solution)/shard_map/all_to_all | solution.py:365
  50.1 3.0 %collective-permute-start.5 = (bf16[2,256,512]{2,1,0:T(8,128)(2,1)S(1)}, bf16[2,256,512]{2,1,0:T(8,128)(2,1)S(1)}, u32[]{:S(2)}, u32[]{:S(2)}) collective-permute-start(bf16[2,256,512]{2,1,0:T(8,128)(2,1)S(1)} %pad_maximum_fusion.refs_4_), channel_id=1, source_target_pairs={{0,64},{32,96},{64,0},{96,32},{1,65},{33,97},{65,1},{97,33},{2,66}... | collective-permute-start | bytes 1572872 | tf_op jit(solution)/shard_map/ppermute | solution.py:332
  53.1 16.3 %all-to-all-done.1.in_ref = bf16[8,2,64,128]{3,2,1,0:T(8,128)(2,1)S(1)} async-done(((bf16[8,2,64,128]{3,2,1,0:T(8,128)(2,1)}), bf16[8,2,64,128]{3,2,1,0:T(8,128)(2,1)S(1)}, u32[]{:S(2)}, u32[]{:S(2)}) %all-to-all-start.1) | async-done | bytes 262176 | tf_op jit(solution)/shard_map/all_to_all | solution.py:365
  69.7 1.3 %collective-permute-start.10 = (bf16[2,256,256]{2,1,0:T(8,128)(2,1)S(1)}, bf16[2,256,256]{2,1,0:T(8,128)(2,1)S(1)}, u32[]{:S(2)}, u32[]{:S(2)}) collective-permute-start(bf16[2,256,256]{2,1,0:T(8,128)(2,1)S(1)} %gate.1.refs_0_), channel_id=1, source_target_pairs={{0,4},{4,8},{8,12},{12,0},{1,5},{5,9},{9,13},{13,1},{2,6},{6,10},{... | collective-permute-start | bytes 786440 | tf_op jit(solution)/shard_map/ppermute | solution.py:332
  71.0 1.5 %collective-permute-start.8 = (bf16[2,256,256]{2,1,0:T(8,128)(2,1)S(1)}, bf16[2,256,256]{2,1,0:T(8,128)(2,1)S(1)}, u32[]{:S(2)}, u32[]{:S(2)}) collective-permute-start(bf16[2,256,256]{2,1,0:T(8,128)(2,1)S(1)} %gate.1.refs_0_), channel_id=1, source_target_pairs={{0,12},{4,0},{8,4},{12,8},{1,13},{5,1},{9,5},{13,9},{2,14},{6,2},{... | collective-permute-start | bytes 786440 | tf_op jit(solution)/shard_map/ppermute | solution.py:332
  72.5 1.5 %collective-permute-start.9 = (bf16[2,256,256]{2,1,0:T(8,128)(2,1)S(1)}, bf16[2,256,256]{2,1,0:T(8,128)(2,1)S(1)}, u32[]{:S(2)}, u32[]{:S(2)}) collective-permute-start(bf16[2,256,256]{2,1,0:T(8,128)(2,1)S(1)} %gate.1.refs_0_), channel_id=1, source_target_pairs={{0,8},{4,12},{8,0},{12,4},{1,9},{5,13},{9,1},{13,5},{2,10},{6,14},... | collective-permute-start | bytes 786440 | tf_op jit(solution)/shard_map/ppermute | solution.py:332
  74.0 1.2 %collective-permute-start.15 = (bf16[2,256,512]{2,1,0:T(8,128)(2,1)S(1)}, bf16[2,256,512]{2,1,0:T(8,128)(2,1)S(1)}, u32[]{:S(2)}, u32[]{:S(2)}) collective-permute-start(bf16[2,256,512]{2,1,0:T(8,128)(2,1)S(1)} %collective-permute-done.6.refs_8_), channel_id=1, source_target_pairs={{0,64},{32,96},{64,0},{96,32},{1,65},{33,97},{65,1},{97,33},{2,66}... | collective-permute-start | bytes 1572872 | tf_op jit(solution)/shard_map/ppermute | solution.py:332
  75.2 2.8 %collective-permute-done.10.refs_3_ = bf16[2,256,256]{2,1,0:T(8,128)(2,1)S(1)} collective-permute-done((bf16[2,256,256]{2,1,0:T(8,128)(2,1)S(1)}, bf16[2,256,256]{2,1,0:T(8,128)(2,1)S(1)}, u32[]{:S(2)}, u32[]{:S(2)}) %collective-permute-start.10) | collective-permute-done | bytes 262176 | tf_op jit(solution)/shard_map/ppermute | solution.py:332
  78.0 6.8 %collective-permute-done.7.g0 = bf16[2,256,256]{2,1,0:T(8,128)(2,1)S(1)} collective-permute-done((bf16[2,256,256]{2,1,0:T(8,128)(2,1)S(1)}, bf16[2,256,256]{2,1,0:T(8,128)(2,1)S(1)}, u32[]{:S(2)}, u32[]{:S(2)}) %collective-permute-start.7) | collective-permute-done | bytes 262176 | tf_op jit(solution)/shard_map/ppermute | solution.py:370
  84.9 1.0 collective-permute-start.14
  86.3 1.5 %collective-permute-start.11 = (bf16[2,256,256]{2,1,0:T(8,128)(2,1)S(1)}, bf16[2,256,256]{2,1,0:T(8,128)(2,1)S(1)}, u32[]{:S(2)}, u32[]{:S(2)}) collective-permute-start(bf16[2,256,256]{2,1,0:T(8,128)(2,1)S(1)} %collective-permute-done.7.g0), channel_id=1, source_target_pairs={{0,12},{4,0},{8,4},{12,8},{1,13},{5,1},{9,5},{13,9},{2,14},{6,2},{... | collective-permute-start | bytes 786440 | tf_op jit(solution)/shard_map/ppermute | solution.py:332
  87.8 1.5 %collective-permute-start.12 = (bf16[2,256,256]{2,1,0:T(8,128)(2,1)S(1)}, bf16[2,256,256]{2,1,0:T(8,128)(2,1)S(1)}, u32[]{:S(2)}, u32[]{:S(2)}) collective-permute-start(bf16[2,256,256]{2,1,0:T(8,128)(2,1)S(1)} %collective-permute-done.7.g0), channel_id=1, source_target_pairs={{0,8},{4,12},{8,0},{12,4},{1,9},{5,13},{9,1},{13,5},{2,10},{6,14},... | collective-permute-start | bytes 786440 | tf_op jit(solution)/shard_map/ppermute | solution.py:332
  89.6 8.0 %collective-permute-done.14.refs_9_ = bf16[2,256,512]{2,1,0:T(8,128)(2,1)S(1)} collective-permute-done((bf16[2,256,512]{2,1,0:T(8,128)(2,1)S(1)}, bf16[2,256,512]{2,1,0:T(8,128)(2,1)S(1)}, u32[]{:S(2)}, u32[]{:S(2)}) %collective-permute-start.14) | collective-permute-done | bytes 524320 | tf_op jit(solution)/shard_map/ppermute | solution.py:332
  97.7 1.4 %collective-permute-done.16.refs_11_ = bf16[2,256,512]{2,1,0:T(8,128)(2,1)S(1)} collective-permute-done((bf16[2,256,512]{2,1,0:T(8,128)(2,1)S(1)}, bf16[2,256,512]{2,1,0:T(8,128)(2,1)S(1)}, u32[]{:S(2)}, u32[]{:S(2)}) %collective-permute-start.16) | collective-permute-done | bytes 524320 | tf_op jit(solution)/shard_map/ppermute | solution.py:332
  99.0 1.9 %project_first.1 = (f32[2,256,512]{2,1,0:T(8,128)S(1)}, f32[2,256,512]{2,1,0:T(8,128)S(1)}, bf16[1024,512]{1,0:T(8,128)(2,1)S(1)}, bf16[1024,512]{1,0:T(8,128)(2,1)S(1)}) custom-call(bf16[2,256,256]{2,1,0:T(8,128)(2,1)S(1)} %gate.1.refs_0_, bf16[2,256,256]{2,1,0:T(8,128)(2,1)S(1)} %collective-permute-done.8.refs_1_, ...), custom_call_target="tpu_custom_call" | custom-call | flops 5368709120 | tf_op jit(solution)/shard_map/project_first/pallas_call | solution.py:305
  100.9 1.5 %collective-permute-done.13.g3 = bf16[2,256,256]{2,1,0:T(8,128)(2,1)S(1)} collective-permute-done((bf16[2,256,256]{2,1,0:T(8,128)(2,1)S(1)}, bf16[2,256,256]{2,1,0:T(8,128)(2,1)S(1)}, u32[]{:S(2)}, u32[]{:S(2)}) %collective-permute-start.13) | collective-permute-done | bytes 262176 | tf_op jit(solution)/shard_map/ppermute | solution.py:332
  102.5 0.7 project_rest.3
  103.2 1.2 %collective-permute-start.18 = (f32[256,512]{1,0:T(8,128)S(1)}, f32[256,512]{1,0:T(8,128)S(1)}, u32[]{:S(2)}, u32[]{:S(2)}) collective-permute-start(f32[256,512]{1,0:T(8,128)S(1)} %get-tuple-element.66), channel_id=1, source_target_pairs={{0,16},{16,0},{1,17},{17,1},{2,18},{18,2},{3,19},{19,3},{4,20},{20... | collective-permute-start | bytes 1572872 | tf_op jit(solution)/shard_map/ppermute | solution.py:332
  104.4 0.7 project_rest.2
  105.2 0.7 collective-permute-done.18
  106.1 1.2 %collective-permute-start.19 = (bf16[256,512]{1,0:T(8,128)(2,1)S(1)}, bf16[256,512]{1,0:T(8,128)(2,1)S(1)}, u32[]{:S(2)}, u32[]{:S(2)}) collective-permute-start(bf16[256,512]{1,0:T(8,128)(2,1)S(1)} %add_convert_fusion.1), channel_id=1, source_target_pairs={{0,1},{1,0},{2,3},{3,2},{4,5},{5,4},{6,7},{7,6},{8,9},{9,8},{10,11... | collective-permute-start | bytes 786440 | tf_op jit(solution)/shard_map/ppermute | solution.py:380
  107.4 6.3 %collective-permute-done.19 = bf16[256,512]{1,0:T(8,128)(2,1)S(1)} collective-permute-done((bf16[256,512]{1,0:T(8,128)(2,1)S(1)}, bf16[256,512]{1,0:T(8,128)(2,1)S(1)}, u32[]{:S(2)}, u32[]{:S(2)}) %collective-permute-start.19) | collective-permute-done | bytes 262176 | tf_op jit(solution)/shard_map/ppermute | solution.py:380
  113.7 0.8 add_convert_fusion
  (28 shorter events, 2.3 us)
Async XLA Ops:
  0.0 18.0 %collective-permute-start.1 = (bf16[512,512]{1,0:T(8,128)(2,1)}, bf16[512,512]{1,0:T(8,128)(2,1)S(1)}, u32[]{:S(2)}, u32[]{:S(2)}) collective-permute-start(bf16[512,512]{1,0:T(8,128)(2,1)} %param.13), channel_id=1, source_target_pairs={{0,0},{1,16},{2,2},{3,18},{16,1},{17,17},{18,3},{19,19},{4,4},{5,2... | collective-permute-start | bytes 1572872 | tf_op jit(solution)/shard_map/ppermute | solution.py:355
  7.6 10.7 %copy-start = (bf16[256,512]{1,0:T(8,128)(2,1)S(1)}, bf16[256,512]{1,0:T(8,128)(2,1)}, u32[]{:S(2)}) copy-start(bf16[256,512]{1,0:T(8,128)(2,1)} %own_ref.1) | copy-start | bytes 786436
  7.6 25.5 %all-to-all-start = ((bf16[16,2,64,128]{3,2,1,0:T(8,128)(2,1)}), bf16[16,2,64,128]{3,2,1,0:T(8,128)(2,1)S(1)}, u32[]{:S(2)}, u32[]{:S(2)}) async-start(bf16[16,2,64,128]{3,2,1,0:T(8,128)(2,1)} %bitcast.5), calls=%async_computation | async-start | bytes 1048576 | tf_op jit(solution)/shard_map/all_to_all | solution.py:344
  18.1 1.6 %collective-permute-start.2 = (bf16[256,512]{1,0:T(8,128)(2,1)S(1)}, bf16[256,512]{1,0:T(8,128)(2,1)S(1)}, u32[]{:S(2)}, u32[]{:S(2)}) collective-permute-start(bf16[256,512]{1,0:T(8,128)(2,1)S(1)} %get-tuple-element.70), channel_id=1, source_target_pairs={{0,16},{16,0},{1,17},{17,1},{2,18},{18,2},{3,19},{19,3},{4,20},{20... | collective-permute-start | bytes 786440 | tf_op jit(solution)/shard_map/ppermute | solution.py:332
  18.3 4.2 %collective-permute-start = (bf16[256,256]{1,0:T(8,128)(2,1)S(1)}, bf16[256,256]{1,0:T(8,128)(2,1)S(1)}, u32[]{:S(2)}, u32[]{:S(2)}) collective-permute-start(bf16[256,256]{1,0:T(8,128)(2,1)S(1)} %constant_dynamic-slice_fusion.1), channel_id=1, source_target_pairs={{0,16},{16,0},{1,17},{17,1},{2,18},{18,2},{3,19},{19,3},{4,20},{20... | collective-permute-start | bytes 393224 | tf_op jit(solution)/shard_map/ppermute | solution.py:332
  19.8 23.0 %collective-permute-start.3 = (bf16[2,256,512]{2,1,0:T(8,128)(2,1)S(1)}, bf16[2,256,512]{2,1,0:T(8,128)(2,1)S(1)}, u32[]{:S(2)}, u32[]{:S(2)}) collective-permute-start(bf16[2,256,512]{2,1,0:T(8,128)(2,1)S(1)} %pad_maximum_fusion.refs_4_), channel_id=1, source_target_pairs={{0,32},{32,64},{64,96},{96,0},{1,33},{33,65},{65,97},{97,1},{2,34}... | collective-permute-start | bytes 1572872 | tf_op jit(solution)/shard_map/ppermute | solution.py:332
  21.2 21.6 %collective-permute-start.4 = (bf16[2,256,512]{2,1,0:T(8,128)(2,1)S(1)}, bf16[2,256,512]{2,1,0:T(8,128)(2,1)S(1)}, u32[]{:S(2)}, u32[]{:S(2)}) collective-permute-start(bf16[2,256,512]{2,1,0:T(8,128)(2,1)S(1)} %pad_maximum_fusion.refs_4_), channel_id=1, source_target_pairs={{0,96},{32,0},{64,32},{96,64},{1,97},{33,1},{65,33},{97,65},{2,98}... | collective-permute-start | bytes 1572872 | tf_op jit(solution)/shard_map/ppermute | solution.py:332
  33.1 0.8 copy-start.1
  33.1 20.0 %collective-permute-start.6 = (bf16[2,256,512]{2,1,0:T(8,128)(2,1)S(1)}, bf16[2,256,512]{2,1,0:T(8,128)(2,1)S(1)}, u32[]{:S(2)}, u32[]{:S(2)}) collective-permute-start(bf16[2,256,512]{2,1,0:T(8,128)(2,1)S(1)} %pad_maximum_fusion.refs_4_), channel_id=1, source_target_pairs={{0,128},{128,0},{1,129},{129,1},{2,130},{130,2},{3,131},{131,3},{4... | collective-permute-start | bytes 1572872 | tf_op jit(solution)/shard_map/ppermute | solution.py:332
  42.8 26.5 %all-to-all-start.1 = ((bf16[8,2,64,128]{3,2,1,0:T(8,128)(2,1)}), bf16[8,2,64,128]{3,2,1,0:T(8,128)(2,1)S(1)}, u32[]{:S(2)}, u32[]{:S(2)}) async-start(bf16[8,2,64,128]{3,2,1,0:T(8,128)(2,1)} %convolve.1), calls=%async_computation.1 | async-start | bytes 524288 | tf_op jit(solution)/shard_map/all_to_all | solution.py:365
  50.1 23.9 %collective-permute-start.5 = (bf16[2,256,512]{2,1,0:T(8,128)(2,1)S(1)}, bf16[2,256,512]{2,1,0:T(8,128)(2,1)S(1)}, u32[]{:S(2)}, u32[]{:S(2)}) collective-permute-start(bf16[2,256,512]{2,1,0:T(8,128)(2,1)S(1)} %pad_maximum_fusion.refs_4_), channel_id=1, source_target_pairs={{0,64},{32,96},{64,0},{96,32},{1,65},{33,97},{65,1},{97,33},{2,66}... | collective-permute-start | bytes 1572872 | tf_op jit(solution)/shard_map/ppermute | solution.py:332
  69.7 8.3 %collective-permute-start.10 = (bf16[2,256,256]{2,1,0:T(8,128)(2,1)S(1)}, bf16[2,256,256]{2,1,0:T(8,128)(2,1)S(1)}, u32[]{:S(2)}, u32[]{:S(2)}) collective-permute-start(bf16[2,256,256]{2,1,0:T(8,128)(2,1)S(1)} %gate.1.refs_0_), channel_id=1, source_target_pairs={{0,4},{4,8},{8,12},{12,0},{1,5},{5,9},{9,13},{13,1},{2,6},{6,10},{... | collective-permute-start | bytes 786440 | tf_op jit(solution)/shard_map/ppermute | solution.py:332
  71.0 13.9 %collective-permute-start.7 = (bf16[2,256,256]{2,1,0:T(8,128)(2,1)S(1)}, bf16[2,256,256]{2,1,0:T(8,128)(2,1)S(1)}, u32[]{:S(2)}, u32[]{:S(2)}) collective-permute-start(bf16[2,256,256]{2,1,0:T(8,128)(2,1)S(1)} %gate.1.refs_0_), channel_id=1, source_target_pairs={{0,2},{1,3},{2,0},{3,1},{4,6},{5,7},{6,4},{7,5},{8,10},{9,11},{10,... | collective-permute-start | bytes 786440 | tf_op jit(solution)/shard_map/ppermute | solution.py:370
  71.0 13.9 %collective-permute-start.8 = (bf16[2,256,256]{2,1,0:T(8,128)(2,1)S(1)}, bf16[2,256,256]{2,1,0:T(8,128)(2,1)S(1)}, u32[]{:S(2)}, u32[]{:S(2)}) collective-permute-start(bf16[2,256,256]{2,1,0:T(8,128)(2,1)S(1)} %gate.1.refs_0_), channel_id=1, source_target_pairs={{0,12},{4,0},{8,4},{12,8},{1,13},{5,1},{9,5},{13,9},{2,14},{6,2},{... | collective-permute-start | bytes 786440 | tf_op jit(solution)/shard_map/ppermute | solution.py:332
  72.5 12.4 %collective-permute-start.9 = (bf16[2,256,256]{2,1,0:T(8,128)(2,1)S(1)}, bf16[2,256,256]{2,1,0:T(8,128)(2,1)S(1)}, u32[]{:S(2)}, u32[]{:S(2)}) collective-permute-start(bf16[2,256,256]{2,1,0:T(8,128)(2,1)S(1)} %gate.1.refs_0_), channel_id=1, source_target_pairs={{0,8},{4,12},{8,0},{12,4},{1,9},{5,13},{9,1},{13,5},{2,10},{6,14},... | collective-permute-start | bytes 786440 | tf_op jit(solution)/shard_map/ppermute | solution.py:332
  74.0 15.3 %collective-permute-start.15 = (bf16[2,256,512]{2,1,0:T(8,128)(2,1)S(1)}, bf16[2,256,512]{2,1,0:T(8,128)(2,1)S(1)}, u32[]{:S(2)}, u32[]{:S(2)}) collective-permute-start(bf16[2,256,512]{2,1,0:T(8,128)(2,1)S(1)} %collective-permute-done.6.refs_8_), channel_id=1, source_target_pairs={{0,64},{32,96},{64,0},{96,32},{1,65},{33,97},{65,1},{97,33},{2,66}... | collective-permute-start | bytes 1572872 | tf_op jit(solution)/shard_map/ppermute | solution.py:332
  84.9 12.8 %collective-permute-start.14 = (bf16[2,256,512]{2,1,0:T(8,128)(2,1)S(1)}, bf16[2,256,512]{2,1,0:T(8,128)(2,1)S(1)}, u32[]{:S(2)}, u32[]{:S(2)}) collective-permute-start(bf16[2,256,512]{2,1,0:T(8,128)(2,1)S(1)} %collective-permute-done.6.refs_8_), channel_id=1, source_target_pairs={{0,96},{32,0},{64,32},{96,64},{1,97},{33,1},{65,33},{97,65},{2,98}... | collective-permute-start | bytes 1572872 | tf_op jit(solution)/shard_map/ppermute | solution.py:332
  85.9 13.1 %collective-permute-start.16 = (bf16[2,256,512]{2,1,0:T(8,128)(2,1)S(1)}, bf16[2,256,512]{2,1,0:T(8,128)(2,1)S(1)}, u32[]{:S(2)}, u32[]{:S(2)}) collective-permute-start(bf16[2,256,512]{2,1,0:T(8,128)(2,1)S(1)} %collective-permute-done.6.refs_8_), channel_id=1, source_target_pairs={{0,32},{32,64},{64,96},{96,0},{1,33},{33,65},{65,97},{97,1},{2,34}... | collective-permute-start | bytes 1572872 | tf_op jit(solution)/shard_map/ppermute | solution.py:332
  86.3 14.6 %collective-permute-start.11 = (bf16[2,256,256]{2,1,0:T(8,128)(2,1)S(1)}, bf16[2,256,256]{2,1,0:T(8,128)(2,1)S(1)}, u32[]{:S(2)}, u32[]{:S(2)}) collective-permute-start(bf16[2,256,256]{2,1,0:T(8,128)(2,1)S(1)} %collective-permute-done.7.g0), channel_id=1, source_target_pairs={{0,12},{4,0},{8,4},{12,8},{1,13},{5,1},{9,5},{13,9},{2,14},{6,2},{... | collective-permute-start | bytes 786440 | tf_op jit(solution)/shard_map/ppermute | solution.py:332
  87.8 13.1 %collective-permute-start.12 = (bf16[2,256,256]{2,1,0:T(8,128)(2,1)S(1)}, bf16[2,256,256]{2,1,0:T(8,128)(2,1)S(1)}, u32[]{:S(2)}, u32[]{:S(2)}) collective-permute-start(bf16[2,256,256]{2,1,0:T(8,128)(2,1)S(1)} %collective-permute-done.7.g0), channel_id=1, source_target_pairs={{0,8},{4,12},{8,0},{12,4},{1,9},{5,13},{9,1},{13,5},{2,10},{6,14},... | collective-permute-start | bytes 786440 | tf_op jit(solution)/shard_map/ppermute | solution.py:332
  89.3 13.2 %collective-permute-start.13 = (bf16[2,256,256]{2,1,0:T(8,128)(2,1)S(1)}, bf16[2,256,256]{2,1,0:T(8,128)(2,1)S(1)}, u32[]{:S(2)}, u32[]{:S(2)}) collective-permute-start(bf16[2,256,256]{2,1,0:T(8,128)(2,1)S(1)} %collective-permute-done.7.g0), channel_id=1, source_target_pairs={{0,4},{4,8},{8,12},{12,0},{1,5},{5,9},{9,13},{13,1},{2,6},{6,10},{... | collective-permute-start | bytes 786440 | tf_op jit(solution)/shard_map/ppermute | solution.py:332
  103.2 2.8 %collective-permute-start.18 = (f32[256,512]{1,0:T(8,128)S(1)}, f32[256,512]{1,0:T(8,128)S(1)}, u32[]{:S(2)}, u32[]{:S(2)}) collective-permute-start(f32[256,512]{1,0:T(8,128)S(1)} %get-tuple-element.66), channel_id=1, source_target_pairs={{0,16},{16,0},{1,17},{17,1},{2,18},{18,2},{3,19},{19,3},{4,20},{20... | collective-permute-start | bytes 1572872 | tf_op jit(solution)/shard_map/ppermute | solution.py:332
  105.1 2.1 %collective-permute-start.17 = (f32[256,512]{1,0:T(8,128)S(1)}, f32[256,512]{1,0:T(8,128)S(1)}, u32[]{:S(2)}, u32[]{:S(2)}) collective-permute-start(f32[256,512]{1,0:T(8,128)S(1)} %get-tuple-element.62), channel_id=1, source_target_pairs={{0,16},{16,0},{1,17},{17,1},{2,18},{18,2},{3,19},{19,3},{4,20},{20... | collective-permute-start | bytes 1572872 | tf_op jit(solution)/shard_map/ppermute | solution.py:332
  106.1 7.6 %collective-permute-start.19 = (bf16[256,512]{1,0:T(8,128)(2,1)S(1)}, bf16[256,512]{1,0:T(8,128)(2,1)S(1)}, u32[]{:S(2)}, u32[]{:S(2)}) collective-permute-start(bf16[256,512]{1,0:T(8,128)(2,1)S(1)} %add_convert_fusion.1), channel_id=1, source_target_pairs={{0,1},{1,0},{2,3},{3,2},{4,5},{5,4},{6,7},{7,6},{8,9},{9,8},{10,11... | collective-permute-start | bytes 786440 | tf_op jit(solution)/shard_map/ppermute | solution.py:380
